TPU v7x, 32 devices: a whole 2x2x4 slice. The times are simulated.
32 devices in a mesh: lat: 8 (over y, x, core), lon: 4 (over z).
Axes of the slice: x: 2, y: 2, z: 4, core: 2. Of those that a mesh axis runs over, the one named last changes fastest.
Arguments:
- fields: bfloat16 [384, 512, 128], P('lat', 'lon'), may hold values from -6 to 6
- wet_mask: int32 [384, 512], P('lat', 'lon'), may hold values 0 or 1
- conv_kernel: float32 [2, 49, 128], replicated, may hold values from -0.875 to 0.875
- conv_bias: float32 [2, 128], replicated, may hold values from -3 to 3
- norm_gain: float32 [2, 128], replicated, may hold values from 0.5 to 1.5
- norm_bias: float32 [2, 128], replicated, may hold values from -2 to 2
- in_weight: bfloat16 [2, 128, 512], replicated, may hold values from -0.5 to 0.5
- in_bias: float32 [2, 512], replicated, may hold values from -3 to 3
- out_weight: bfloat16 [2, 512, 128], replicated, may hold values from -0.25 to 0.25
- out_bias: float32 [2, 128], replicated, may hold values from -2 to 2
- layer_scale: float32 [2, 128], replicated, may hold values from 0.5 to 1.5
Outputs:
- result: bfloat16 [384, 512, 128], P('lat', 'lon')
Inputs may be any that keep to these rules, and one draw needn't show every extreme that they name: wet_mask holds only 0 and 1.
All inputs are finite; a program needn't handle non-finite values. No bound on the sum of `wet_mask` on one device may be relied on, other than what follows from the above.
Results may differ from a plain program's by a relative error of at most 0.0057.
Values may be sent and summed in bfloat16 or wider, within the bound.
No kernel may reach another device: no remote copies, remote signals or barrier semaphores. Data moves between devices by JAX's collectives and lax.ppermute only.
A program may use at most 64 MiB of HBM per device.

v0:
```python
import functools

import jax
import jax.numpy as jnp
import numpy as np
from jax import lax
from jax.experimental import pallas as pl
from jax.experimental.pallas import tpu as pltpu
from jax.sharding import PartitionSpec as P

BF = jnp.bfloat16
F32 = jnp.float32
TAPS = 7
HALO = 3
VMEM_LIMIT = 56 * 1024 * 1024


def partners(nlat, nlon, parity):
    route = []
    for lat in range(nlat):
        for lon in range(nlon):
            here = lat * nlon + lon
            if lat % 2 == parity:
                there = here + nlon if lat + 1 < nlat else lat * nlon + nlon - 1 - lon
            elif lat > 0:
                there = here - nlon
            else:
                continue
            route.append((here, there))
    return route


def exchange(state):
    nlat, nlon = lax.axis_size("lat"), lax.axis_size("lon")
    lat = lax.axis_index("lat")
    rows, cols = state.shape[0], state.shape[1]
    up = [(i, (i + 1) % nlon) for i in range(nlon)]
    down = [(j, i) for i, j in up]
    left = lax.ppermute(state[:, cols - HALO :], "lon", up)
    right = lax.ppermute(state[:, :HALO], "lon", down)
    first = jnp.concatenate([left[:HALO], state[:HALO], right[:HALO]], axis=1)
    last = jnp.concatenate([left[rows - HALO :], state[rows - HALO :], right[rows - HALO :]], axis=1)
    even = lat % 2 == 0
    got_a = lax.ppermute(jnp.where(even, last, first), ("lat", "lon"), partners(nlat, nlon, 0))
    got_b = lax.ppermute(jnp.where(even, first, last), ("lat", "lon"), partners(nlat, nlon, 1))
    north = jnp.where(even, got_a, got_b)
    south = jnp.where(even, got_b, got_a)
    north = jnp.where(lat == nlat - 1, north[::-1, ::-1], north)
    return left, right, south, north


def taps_kernel(k_ref, w_ref):
    ch = k_ref.shape[2]
    diag = lax.broadcasted_iota(jnp.int32, (ch, ch), 0) == lax.broadcasted_iota(jnp.int32, (ch, ch), 1)
    zero = jnp.zeros((ch, ch), BF)
    for s in range(TAPS):
        for a in range(TAPS + 1):
            for o in range(2):
                r = a - o
                if 0 <= r < TAPS:
                    tile = jnp.where(diag, k_ref[0, pl.ds(TAPS * r + s, 1), :], 0.0).astype(BF)
                else:
                    tile = zero
                w_ref[0, pl.ds((s * (TAPS + 1) + a) * ch, ch), o * ch : (o + 1) * ch] = tile


def tap_matrices(conv_kernel):
    blocks, _, ch = conv_kernel.shape
    depth = TAPS * (TAPS + 1) * ch
    return pl.pallas_call(
        taps_kernel,
        grid=(blocks,),
        in_specs=[pl.BlockSpec((1, TAPS * TAPS, ch), lambda b: (b, 0, 0))],
        out_specs=pl.BlockSpec((1, depth, 2 * ch), lambda b: (b, 0, 0)),
        out_shape=jax.ShapeDtypeStruct((blocks, depth, 2 * ch), BF),
        compiler_params=pltpu.CompilerParams(vmem_limit_bytes=VMEM_LIMIT),
        cost_estimate=pl.CostEstimate(flops=0, bytes_accessed=2 * blocks * depth * 2 * ch, transcendentals=0),
        name="tap_matrices",
    )(conv_kernel)


def block_kernel(
    pairs,
    last,
    x_ref,
    left_ref,
    right_ref,
    south_ref,
    north_ref,
    mask_ref,
    w_ref,
    vec_ref,
    inw_ref,
    inb_ref,
    outw_ref,
    out_ref,
    pad_ref,
    shifted_ref,
):
    rows, cols, ch = x_ref.shape
    base = 8
    lead = base - HALO
    wide = cols + 2 * HALO
    pad_ref[0:HALO, lead : lead + wide, :] = south_ref[...].astype(F32)
    pad_ref[rows + HALO : rows + 2 * HALO, lead : lead + wide, :] = north_ref[...].astype(F32)

    def fill(i, carry):
        pad_ref[i + HALO, lead:base, :] = left_ref[i].astype(F32)
        pad_ref[i + HALO, base : base + cols, :] = x_ref[i].astype(F32)
        pad_ref[i + HALO, base + cols : base + cols + HALO, :] = right_ref[i].astype(F32)
        return carry

    lax.fori_loop(0, rows, fill, 0)

    def shift(q, carry):
        for s in range(TAPS):
            for h in range(2):
                shifted_ref[s, q, :, h * ch : (h + 1) * ch] = pad_ref[2 * q + h, lead + s : lead + s + cols, :].astype(BF)
        return carry

    lax.fori_loop(0, (rows + 2 * HALO) // 2, shift, 0)

    conv_bias, gain, nbias, outb, scale = (vec_ref[i : i + 1, :] for i in range(5))
    inb = inb_ref[...]
    if last:
        diag = lax.broadcasted_iota(jnp.int32, (cols, cols), 0) == lax.broadcasted_iota(jnp.int32, (cols, cols), 1)

    def chunk(t, carry):
        p = t * pairs
        cells = pairs * cols
        parts = []
        for s in range(TAPS):
            for a in range((TAPS + 1) // 2):
                parts.append(shifted_ref[s, pl.ds(p + a, pairs)].reshape(cells, 2 * ch))
        acc = jnp.dot(jnp.concatenate(parts, axis=1), w_ref[...], preferred_element_type=F32)
        for h in range(2):
            conv = acc[:, h * ch : (h + 1) * ch] + conv_bias
            mean = jnp.mean(conv, axis=-1, keepdims=True)
            cen = conv - mean
            var = jnp.mean(cen * cen, axis=-1, keepdims=True)
            normed = (cen * lax.rsqrt(var + 1e-6) * gain + nbias).astype(BF)
            hid = jnp.dot(normed, inw_ref[...], preferred_element_type=F32) + inb
            hid = (0.5 * hid * (1.0 + lax.erf(hid * np.float32(np.sqrt(0.5))))).astype(BF)
            branch = (jnp.dot(hid, outw_ref[...], preferred_element_type=F32) + outb) * scale
            for j in range(pairs):
                row = 2 * (p + j) + h
                new = (x_ref[row].astype(F32) + branch[j * cols : (j + 1) * cols]).astype(BF)
                if last:
                    keep = jnp.where(diag, mask_ref[pl.ds(row, 1), :], 0.0).astype(BF)
                    new = jnp.dot(keep, new, preferred_element_type=F32).astype(BF)
                out_ref[row] = new
        return carry

    lax.fori_loop(0, rows // (2 * pairs), chunk, 0)


def run_block(state, halos, mask, w, vec, inw, inb, outw, last):
    rows, cols, ch = state.shape
    hid = inw.shape[1]
    half = rows // 2
    pairs = max(d for d in (1, 2, 4) if half % d == 0)
    spec = pl.BlockSpec(memory_space=pltpu.VMEM)
    cells = rows * cols
    return pl.pallas_call(
        functools.partial(block_kernel, pairs, last),
        in_specs=[spec] * 11,
        out_specs=spec,
        out_shape=jax.ShapeDtypeStruct(state.shape, BF),
        scratch_shapes=[
            pltpu.VMEM((rows + 2 * HALO, cols + 16, ch), F32),
            pltpu.VMEM((TAPS, (rows + 2 * HALO) // 2, cols, 2 * ch), BF),
        ],
        compiler_params=pltpu.CompilerParams(vmem_limit_bytes=VMEM_LIMIT),
        cost_estimate=pl.CostEstimate(
            flops=cells * (4 * ch * hid + 2 * ch * w.shape[0]), bytes_accessed=4 * cells * ch, transcendentals=cells * hid
        ),
        name="block",
    )(state, *halos, mask, w, vec, inw, inb, outw)


def shards(
    fields,
    wet_mask,
    conv_kernel,
    conv_bias,
    norm_gain,
    norm_bias,
    in_weight,
    in_bias,
    out_weight,
    out_bias,
    layer_scale,
):
    state = fields * wet_mask.astype(BF)[:, :, None]
    mask = wet_mask.astype(F32)
    w = tap_matrices(conv_kernel)
    vec = jnp.stack([conv_bias, norm_gain, norm_bias, out_bias, layer_scale], axis=1)
    blocks = conv_kernel.shape[0]
    for b in range(blocks):
        halos = exchange(state)
        state = run_block(
            state, halos, mask, w[b], vec[b], in_weight[b], in_bias[b][None], out_weight[b], b == blocks - 1
        )
    return state


def solution(mesh):
    return jax.shard_map(
        shards,
        mesh=mesh,
        in_specs=(P("lat", "lon", None), P("lat", "lon")) + (P(),) * 9,
        out_specs=P("lat", "lon", None),
        check_vma=False,
    )
```

profile of v0, /device:TPU:1, one launch (start us, length us, event | category | flops | bytes accessed | tf_op | source)
XLA Modules:
  0.0 107.2 jit_solution(7591757204576920859)
XLA Ops:
  0.0 1.4 %fusion.8 = (f32[48,128]{1,0:T(8,128)}, bf16[48,128]{1,0:T(8,128)(2,1)S(1)}) fusion(s32[48,128]{1,0:T(8,128)} %param.12), kind=kLoop, calls=%fused_computation.31 | loop fusion | flops 12288 | bytes 61440 | tf_op jit(solution)/shard_map/convert_element_type | solution.py:195
  1.4 2.1 %broadcast_multiply_fusion.x_ref = bf16[48,128,128]{2,1,0:T(8,128)(2,1)S(1)} fusion(bf16[48,128,128]{2,1,0:T(8,128)(2,1)} %param.11, bf16[48,128]{1,0:T(8,128)(2,1)S(1)} %get-tuple-element.36), kind=kLoop, calls=%fused_computation.2 | loop fusion | flops 786432 | bytes 3158016 | tf_op jit(solution)/shard_map/mul | solution.py:194
  3.6 2.2 %collective-permute-start = (bf16[48,3,128]{2,1,0:T(4,128)(2,1)S(1)}, bf16[48,3,128]{2,1,0:T(4,128)(2,1)S(1)}, u32[]{:S(2)}, u32[]{:S(2)}) collective-permute-start(bf16[48,3,128]{2,1,0:T(4,128)(2,1)S(1)} %get-tuple-element.14), channel_id=1, source_target_pairs={{0,1},{1,2},{2,3},{3,0},{4,5},{5,6},{6,7},{7,4},{8,9},{9,10},{10,1... | collective-permute-start | bytes 110600 | tf_op jit(solution)/shard_map/ppermute | solution.py:39
  5.8 2.1 %collective-permute-start.1 = (bf16[48,3,128]{2,1,0:T(4,128)(2,1)S(1)}, bf16[48,3,128]{2,1,0:T(4,128)(2,1)S(1)}, u32[]{:S(2)}, u32[]{:S(2)}) collective-permute-start(bf16[48,3,128]{2,1,0:T(4,128)(2,1)S(1)} %get-tuple-element.13), channel_id=1, source_target_pairs={{1,0},{2,1},{3,2},{0,3},{5,4},{6,5},{7,6},{4,7},{9,8},{10,9},{11,1... | collective-permute-start | bytes 110600 | tf_op jit(solution)/shard_map/ppermute | solution.py:40
  7.9 0.6 copy.12.k_ref
  8.5 4.1 %tap_matrices.1 = bf16[2,7168,256]{2,1,0:T(8,128)(2,1)} custom-call(f32[2,49,128]{2,1,0:T(8,128)} %copy.12.k_ref), custom_call_target="tpu_custom_call" | custom-call | bytes 7340032 | tf_op jit(solution)/shard_map/tap_matrices/pallas_call | solution.py:70
  12.7 6.7 %slice_bitcast_fusion = (bf16[7168,256]{1,0:T(8,128)(2,1)}, bf16[7168,256]{1,0:T(8,128)(2,1)}) fusion(bf16[2,7168,256]{2,1,0:T(8,128)(2,1)} %tap_matrices.1), kind=kLoop, calls=%fused_computation | loop fusion | bytes 14680064 | tf_op jit(solution)/shard_map/squeeze | solution.py:202
  19.4 0.7 slice_bitcast_fusion.2
  20.1 0.7 slice_bitcast_fusion.3
  20.9 0.6 slice_bitcast_fusion.6
  21.6 0.1 broadcast_select_fusion.8
  21.6 4.1 %collective-permute-start.2 = (bf16[3,134,128]{2,1,0:T(8,128)(2,1)S(1)}, bf16[3,134,128]{2,1,0:T(8,128)(2,1)S(1)}, u32[]{:S(2)}, u32[]{:S(2)}) collective-permute-start(bf16[3,134,128]{2,1,0:T(8,128)(2,1)S(1)} %get-tuple-element.26), channel_id=1, source_target_pairs={{4,8},{5,9},{6,10},{7,11},{8,4},{9,5},{10,6},{11,7},{12,16},{13,17... | collective-permute-start | bytes 308744 | tf_op jit(solution)/shard_map/ppermute | solution.py:45
  25.8 0.1 collective-permute-start.3
  25.9 0.6 fusion.9
  26.5 1.9 %collective-permute-done.2 = bf16[3,134,128]{2,1,0:T(8,128)(2,1)S(1)} collective-permute-done((bf16[3,134,128]{2,1,0:T(8,128)(2,1)S(1)}, bf16[3,134,128]{2,1,0:T(8,128)(2,1)S(1)}, u32[]{:S(2)}, u32[]{:S(2)}) %collective-permute-start.2) | collective-permute-done | bytes 102944 | tf_op jit(solution)/shard_map/ppermute | solution.py:45
  28.4 0.7 broadcast_select_fusion.6
  29.0 0.4 rev.6
  29.5 0.7 broadcast_select_fusion.1.north_ref
  30.2 29.8 %block.2.x_ref = bf16[48,128,128]{2,1,0:T(8,128)(2,1)} custom-call(bf16[48,128,128]{2,1,0:T(8,128)(2,1)} %copy-done, bf16[48,3,128]{2,1,0:T(4,128)(2,1)} %copy-done.10, bf16[48,3,128]{2,1,0:T(4,128)(2,1)} %copy-done.11, bf16[3,134,128]{2,1,0:T(8,128)(2,1)} %get-tuple-element.24.south_ref, bf16[3,134,128]{2,1,0:T(8,128)(2,1)} %broadcast_select_fusion.1.north_ref, ...), custom_call_target="tpu_custom_call" | custom-call | flops 12884901888 | bytes 3145728 | tf_op jit(solution)/shard_map/block/pallas_call | solution.py:164
  60.0 1.0 fusion.1
  61.0 1.0 fusion
  62.0 3.3 %collective-permute-start.5 = (bf16[48,3,128]{2,1,0:T(4,128)(2,1)S(1)}, bf16[48,3,128]{2,1,0:T(4,128)(2,1)S(1)}, u32[]{:S(2)}, u32[]{:S(2)}) collective-permute-start(bf16[48,3,128]{2,1,0:T(4,128)(2,1)S(1)} %get-tuple-element.9), channel_id=1, source_target_pairs={{1,0},{2,1},{3,2},{0,3},{5,4},{6,5},{7,6},{4,7},{9,8},{10,9},{11,1... | collective-permute-start | bytes 110600 | tf_op jit(solution)/shard_map/ppermute | solution.py:40
  65.3 0.7 collective-permute-done.4.left_ref
  66.0 0.6 collective-permute-done.5.right_ref
  66.5 0.1 broadcast_select_fusion.4
  66.6 4.6 %collective-permute-start.6 = (bf16[3,134,128]{2,1,0:T(8,128)(2,1)S(1)}, bf16[3,134,128]{2,1,0:T(8,128)(2,1)S(1)}, u32[]{:S(2)}, u32[]{:S(2)}) collective-permute-start(bf16[3,134,128]{2,1,0:T(8,128)(2,1)S(1)} %get-tuple-element.22), channel_id=1, source_target_pairs={{4,8},{5,9},{6,10},{7,11},{8,4},{9,5},{10,6},{11,7},{12,16},{13,17... | collective-permute-start | bytes 308744 | tf_op jit(solution)/shard_map/ppermute | solution.py:45
  71.3 0.1 collective-permute-start.7
  71.3 2.3 %collective-permute-done.6 = bf16[3,134,128]{2,1,0:T(8,128)(2,1)S(1)} collective-permute-done((bf16[3,134,128]{2,1,0:T(8,128)(2,1)S(1)}, bf16[3,134,128]{2,1,0:T(8,128)(2,1)S(1)}, u32[]{:S(2)}, u32[]{:S(2)}) %collective-permute-start.6) | collective-permute-done | bytes 102944 | tf_op jit(solution)/shard_map/ppermute | solution.py:45
  73.6 0.7 broadcast_select_fusion.2
  74.3 0.4 rev.7
  74.8 0.7 broadcast_select_fusion.north_ref
  75.4 31.8 %block.3 = bf16[48,128,128]{2,1,0:T(8,128)(2,1)} custom-call(bf16[48,128,128]{2,1,0:T(8,128)(2,1)} %block.2.x_ref, bf16[48,3,128]{2,1,0:T(4,128)(2,1)} %copy-done.12, bf16[48,3,128]{2,1,0:T(4,128)(2,1)} %copy-done.13, bf16[3,134,128]{2,1,0:T(8,128)(2,1)} %get-tuple-element.20.south_ref, bf16[3,134,128]{2,1,0:T(8,128)(2,1)} %broadcast_select_fusion.north_ref, ...), custom_call_target="tpu_custom_call" | custom-call | flops 12884901888 | bytes 3145728 | tf_op jit(solution)/shard_map/block/pallas_call | solution.py:164
  (40 shorter events, 0.2 us)
Async XLA Ops:
  1.4 6.5 %copy-start.3 = (f32[2,49,128]{2,0,1:T(2,128)S(1)}, f32[2,49,128]{2,0,1:T(2,128)}, u32[]{:S(2)}) copy-start(f32[2,49,128]{2,0,1:T(2,128)} %param.13) | copy-start | bytes 150532
  3.5 9.1 %copy-start = (bf16[48,128,128]{2,1,0:T(8,128)(2,1)}, bf16[48,128,128]{2,1,0:T(8,128)(2,1)S(1)}, u32[]{:S(2)}) copy-start(bf16[48,128,128]{2,1,0:T(8,128)(2,1)S(1)} %broadcast_multiply_fusion.x_ref) | copy-start | bytes 4718596
  3.6 17.9 %collective-permute-start = (bf16[48,3,128]{2,1,0:T(4,128)(2,1)S(1)}, bf16[48,3,128]{2,1,0:T(4,128)(2,1)S(1)}, u32[]{:S(2)}, u32[]{:S(2)}) collective-permute-start(bf16[48,3,128]{2,1,0:T(4,128)(2,1)S(1)} %get-tuple-element.14), channel_id=1, source_target_pairs={{0,1},{1,2},{2,3},{3,0},{4,5},{5,6},{6,7},{7,4},{8,9},{9,10},{10,1... | collective-permute-start | bytes 110600 | tf_op jit(solution)/shard_map/ppermute | solution.py:39
  5.8 15.7 %collective-permute-start.1 = (bf16[48,3,128]{2,1,0:T(4,128)(2,1)S(1)}, bf16[48,3,128]{2,1,0:T(4,128)(2,1)S(1)}, u32[]{:S(2)}, u32[]{:S(2)}) collective-permute-start(bf16[48,3,128]{2,1,0:T(4,128)(2,1)S(1)} %get-tuple-element.13), channel_id=1, source_target_pairs={{1,0},{2,1},{3,2},{0,3},{5,4},{6,5},{7,6},{4,7},{9,8},{10,9},{11,1... | collective-permute-start | bytes 110600 | tf_op jit(solution)/shard_map/ppermute | solution.py:40
  12.6 6.7 %copy-start.1 = (bf16[2,512,128]{2,1,0:T(8,128)(2,1)S(1)}, bf16[2,512,128]{2,1,0:T(8,128)(2,1)}, u32[]{:S(2)}) copy-start(bf16[2,512,128]{2,1,0:T(8,128)(2,1)} %param.19) | copy-start | bytes 786436
  12.6 7.5 %copy-start.2 = (bf16[2,128,512]{2,1,0:T(8,128)(2,1)S(1)}, bf16[2,128,512]{2,1,0:T(8,128)(2,1)}, u32[]{:S(2)}) copy-start(bf16[2,128,512]{2,1,0:T(8,128)(2,1)} %param.17) | copy-start | bytes 786436
  12.7 8.2 %copy-start.5 = (f32[2,128]{1,0:T(2,128)S(1)}, f32[2,128]{1,0:T(2,128)}, u32[]{:S(2)}) copy-start(f32[2,128]{1,0:T(2,128)} %param.14) | copy-start | bytes 3076
  12.7 8.2 %copy-start.6 = (f32[2,128]{1,0:T(2,128)S(1)}, f32[2,128]{1,0:T(2,128)}, u32[]{:S(2)}) copy-start(f32[2,128]{1,0:T(2,128)} %param.15) | copy-start | bytes 3076
  12.7 8.2 %copy-start.7 = (f32[2,128]{1,0:T(2,128)S(1)}, f32[2,128]{1,0:T(2,128)}, u32[]{:S(2)}) copy-start(f32[2,128]{1,0:T(2,128)} %param.16) | copy-start | bytes 3076
  12.7 8.2 %copy-start.8 = (f32[2,128]{1,0:T(2,128)S(1)}, f32[2,128]{1,0:T(2,128)}, u32[]{:S(2)}) copy-start(f32[2,128]{1,0:T(2,128)} %param.20) | copy-start | bytes 3076
  12.7 8.2 %copy-start.9 = (f32[2,128]{1,0:T(2,128)S(1)}, f32[2,128]{1,0:T(2,128)}, u32[]{:S(2)}) copy-start(f32[2,128]{1,0:T(2,128)} %param.21) | copy-start | bytes 3076
  19.4 6.5 %copy-start.4 = (f32[2,512]{1,0:T(2,128)S(1)}, f32[2,512]{1,0:T(2,128)}, u32[]{:S(2)}) copy-start(f32[2,512]{1,0:T(2,128)} %param.18) | copy-start | bytes 12292
  21.5 8.6 %copy-start.10 = (bf16[48,3,128]{2,1,0:T(4,128)(2,1)}, bf16[48,3,128]{2,1,0:T(4,128)(2,1)S(1)}, u32[]{:S(2)}) copy-start(bf16[48,3,128]{2,1,0:T(4,128)(2,1)S(1)} %collective-permute-done.left_ref) | copy-start | bytes 110596
  21.5 8.6 %copy-start.11 = (bf16[48,3,128]{2,1,0:T(4,128)(2,1)}, bf16[48,3,128]{2,1,0:T(4,128)(2,1)S(1)}, u32[]{:S(2)}) copy-start(bf16[48,3,128]{2,1,0:T(4,128)(2,1)S(1)} %collective-permute-done.1.right_ref) | copy-start | bytes 110596
  21.6 6.7 %collective-permute-start.2 = (bf16[3,134,128]{2,1,0:T(8,128)(2,1)S(1)}, bf16[3,134,128]{2,1,0:T(8,128)(2,1)S(1)}, u32[]{:S(2)}, u32[]{:S(2)}) collective-permute-start(bf16[3,134,128]{2,1,0:T(8,128)(2,1)S(1)} %get-tuple-element.26), channel_id=1, source_target_pairs={{4,8},{5,9},{6,10},{7,11},{8,4},{9,5},{10,6},{11,7},{12,16},{13,17... | collective-permute-start | bytes 308744 | tf_op jit(solution)/shard_map/ppermute | solution.py:45
  25.8 2.6 %collective-permute-start.3 = (bf16[3,134,128]{2,1,0:T(8,128)(2,1)S(1)}, bf16[3,134,128]{2,1,0:T(8,128)(2,1)S(1)}, u32[]{:S(2)}, u32[]{:S(2)}) collective-permute-start(bf16[3,134,128]{2,1,0:T(8,128)(2,1)S(1)} %get-tuple-element.25), channel_id=1, source_target_pairs={{0,4},{1,5},{2,6},{3,7},{4,0},{5,1},{6,2},{7,3},{8,12},{9,13},{10,... | collective-permute-start | bytes 308744 | tf_op jit(solution)/shard_map/ppermute | solution.py:44
  61.0 5.0 %collective-permute-start.4 = (bf16[48,3,128]{2,1,0:T(4,128)(2,1)S(1)}, bf16[48,3,128]{2,1,0:T(4,128)(2,1)S(1)}, u32[]{:S(2)}, u32[]{:S(2)}) collective-permute-start(bf16[48,3,128]{2,1,0:T(4,128)(2,1)S(1)} %get-tuple-element.10), channel_id=1, source_target_pairs={{0,1},{1,2},{2,3},{3,0},{4,5},{5,6},{6,7},{7,4},{8,9},{9,10},{10,1... | collective-permute-start | bytes 110600 | tf_op jit(solution)/shard_map/ppermute | solution.py:39
  62.0 4.5 %collective-permute-start.5 = (bf16[48,3,128]{2,1,0:T(4,128)(2,1)S(1)}, bf16[48,3,128]{2,1,0:T(4,128)(2,1)S(1)}, u32[]{:S(2)}, u32[]{:S(2)}) collective-permute-start(bf16[48,3,128]{2,1,0:T(4,128)(2,1)S(1)} %get-tuple-element.9), channel_id=1, source_target_pairs={{1,0},{2,1},{3,2},{0,3},{5,4},{6,5},{7,6},{4,7},{9,8},{10,9},{11,1... | collective-permute-start | bytes 110600 | tf_op jit(solution)/shard_map/ppermute | solution.py:40
  66.0 9.5 %copy-start.12 = (bf16[48,3,128]{2,1,0:T(4,128)(2,1)}, bf16[48,3,128]{2,1,0:T(4,128)(2,1)S(1)}, u32[]{:S(2)}) copy-start(bf16[48,3,128]{2,1,0:T(4,128)(2,1)S(1)} %collective-permute-done.4.left_ref) | copy-start | bytes 110596
  66.5 8.9 %copy-start.13 = (bf16[48,3,128]{2,1,0:T(4,128)(2,1)}, bf16[48,3,128]{2,1,0:T(4,128)(2,1)S(1)}, u32[]{:S(2)}) copy-start(bf16[48,3,128]{2,1,0:T(4,128)(2,1)S(1)} %collective-permute-done.5.right_ref) | copy-start | bytes 110596
  66.6 7.0 %collective-permute-start.6 = (bf16[3,134,128]{2,1,0:T(8,128)(2,1)S(1)}, bf16[3,134,128]{2,1,0:T(8,128)(2,1)S(1)}, u32[]{:S(2)}, u32[]{:S(2)}) collective-permute-start(bf16[3,134,128]{2,1,0:T(8,128)(2,1)S(1)} %get-tuple-element.22), channel_id=1, source_target_pairs={{4,8},{5,9},{6,10},{7,11},{8,4},{9,5},{10,6},{11,7},{12,16},{13,17... | collective-permute-start | bytes 308744 | tf_op jit(solution)/shard_map/ppermute | solution.py:45
  71.3 2.4 %collective-permute-start.7 = (bf16[3,134,128]{2,1,0:T(8,128)(2,1)S(1)}, bf16[3,134,128]{2,1,0:T(8,128)(2,1)S(1)}, u32[]{:S(2)}, u32[]{:S(2)}) collective-permute-start(bf16[3,134,128]{2,1,0:T(8,128)(2,1)S(1)} %get-tuple-element.21), channel_id=1, source_target_pairs={{0,4},{1,5},{2,6},{3,7},{4,0},{5,1},{6,2},{7,3},{8,12},{9,13},{10,... | collective-permute-start | bytes 308744 | tf_op jit(solution)/shard_map/ppermute | solution.py:44
where the time goes:
time: 109 us; the launch traced here: 107 us
  Pallas kernels  65.7 us (60%)
  starting transfers between devices  16.5 us (15%)
  local copies, waits for them, and re-layouts  12.9 us (12%)
  other arithmetic  6.4 us (6%)
  waiting for transfers between devices  5.41 us (5%)
    pallas_call x2, Pallas kernels, run_block(): pl.pallas_call(functools.partial(block_kernel, pairs, last), in_specs=[sp...  61.6 us
    ppermute x2, starting transfers between devices, exchange(): lax.ppermute(jnp.where(even, first, last), ('lat', 'lon'), partners(nlat,...  8.74 us
    squeeze x1, local copies, waits for them, and re-layouts, shards(): w[b]  6.68 us
    ppermute x2, starting transfers between devices, exchange(): right = lax.ppermute(state[:, :HALO], 'lon', down)  5.39 us
    ppermute x2, waiting for transfers between devices, exchange(): lax.ppermute(jnp.where(even, first, last), ('lat', 'lon'), partners(nlat,...  4.17 us
    pallas_call x1, Pallas kernels, tap_matrices(): pl.pallas_call(taps_kernel, grid=(blocks,), in_specs=[pl.BlockSpec((1, TA...  4.12 us
    ppermute x2, starting transfers between devices, exchange(): left = lax.ppermute(state[:, cols - HALO:], 'lon', up)  2.24 us
  transfers between devices with their start and end apart: 8, of which 4 were waited for; matrix products, arithmetic and copies ran while one was open for 10% of the time, Pallas kernels for 4%

commit v1 on v0

v1 whole, which is shorter than its diff:
```python
import functools

import jax
import jax.numpy as jnp
from jax import lax
from jax.experimental import pallas as pl
from jax.experimental.pallas import tpu as pltpu
from jax.sharding import PartitionSpec as P

BF = jnp.bfloat16
F32 = jnp.float32
TAPS = 7
HALO = 3
REACH = 2 * HALO
OUTS = 8
VMEM_LIMIT = 62 * 1024 * 1024
ERF_POLY = (0.7978323547267507, 0.036463673384825215, -0.0001230322006747663, -3.081922192956723e-05, 1.128904780388478e-06)


def partners(nlat, nlon, parity):
    route = []
    for lat in range(nlat):
        for lon in range(nlon):
            here = lat * nlon + lon
            if lat % 2 == parity:
                there = here + nlon if lat + 1 < nlat else lat * nlon + nlon - 1 - lon
            elif lat > 0:
                there = here - nlon
            else:
                continue
            route.append((here, there))
    return route


def exchange(fields, wet_mask):
    nlat, nlon = lax.axis_size("lat"), lax.axis_size("lon")
    lat = lax.axis_index("lat")
    rows, cols = wet_mask.shape

    def edge(r0, r1, c0, c1):
        return fields[r0:r1, c0:c1] * wet_mask[r0:r1, c0:c1].astype(BF)[:, :, None]

    up = [(i, (i + 1) % nlon) for i in range(nlon)]
    down = [(j, i) for i, j in up]
    left = lax.ppermute(edge(0, rows, cols - REACH, cols), "lon", up)
    right = lax.ppermute(edge(0, rows, 0, REACH), "lon", down)
    first = jnp.concatenate([left[:REACH], edge(0, REACH, 0, cols), right[:REACH]], axis=1)
    last = jnp.concatenate([left[rows - REACH :], edge(rows - REACH, rows, 0, cols), right[rows - REACH :]], axis=1)
    even = lat % 2 == 0
    got_a = lax.ppermute(jnp.where(even, last, first), ("lat", "lon"), partners(nlat, nlon, 0))
    got_b = lax.ppermute(jnp.where(even, first, last), ("lat", "lon"), partners(nlat, nlon, 1))
    flags = jnp.stack([even, lat == nlat - 1, lat == 0]).astype(jnp.int32)
    return left, right, got_a, got_b, flags


def tap_vectors(conv_kernel):
    blocks, _, ch = conv_kernel.shape
    width = 2 * ch // OUTS
    taps = conv_kernel.reshape(blocks, TAPS, TAPS, ch // width, width)
    taps = jnp.pad(taps, ((0, 0), (OUTS - 1, 2 * OUTS - TAPS), (0, 0), (0, 0), (0, 0)))
    by_out = [taps[:, OUTS - 1 - o : 3 * OUTS - 1 - o] for o in range(OUTS)]
    stacked = jnp.stack(by_out, axis=4)
    return stacked.transpose(0, 3, 2, 1, 4, 5).reshape(blocks, ch // width * TAPS, 2 * OUTS, OUTS * width)


def regroup(parts, width):
    parts = list(parts)
    ch = parts[0].shape[-1]
    block = lax.broadcasted_iota(jnp.int32, parts[0].shape, parts[0].ndim - 1) // width
    step = 1
    while step < len(parts):
        low = (block & step) == 0
        for i in range(len(parts)):
            if not i & step:
                x, y = parts[i], parts[i + step]
                parts[i] = jnp.where(low, x, pltpu.roll(y, step * width, x.ndim - 1))
                parts[i + step] = jnp.where(low, pltpu.roll(x, ch - step * width, x.ndim - 1), y)
        step *= 2
    return parts


def both_blocks(
    flags_ref,
    x_ref,
    mask_ref,
    left_ref,
    right_ref,
    a_ref,
    b_ref,
    k_ref,
    kv_ref,
    vec_ref,
    inw_ref,
    inb_ref,
    outw_ref,
    out_ref,
    x0_ref,
    x1_ref,
    shifted_ref,
    group_ref,
    w_ref,
    acc_ref,
    strip_ref,
    flip_ref,
):
    rows, cols, ch = x_ref.shape
    width = 2 * ch // OUTS
    groups = ch // width
    octets = rows // OUTS
    quads = 2 * octets + 2
    wide0 = x1_ref.shape[1]
    base = 8
    ext = cols + 2 * REACH
    lead = base - REACH
    total = x0_ref.shape[1]
    even, top, bottom = (flags_ref[i] == 1 for i in range(3))

    def fill(i, carry):
        x0_ref[i + REACH, 0:base, :] = jnp.zeros((base, ch), F32)
        x0_ref[i + REACH, lead:base, :] = left_ref[i].astype(F32)
        x0_ref[i + REACH, base : base + cols, :] = x_ref[i].astype(F32)
        x0_ref[i + REACH, base + cols : total, :] = jnp.zeros((total - base - cols, ch), F32)
        x0_ref[i + REACH, base + cols : base + cols + REACH, :] = right_ref[i].astype(F32)
        return carry

    lax.fori_loop(0, rows, fill, 0)
    flip_ref[...] = jnp.zeros(flip_ref.shape, F32)
    at = lax.broadcasted_iota(jnp.int32, (wide0, wide0), 0)
    to = lax.broadcasted_iota(jnp.int32, (wide0, wide0), 1)
    mirror = jnp.where(to == jnp.where(top, ext - 1 - at, at), 1.0, 0.0).astype(BF)
    for i in range(REACH):
        x0_ref[i, :, :] = jnp.zeros((total, ch), F32)
        x0_ref[i, lead : lead + ext, :] = jnp.where(even, b_ref[i].astype(F32), a_ref[i].astype(F32))
        src = jnp.where(top, REACH - 1 - i, i)
        flip_ref[0:ext, :] = jnp.where(even, a_ref[src].astype(F32), b_ref[src].astype(F32))
        turned = jnp.dot(mirror, flip_ref[0:wide0, :].astype(BF), preferred_element_type=F32)
        x0_ref[rows + REACH + i, :, :] = jnp.zeros((total, ch), F32)
        x0_ref[rows + REACH + i, lead : lead + wide0, :] = turned

    own = (lax.broadcasted_iota(jnp.int32, (width, OUTS * width), 1) & (width - 1)) == lax.broadcasted_iota(
        jnp.int32, (width, OUTS * width), 0
    )

    def build(b):
        for s in range(TAPS):
            def one(gr, carry):
                for a in range(2 * OUTS):
                    vec = kv_ref[b, gr * TAPS + s, a : a + 1, :]
                    w_ref[gr, (s * 2 * OUTS + a) * width : (s * 2 * OUTS + a + 1) * width, :] = jnp.where(
                        own, vec, 0.0
                    ).astype(BF)
                return carry

            lax.fori_loop(0, groups, one, 0)

    def shift(src_ref, row0, col0, wide):
        span = wide + 8

        def one(q, carry):
            parts = [src_ref[row0 + 4 * q + j, :, :] for j in range(groups)]
            for j, part in enumerate(regroup(parts, width)):
                group_ref[j, 0 : part.shape[0], :] = part
            for s in range(TAPS):
                for j in range(groups):
                    shifted_ref[s, j, q % 2, q // 2, 0:wide, :] = group_ref[j, col0 + s : col0 + s + wide, :].astype(BF)
            return carry

        lax.fori_loop(0, quads, one, 0)

    def conv(wide):
        def one(gr, carry):
            parts = []
            for s in range(TAPS):
                for a in range(4):
                    part = shifted_ref[s, gr, a % 2, a // 2 : a // 2 + octets, 0:wide, :]
                    parts.append(part.reshape(octets * wide, ch))
            acc_ref[gr, 0 : octets * wide, :] = jnp.dot(
                jnp.concatenate(parts, axis=1), w_ref[gr], preferred_element_type=F32
            )
            return carry

        lax.fori_loop(0, groups, one, 0)

    def mlp(b, conv_rows):
        conv_bias, gain, nbias, outb, scale = (vec_ref[b, i : i + 1, :] for i in range(5))
        val = jnp.concatenate(conv_rows, axis=0) + conv_bias
        mean = jnp.mean(val, axis=-1, keepdims=True)
        cen = val - mean
        var = jnp.mean(cen * cen, axis=-1, keepdims=True)
        normed = (cen * lax.rsqrt(var + 1e-6) * gain + nbias).astype(BF)
        h = jnp.dot(normed, inw_ref[b], preferred_element_type=F32) + inb_ref[b : b + 1, :]
        z = h * h
        p = jnp.full_like(z, ERF_POLY[-1])
        for coef in ERF_POLY[-2::-1]:
            p = p * z + coef
        t = jnp.tanh(h * p)
        twice = (h + h * t).astype(BF)
        branch = jnp.dot(twice, outw_ref[b], preferred_element_type=F32) * (0.5 * scale) + outb * scale
        n = conv_rows[0].shape[0]
        return [branch[i * n : (i + 1) * n] for i in range(len(conv_rows))]

    def inner(b, wide, emit):
        def one(t, carry):
            for half in range(2):
                parts = [
                    acc_ref[gr, pl.ds(pl.multiple_of(t * wide, 16), wide), half * ch : (half + 1) * ch]
                    for gr in range(groups)
                ]
                for j, branch in enumerate(mlp(b, regroup(parts, width))):
                    emit(OUTS * t + half * (OUTS // 2) + j, branch)
            return carry

        lax.fori_loop(0, octets, one, 0)

    build(0)
    shift(x0_ref, REACH - HALO, lead, wide0)
    conv(wide0)

    def keep0(row, branch):
        new = x0_ref[row + REACH, lead + HALO : lead + HALO + wide0, :] + branch
        x1_ref[row + HALO, :, :] = new.astype(BF).astype(F32)

    inner(0, wide0, keep0)
    piece = wide0 // 3
    for side in range(2):
        first = 0 if side == 0 else rows + HALO
        for c in range(0, wide0, piece):
            sums = [jnp.zeros((piece, ch), F32) for _ in range(HALO)]
            for s in range(TAPS):
                lines = [x0_ref[first + i, lead + s + c : lead + s + c + piece, :] for i in range(TAPS + HALO - 1)]
                for r in range(TAPS):
                    tap = TAPS * r + s
                    if side == 1:
                        tap = jnp.where(top, TAPS * TAPS - 1 - tap, tap)
                    weight = k_ref[0, pl.ds(tap, 1), :]
                    for i in range(HALO):
                        sums[i] = sums[i] + lines[i + r] * weight
            for i in range(HALO):
                strip_ref[side * HALO + i, c : c + piece, :] = sums[i]
    for side in range(2):
        branches = mlp(0, [strip_ref[side * HALO + i] for i in range(HALO)])
        for i, branch in enumerate(branches):
            row = i - HALO if side == 0 else rows + i
            new = x0_ref[row + REACH, lead + HALO : lead + HALO + wide0, :] + branch
            new = new.astype(BF).astype(F32)
            if side == 0:
                new = jnp.where(bottom, 0.0, new)
            x1_ref[row + HALO, :, :] = new
    for i in range(rows + 2 * HALO, x1_ref.shape[0]):
        x1_ref[i, :, :] = jnp.zeros((wide0, ch), F32)

    build(1)
    shift(x1_ref, 0, 0, cols)
    conv(cols)

    def keep1(row, branch):
        new = x1_ref[row + HALO, HALO : HALO + cols, :] + branch
        out_ref[row] = new.astype(BF) * mask_ref[row]

    inner(1, cols, keep1)


def shards(
    fields,
    wet_mask,
    conv_kernel,
    conv_bias,
    norm_gain,
    norm_bias,
    in_weight,
    in_bias,
    out_weight,
    out_bias,
    layer_scale,
):
    rows, cols, ch = fields.shape
    left, right, got_a, got_b, flags = exchange(fields, wet_mask)
    mask = jnp.broadcast_to(wet_mask.astype(BF)[:, :, None], fields.shape)
    state = fields * mask
    vec = jnp.stack([conv_bias, norm_gain, norm_bias, out_bias, layer_scale], axis=1)
    vectors = tap_vectors(conv_kernel)
    hid = in_weight.shape[2]
    width = 2 * ch // OUTS
    groups = ch // width
    wide0 = cols + 16
    octets = rows // OUTS
    cells = rows * cols
    vmem = pl.BlockSpec(memory_space=pltpu.VMEM)
    return pl.pallas_call(
        both_blocks,
        in_specs=[pl.BlockSpec(memory_space=pltpu.SMEM)] + [vmem] * 12,
        out_specs=vmem,
        out_shape=jax.ShapeDtypeStruct(fields.shape, BF),
        scratch_shapes=[
            pltpu.VMEM((rows + 2 * REACH, wide0 + 8, ch), F32),
            pltpu.VMEM((rows + 8, wide0, ch), F32),
            pltpu.VMEM((TAPS, groups, 2, octets + 1, wide0, ch), BF),
            pltpu.VMEM((groups, wide0 + 8, ch), F32),
            pltpu.VMEM((groups, TAPS * 2 * OUTS * width, OUTS * width), BF),
            pltpu.VMEM((groups, octets * wide0, OUTS * width), F32),
            pltpu.VMEM((2 * HALO, wide0, ch), F32),
            pltpu.VMEM((wide0 + 8, ch), F32),
        ],
        compiler_params=pltpu.CompilerParams(vmem_limit_bytes=VMEM_LIMIT),
        cost_estimate=pl.CostEstimate(
            flops=4 * cells * (4 * ch * hid + 8 * ch * 2 * ch), bytes_accessed=6 * cells * ch, transcendentals=2 * cells * hid
        ),
        name="both_blocks",
    )(flags, state, mask, left, right, got_a, got_b, conv_kernel, vectors, vec, in_weight, in_bias, out_weight)


def solution(mesh):
    return jax.shard_map(
        shards,
        mesh=mesh,
        in_specs=(P("lat", "lon", None), P("lat", "lon")) + (P(),) * 9,
        out_specs=P("lat", "lon", None),
        check_vma=False,
    )
```

time: 109 us -> 105 us (0.963)
  local copies, waits for them, and re-layouts: 12.9 us -> 21.4 us
  starting transfers between devices: 16.5 us -> 8.64 us
  other arithmetic: 6.4 us -> 4.78 us
  waiting for transfers between devices: 5.41 us -> 3.98 us
    another operation x0 -> x1, local copies, waits for them, and re-layouts: none -> 10.7 us  [tap_vectors(): stacked = jnp.stack(by_out, axis=4)]
    squeeze x4 -> x0, local copies, waits for them, and re-layouts: 8.73 us -> none  [the longest x1 6.68 us: shards(): w[b]]
    ppermute x2 -> x1, starting transfers between devices: 8.74 us -> 3.35 us  [exchange(): lax.ppermute(jnp.where(even, first, last), ('lat', 'lon'), partners(nlat,...]
    reshape x0 -> x3, local copies, waits for them, and re-layouts: none -> 4.94 us  [the longest x1 3.93 us: tap_vectors(): stacked.transpose(0, 3, 2, 1, 4, 5)]
    ppermute x4 -> x2, starting transfers between devices: 7.63 us -> 4.27 us  [the longest x1 2.18 us: exchange(): left = lax.ppermute(edge(0, rows, cols - REACH, cols), 'lon', up)]
    select_n x6 -> x1, other arithmetic: 2.88 us -> 0.16 us  [exchange(): jnp.where(even, first, last)]
    broadcast_in_dim x0 -> x1, local copies, waits for them, and re-layouts: none -> 1.84 us  [shards(): mask = jnp.broadcast_to(wet_mask.astype(BF)[:, :, None], fields.shape)]
    ppermute x4 -> x2, waiting for transfers between devices: 1.24 us -> 0.01 us  [the longest x1 0.01 us: exchange(): left = lax.ppermute(edge(0, rows, cols - REACH, cols), 'lon', up)]
  transfers between devices with their start and end apart: 8 -> 4, of which waited for: 4 -> 1; matrix products, arithmetic and copies ran while one was open for 10% -> 21% of each run, Pallas kernels for 4% -> 0%
where the time goes in v1:
time: 105 us; the launch traced here: 104 us
  Pallas kernels  65.1 us (62%)
  local copies, waits for them, and re-layouts  21.4 us (20%)
  starting transfers between devices  8.64 us (8%)
  other arithmetic  4.78 us (5%)
  waiting for transfers between devices  3.98 us (4%)
    pallas_call x1, Pallas kernels, shards(): pl.pallas_call(both_blocks, in_specs=[pl.BlockSpec(memory_space=pltpu.SME...  65.1 us
    another operation x1, local copies, waits for them, and re-layouts, tap_vectors(): stacked = jnp.stack(by_out, axis=4)  10.7 us
    ppermute x1, waiting for transfers between devices, exchange(): lax.ppermute(jnp.where(even, first, last), ('lat', 'lon'), partners(nlat,...  3.97 us
    reshape x1, local copies, waits for them, and re-layouts, tap_vectors(): stacked.transpose(0, 3, 2, 1, 4, 5)  3.93 us
    ppermute x1, starting transfers between devices, exchange(): lax.ppermute(jnp.where(even, first, last), ('lat', 'lon'), partners(nlat,...  3.35 us
    ppermute x1, starting transfers between devices, exchange(): left = lax.ppermute(edge(0, rows, cols - REACH, cols), 'lon', up)  2.18 us
  transfers between devices with their start and end apart: 4, of which 1 were waited for; matrix products, arithmetic and copies ran while one was open for 21% of the time, Pallas kernels for 0%

profile of v1, /device:TPU:1, one launch (start us, length us, event | category | flops | bytes accessed | tf_op | source)
XLA Modules:
  0.0 104.1 jit_solution(4769881802505995237)
XLA Ops:
  0.0 0.7 convert_element_type.6
  0.7 0.1 fusion.3
  0.8 1.1 %slice_multiply_fusion.2 = (bf16[48,6,128]{2,1,0:T(8,128)(2,1)S(1)}, bf16[48,6,128]{2,1,0:T(8,128)(2,1)S(1)}) fusion(bf16[48,128,128]{2,1,0:T(8,128)(2,1)} %param.11, bf16[48,6]{1,0:T(8,128)(2,1)S(1)} %get-tuple-element.25, bf16[48,6]{1,0:T(8,128)(2,1)S(1)} %get-tuple-element.26), kind=kLoop, calls=%fused_computation.15 | loop fusion | flops 73728 | bytes 296064 | tf_op jit(solution)/shard_map/mul | solution.py:41
  1.9 2.2 %collective-permute-start = (bf16[48,6,128]{2,1,0:T(8,128)(2,1)S(1)}, bf16[48,6,128]{2,1,0:T(8,128)(2,1)S(1)}, u32[]{:S(2)}, u32[]{:S(2)}) collective-permute-start(bf16[48,6,128]{2,1,0:T(8,128)(2,1)S(1)} %get-tuple-element.8), channel_id=1, source_target_pairs={{0,1},{1,2},{2,3},{3,0},{4,5},{5,6},{6,7},{7,4},{8,9},{9,10},{10,1... | collective-permute-start | bytes 221192 | tf_op jit(solution)/shard_map/ppermute | solution.py:45
  4.1 2.1 %collective-permute-start.1 = (bf16[48,6,128]{2,1,0:T(8,128)(2,1)S(1)}, bf16[48,6,128]{2,1,0:T(8,128)(2,1)}, u32[]{:S(2)}, u32[]{:S(2)}) collective-permute-start(bf16[48,6,128]{2,1,0:T(8,128)(2,1)S(1)} %get-tuple-element.7), channel_id=1, source_target_pairs={{1,0},{2,1},{3,2},{0,3},{5,4},{6,5},{7,6},{4,7},{9,8},{10,9},{11,1... | collective-permute-start | bytes 221192 | tf_op jit(solution)/shard_map/ppermute | solution.py:46
  6.2 1.0 reshape.11
  7.2 1.4 %copy.20.k_ref = f32[2,49,128]{2,1,0:T(8,128)} copy(f32[2,49,128]{2,0,1:T(2,128)} %param.13) | data formatting | bytes 100352 | tf_op args[2]
  8.7 1.0 pad_slice_fusion
  9.7 10.7 %stack.69 = f32[2,16,7,4,8,32]{5,4,1,2,3,0:T(8,128)} concatenate(f32[2,16,7,4,1,32]{5,4,1,2,3,0:T(1,128)} %bitcast.43, f32[2,16,7,4,1,32]{5,4,1,2,3,0:T(1,128)S(1)} %bitcast.37, f32[2,16,7,4,1,32]{5,4,1,2,3,0:T(1,128)S(1)} %bitcast.38, f32[2,16,7,4,1,32]{5,4,1,2,3,0:T(1,128)S(1)} %bitcast.39, f32[2,16,7,4,1,32]{5,4,1,2,3,0:T(1,128)S(1)} %bitcast.40, ...), dimensions={4} | concatenate | bytes 1835008 | tf_op jit(solution)/shard_map/stack | solution.py:62
  20.4 0.0 copy-start.5
  20.4 0.0 copy-start.6
  20.4 3.9 %reshape.12.kv_ref = f32[2,28,16,256]{3,2,1,0:T(8,128)} reshape(f32[2,4,7,16,8,32]{5,4,3,2,1,0:T(8,128)} %bitcast.35) | data formatting | bytes 1835008 | tf_op jit(solution)/shard_map/reshape | solution.py:63
  24.3 0.0 copy-done
  24.3 0.3 slice_multiply_fusion.1
  24.6 0.0 copy-done.2
  24.6 0.0 copy-done.3
  24.6 0.0 copy-done.4
  24.6 0.0 copy-done.5
  24.6 0.0 copy-done.6
  24.7 0.6 stack.75.vec_ref
  25.3 0.6 add_convert_fusion.flags_ref
  25.9 0.0 collective-permute-done.left_ref
  25.9 0.0 collective-permute-done.1.right_ref
  25.9 0.8 fusion.1
  26.7 0.2 broadcast_select_fusion
  26.8 1.0 collective-permute-start.2
  27.8 3.4 %collective-permute-start.3 = (bf16[6,140,128]{2,1,0:T(8,128)(2,1)S(1)}, bf16[6,140,128]{2,1,0:T(8,128)(2,1)S(1)}, u32[]{:S(2)}, u32[]{:S(2)}) collective-permute-start(bf16[6,140,128]{2,1,0:T(8,128)(2,1)S(1)} %get-tuple-element.9), channel_id=1, source_target_pairs={{4,8},{5,9},{6,10},{7,11},{8,4},{9,5},{10,6},{11,7},{12,16},{13,17... | collective-permute-start | bytes 645128 | tf_op jit(solution)/shard_map/ppermute | solution.py:51
  31.2 1.9 %broadcast_multiply_fusion.x_ref = bf16[48,128,128]{2,1,0:T(8,128)(2,1)} fusion(bf16[48,128,128]{2,1,0:T(8,128)(2,1)S(1)} %copy-done, bf16[48,128]{1,0:T(8,128)(2,1)S(1)} %convert_element_type.6), kind=kLoop, calls=%fused_computation.8 | loop fusion | flops 786432 | bytes 3158016 | tf_op jit(solution)/shard_map/mul | solution.py:279
  33.1 0.0 collective-permute-done.2.a_ref
  33.1 4.0 %collective-permute-done.3.b_ref = bf16[6,140,128]{2,1,0:T(8,128)(2,1)S(1)} collective-permute-done((bf16[6,140,128]{2,1,0:T(8,128)(2,1)S(1)}, bf16[6,140,128]{2,1,0:T(8,128)(2,1)S(1)}, u32[]{:S(2)}, u32[]{:S(2)}) %collective-permute-start.3) | collective-permute-done | bytes 215072 | tf_op jit(solution)/shard_map/ppermute | solution.py:51
  37.1 1.8 %broadcast_in_dim.2.mask_ref = bf16[48,128,128]{2,1,0:T(8,128)(2,1)} broadcast(bf16[48,128]{1,0:T(8,128)(2,1)S(1)} %convert_element_type.6), dimensions={0,1} | broadcast | bytes 1585152 | tf_op jit(solution)/shard_map/broadcast_in_dim | solution.py:278
  38.9 65.1 %both_blocks.1 = bf16[48,128,128]{2,1,0:T(8,128)(2,1)} custom-call(s32[3]{0:T(128)} %add_convert_fusion.flags_ref, bf16[48,128,128]{2,1,0:T(8,128)(2,1)} %broadcast_multiply_fusion.x_ref, bf16[48,128,128]{2,1,0:T(8,128)(2,1)} %broadcast_in_dim.2.mask_ref, bf16[48,6,128]{2,1,0:T(8,128)(2,1)} %copy-done.1, ...), custom_call_target="tpu_custom_call" | custom-call | flops 12884901888 | bytes 4718592 | tf_op jit(solution)/shard_map/both_blocks/pallas_call | solution.py:289
  (13 shorter events, 0.1 us)
Async XLA Ops:
  1.9 23.9 %collective-permute-start = (bf16[48,6,128]{2,1,0:T(8,128)(2,1)S(1)}, bf16[48,6,128]{2,1,0:T(8,128)(2,1)S(1)}, u32[]{:S(2)}, u32[]{:S(2)}) collective-permute-start(bf16[48,6,128]{2,1,0:T(8,128)(2,1)S(1)} %get-tuple-element.8), channel_id=1, source_target_pairs={{0,1},{1,2},{2,3},{3,0},{4,5},{5,6},{6,7},{7,4},{8,9},{9,10},{10,1... | collective-permute-start | bytes 221192 | tf_op jit(solution)/shard_map/ppermute | solution.py:45
  4.1 21.8 %collective-permute-start.1 = (bf16[48,6,128]{2,1,0:T(8,128)(2,1)S(1)}, bf16[48,6,128]{2,1,0:T(8,128)(2,1)}, u32[]{:S(2)}, u32[]{:S(2)}) collective-permute-start(bf16[48,6,128]{2,1,0:T(8,128)(2,1)S(1)} %get-tuple-element.7), channel_id=1, source_target_pairs={{1,0},{2,1},{3,2},{0,3},{5,4},{6,5},{7,6},{4,7},{9,8},{10,9},{11,1... | collective-permute-start | bytes 221192 | tf_op jit(solution)/shard_map/ppermute | solution.py:46
  20.4 4.0 %copy-start = (bf16[48,128,128]{2,1,0:T(8,128)(2,1)S(1)}, bf16[48,128,128]{2,1,0:T(8,128)(2,1)}, u32[]{:S(2)}) copy-start(bf16[48,128,128]{2,1,0:T(8,128)(2,1)} %param.11) | copy-start | bytes 4718596
  20.4 4.2 %copy-start.2 = (f32[2,128]{1,0:T(2,128)S(1)}, f32[2,128]{1,0:T(2,128)}, u32[]{:S(2)}) copy-start(f32[2,128]{1,0:T(2,128)} %param.14) | copy-start | bytes 3076
  20.4 4.3 %copy-start.3 = (f32[2,128]{1,0:T(2,128)S(1)}, f32[2,128]{1,0:T(2,128)}, u32[]{:S(2)}) copy-start(f32[2,128]{1,0:T(2,128)} %param.15) | copy-start | bytes 3076
  20.4 4.3 %copy-start.4 = (f32[2,128]{1,0:T(2,128)S(1)}, f32[2,128]{1,0:T(2,128)}, u32[]{:S(2)}) copy-start(f32[2,128]{1,0:T(2,128)} %param.16) | copy-start | bytes 3076
  20.4 4.3 %copy-start.5 = (f32[2,128]{1,0:T(2,128)S(1)}, f32[2,128]{1,0:T(2,128)}, u32[]{:S(2)}) copy-start(f32[2,128]{1,0:T(2,128)} %param.20) | copy-start | bytes 3076
  20.4 4.3 %copy-start.6 = (f32[2,128]{1,0:T(2,128)S(1)}, f32[2,128]{1,0:T(2,128)}, u32[]{:S(2)}) copy-start(f32[2,128]{1,0:T(2,128)} %param.21) | copy-start | bytes 3076
  25.9 7.2 %copy-start.1 = (bf16[48,6,128]{2,1,0:T(8,128)(2,1)}, bf16[48,6,128]{2,1,0:T(8,128)(2,1)S(1)}, u32[]{:S(2)}) copy-start(bf16[48,6,128]{2,1,0:T(8,128)(2,1)S(1)} %collective-permute-done.left_ref) | copy-start | bytes 221188
  26.8 6.3 %collective-permute-start.2 = (bf16[6,140,128]{2,1,0:T(8,128)(2,1)S(1)}, bf16[6,140,128]{2,1,0:T(8,128)(2,1)S(1)}, u32[]{:S(2)}, u32[]{:S(2)}) collective-permute-start(bf16[6,140,128]{2,1,0:T(8,128)(2,1)S(1)} %get-tuple-element.10), channel_id=1, source_target_pairs={{0,4},{1,5},{2,6},{3,7},{4,0},{5,1},{6,2},{7,3},{8,12},{9,13},{10,... | collective-permute-start | bytes 645128 | tf_op jit(solution)/shard_map/ppermute | solution.py:50
  27.8 9.2 %collective-permute-start.3 = (bf16[6,140,128]{2,1,0:T(8,128)(2,1)S(1)}, bf16[6,140,128]{2,1,0:T(8,128)(2,1)S(1)}, u32[]{:S(2)}, u32[]{:S(2)}) collective-permute-start(bf16[6,140,128]{2,1,0:T(8,128)(2,1)S(1)} %get-tuple-element.9), channel_id=1, source_target_pairs={{4,8},{5,9},{6,10},{7,11},{8,4},{9,5},{10,6},{11,7},{12,16},{13,17... | collective-permute-start | bytes 645128 | tf_op jit(solution)/shard_map/ppermute | solution.py:51
  33.1 5.8 %copy-start.7 = (bf16[6,140,128]{2,1,0:T(8,128)(2,1)}, bf16[6,140,128]{2,1,0:T(8,128)(2,1)S(1)}, u32[]{:S(2)}) copy-start(bf16[6,140,128]{2,1,0:T(8,128)(2,1)S(1)} %collective-permute-done.2.a_ref) | copy-start | bytes 645124
  37.1 1.9 %copy-start.8 = (bf16[6,140,128]{2,1,0:T(8,128)(2,1)}, bf16[6,140,128]{2,1,0:T(8,128)(2,1)S(1)}, u32[]{:S(2)}) copy-start(bf16[6,140,128]{2,1,0:T(8,128)(2,1)S(1)} %collective-permute-done.3.b_ref) | copy-start | bytes 645124

commit v2 on v1

--- a/solution.py
+++ b/solution.py
@@ -1,5 +1,3 @@
-import functools
-
 import jax
 import jax.numpy as jnp
 from jax import lax
@@ -14,7 +12,7 @@
 REACH = 2 * HALO
 OUTS = 8
 VMEM_LIMIT = 62 * 1024 * 1024
-ERF_POLY = (0.7978323547267507, 0.036463673384825215, -0.0001230322006747663, -3.081922192956723e-05, 1.128904780388478e-06)
+ERF_POLY = (0.7975078797359708, 0.03700565107996738, -0.0003515176683895368)
 
 
 def partners(nlat, nlon, parity):
@@ -49,18 +47,7 @@
     even = lat % 2 == 0
     got_a = lax.ppermute(jnp.where(even, last, first), ("lat", "lon"), partners(nlat, nlon, 0))
     got_b = lax.ppermute(jnp.where(even, first, last), ("lat", "lon"), partners(nlat, nlon, 1))
-    flags = jnp.stack([even, lat == nlat - 1, lat == 0]).astype(jnp.int32)
-    return left, right, got_a, got_b, flags
-
-
-def tap_vectors(conv_kernel):
-    blocks, _, ch = conv_kernel.shape
-    width = 2 * ch // OUTS
-    taps = conv_kernel.reshape(blocks, TAPS, TAPS, ch // width, width)
-    taps = jnp.pad(taps, ((0, 0), (OUTS - 1, 2 * OUTS - TAPS), (0, 0), (0, 0), (0, 0)))
-    by_out = [taps[:, OUTS - 1 - o : 3 * OUTS - 1 - o] for o in range(OUTS)]
-    stacked = jnp.stack(by_out, axis=4)
-    return stacked.transpose(0, 3, 2, 1, 4, 5).reshape(blocks, ch // width * TAPS, 2 * OUTS, OUTS * width)
+    return left, right, got_a, got_b
 
 
 def regroup(parts, width):
@@ -80,7 +67,6 @@
 
 
 def both_blocks(
-    flags_ref,
     x_ref,
     mask_ref,
     left_ref,
@@ -88,11 +74,14 @@
     a_ref,
     b_ref,
     k_ref,
-    kv_ref,
-    vec_ref,
+    cbias_ref,
+    gain_ref,
+    nbias_ref,
     inw_ref,
     inb_ref,
     outw_ref,
+    outb_ref,
+    scale_ref,
     out_ref,
     x0_ref,
     x1_ref,
@@ -102,6 +91,7 @@
     acc_ref,
     strip_ref,
     flip_ref,
+    kv_ref,
 ):
     rows, cols, ch = x_ref.shape
     width = 2 * ch // OUTS
@@ -113,7 +103,8 @@
     ext = cols + 2 * REACH
     lead = base - REACH
     total = x0_ref.shape[1]
-    even, top, bottom = (flags_ref[i] == 1 for i in range(3))
+    lat = lax.axis_index("lat")
+    even, top, bottom = lat % 2 == 0, lat == lax.axis_size("lat") - 1, lat == 0
 
     def fill(i, carry):
         x0_ref[i + REACH, 0:base, :] = jnp.zeros((base, ch), F32)
@@ -141,29 +132,42 @@
         jnp.int32, (width, OUTS * width), 0
     )
 
+    lanes = OUTS * width
+    out_row = lax.broadcasted_iota(jnp.int32, (TAPS, lanes), 1) // width
+
     def build(b):
-        for s in range(TAPS):
-            def one(gr, carry):
-                for a in range(2 * OUTS):
-                    vec = kv_ref[b, gr * TAPS + s, a : a + 1, :]
-                    w_ref[gr, (s * 2 * OUTS + a) * width : (s * 2 * OUTS + a + 1) * width, :] = jnp.where(
-                        own, vec, 0.0
-                    ).astype(BF)
-                return carry
-
-            lax.fori_loop(0, groups, one, 0)
+        down = [k_ref[b, TAPS * r : TAPS * (r + 1), :] for r in range(TAPS - 1, -1, -1)]
+        down.append(jnp.zeros((TAPS, ch), F32))
+        halves = [regroup(down[i : i + groups], width) for i in range(0, OUTS, groups)]
+        for gr in range(groups):
+            line = jnp.concatenate([half[gr] for half in halves], axis=1)
+            for a in range(2 * OUTS):
+                turned = pltpu.roll(line, (a - TAPS + 1) * width % lanes, 1)
+                seen = (out_row <= a) & (out_row >= a - TAPS + 1)
+                kv_ref[gr, a, 0:TAPS, :] = jnp.where(seen, turned, 0.0)
+
+        def one(i, carry):
+            gr, s = i // TAPS, i % TAPS
+            for a in range(2 * OUTS):
+                vec = kv_ref[gr, a, pl.ds(s, 1), :]
+                at = pl.multiple_of(s * (2 * OUTS * width), 2 * OUTS * width) + a * width
+                w_ref[gr, pl.ds(at, width), :] = jnp.where(own, vec, 0.0).astype(BF)
+            return carry
+
+        lax.fori_loop(0, groups * TAPS, one, 0)
 
     def shift(src_ref, row0, col0, wide):
-        span = wide + 8
-
         def one(q, carry):
             parts = [src_ref[row0 + 4 * q + j, :, :] for j in range(groups)]
             for j, part in enumerate(regroup(parts, width)):
                 group_ref[j, 0 : part.shape[0], :] = part
-            for s in range(TAPS):
+
+            def column(s, inside):
                 for j in range(groups):
-                    shifted_ref[s, j, q % 2, q // 2, 0:wide, :] = group_ref[j, col0 + s : col0 + s + wide, :].astype(BF)
-            return carry
+                    shifted_ref[s, j, q % 2, q // 2, 0:wide, :] = group_ref[j, pl.ds(col0 + s, wide), :].astype(BF)
+                return inside
+
+            return lax.fori_loop(0, TAPS, column, carry)
 
         lax.fori_loop(0, quads, one, 0)
 
@@ -181,22 +185,33 @@
 
         lax.fori_loop(0, groups, one, 0)
 
-    def mlp(b, conv_rows):
-        conv_bias, gain, nbias, outb, scale = (vec_ref[b, i : i + 1, :] for i in range(5))
-        val = jnp.concatenate(conv_rows, axis=0) + conv_bias
-        mean = jnp.mean(val, axis=-1, keepdims=True)
-        cen = val - mean
-        var = jnp.mean(cen * cen, axis=-1, keepdims=True)
-        normed = (cen * lax.rsqrt(var + 1e-6) * gain + nbias).astype(BF)
-        h = jnp.dot(normed, inw_ref[b], preferred_element_type=F32) + inb_ref[b : b + 1, :]
+    def gelu_twice(h):
         z = h * h
         p = jnp.full_like(z, ERF_POLY[-1])
         for coef in ERF_POLY[-2::-1]:
-            p = p * z + coef
-        t = jnp.tanh(h * p)
-        twice = (h + h * t).astype(BF)
-        branch = jnp.dot(twice, outw_ref[b], preferred_element_type=F32) * (0.5 * scale) + outb * scale
+            p = p * z + jnp.asarray(coef, z.dtype)
+        return h + h * jnp.tanh(h * p)
+
+    def norm(b, val):
+        val = val + cbias_ref[b : b + 1, :]
+        cen = val - jnp.mean(val, axis=-1, keepdims=True)
+        var = jnp.mean(cen * cen, axis=-1, keepdims=True)
+        return (cen * lax.rsqrt(var + 1e-6) * gain_ref[b : b + 1, :] + nbias_ref[b : b + 1, :]).astype(BF)
+
+    def mlp(b, conv_rows):
         n = conv_rows[0].shape[0]
+        normed = jnp.concatenate([norm(b, row) for row in conv_rows], axis=0)
+        tile = n // 3 if n % 48 == 0 else n // 2
+        branch = None
+        half_hid = inw_ref.shape[2] // 2
+        for c in range(0, 2 * half_hid, half_hid):
+            hid = jnp.dot(normed, inw_ref[b, :, c : c + half_hid], preferred_element_type=F32)
+            bias = inb_ref[b : b + 1, c : c + half_hid]
+            act = [gelu_twice((hid[i : i + tile] + bias).astype(BF)) for i in range(0, hid.shape[0], tile)]
+            part = jnp.dot(jnp.concatenate(act, axis=0), outw_ref[b, c : c + half_hid, :], preferred_element_type=F32)
+            branch = part if branch is None else branch + part
+        scale = scale_ref[b : b + 1, :]
+        branch = branch * (0.5 * scale) + outb_ref[b : b + 1, :] * scale
         return [branch[i * n : (i + 1) * n] for i in range(len(conv_rows))]
 
     def inner(b, wide, emit):
@@ -274,11 +289,9 @@
     layer_scale,
 ):
     rows, cols, ch = fields.shape
-    left, right, got_a, got_b, flags = exchange(fields, wet_mask)
+    left, right, got_a, got_b = exchange(fields, wet_mask)
     mask = jnp.broadcast_to(wet_mask.astype(BF)[:, :, None], fields.shape)
     state = fields * mask
-    vec = jnp.stack([conv_bias, norm_gain, norm_bias, out_bias, layer_scale], axis=1)
-    vectors = tap_vectors(conv_kernel)
     hid = in_weight.shape[2]
     width = 2 * ch // OUTS
     groups = ch // width
@@ -288,7 +301,7 @@
     vmem = pl.BlockSpec(memory_space=pltpu.VMEM)
     return pl.pallas_call(
         both_blocks,
-        in_specs=[pl.BlockSpec(memory_space=pltpu.SMEM)] + [vmem] * 12,
+        in_specs=[vmem] * 15,
         out_specs=vmem,
         out_shape=jax.ShapeDtypeStruct(fields.shape, BF),
         scratch_shapes=[
@@ -300,13 +313,30 @@
             pltpu.VMEM((groups, octets * wide0, OUTS * width), F32),
             pltpu.VMEM((2 * HALO, wide0, ch), F32),
             pltpu.VMEM((wide0 + 8, ch), F32),
+            pltpu.VMEM((groups, 2 * OUTS, 8, OUTS * width), F32),
         ],
         compiler_params=pltpu.CompilerParams(vmem_limit_bytes=VMEM_LIMIT),
         cost_estimate=pl.CostEstimate(
             flops=4 * cells * (4 * ch * hid + 8 * ch * 2 * ch), bytes_accessed=6 * cells * ch, transcendentals=2 * cells * hid
         ),
         name="both_blocks",
-    )(flags, state, mask, left, right, got_a, got_b, conv_kernel, vectors, vec, in_weight, in_bias, out_weight)
+    )(
+        state,
+        mask,
+        left,
+        right,
+        got_a,
+        got_b,
+        conv_kernel,
+        conv_bias,
+        norm_gain,
+        norm_bias,
+        in_weight,
+        in_bias,
+        out_weight,
+        out_bias,
+        layer_scale,
+    )
 
 
 def solution(mesh):

time: 105 us -> 91.3 us (0.87)
  local copies, waits for them, and re-layouts: 21.4 us -> 3.4 us
  Pallas kernels: 65.1 us -> 67.2 us
  waiting for transfers between devices: 3.98 us -> 5.61 us
    another operation x2 -> x0, local copies, waits for them, and re-layouts: 11.3 us -> none  [the longest x1 10.7 us: tap_vectors(): stacked = jnp.stack(by_out, axis=4)]
    reshape x3 -> x0, local copies, waits for them, and re-layouts: 4.94 us -> none  [the longest x1 3.93 us: tap_vectors(): stacked.transpose(0, 3, 2, 1, 4, 5)]
    ppermute x1, waiting for transfers between devices: 0.01 us -> 2.51 us  [exchange(): left = lax.ppermute(edge(0, rows, cols - REACH, cols), 'lon', up)]
    ppermute x1, starting transfers between devices: 2.18 us -> 0.01 us  [exchange(): left = lax.ppermute(edge(0, rows, cols - REACH, cols), 'lon', up)]
    ppermute x1, starting transfers between devices: 2.09 us -> 4.2 us  [exchange(): right = lax.ppermute(edge(0, rows, 0, REACH), 'lon', down)]
    pallas_call x1, Pallas kernels: 65.1 us -> 67.2 us  [shards(): pl.pallas_call(both_blocks, in_specs=[vmem] * 15, out_specs=vmem, out_sha...]
    ppermute x1, starting transfers between devices: 3.35 us -> 5.11 us  [exchange(): lax.ppermute(jnp.where(even, first, last), ('lat', 'lon'), partners(nlat,...]
  transfers between devices with their start and end apart: 4 -> 4, of which waited for: 1 -> 2; matrix products, arithmetic and copies ran while one was open for 21% -> 5% of each run, Pallas kernels for 0% -> 0%
where the time goes in v2:
time: 91.3 us; the launch traced here: 91 us
  Pallas kernels  67.2 us (74%)
  starting transfers between devices  9.39 us (10%)
  waiting for transfers between devices  5.61 us (6%)
  other arithmetic  5.32 us (6%)
  local copies, waits for them, and re-layouts  3.4 us (4%)
    pallas_call x1, Pallas kernels, shards(): pl.pallas_call(both_blocks, in_specs=[vmem] * 15, out_specs=vmem, out_sha...  67.2 us
    ppermute x1, starting transfers between devices, exchange(): lax.ppermute(jnp.where(even, first, last), ('lat', 'lon'), partners(nlat,...  5.11 us
    ppermute x1, starting transfers between devices, exchange(): right = lax.ppermute(edge(0, rows, 0, REACH), 'lon', down)  4.2 us
    ppermute x1, waiting for transfers between devices, exchange(): lax.ppermute(jnp.where(even, first, last), ('lat', 'lon'), partners(nlat,...  3.09 us
    ppermute x1, waiting for transfers between devices, exchange(): left = lax.ppermute(edge(0, rows, cols - REACH, cols), 'lon', up)  2.51 us
    mul x2, other arithmetic, edge(): return fields[r0:r1, c0:c1] * wet_mask[r0:r1, c0:c1].astype(BF)[:, :, None]  2.4 us
    mul x1, other arithmetic, shards(): state = fields * mask  1.9 us
    broadcast_in_dim x1, local copies, waits for them, and re-layouts, shards(): mask = jnp.broadcast_to(wet_mask.astype(BF)[:, :, None], fields.shape)  1.86 us
  transfers between devices with their start and end apart: 4, of which 2 were waited for; matrix products, arithmetic and copies ran while one was open for 5% of the time, Pallas kernels for 0%

profile of v2, /device:TPU:1, one launch (start us, length us, event | category | flops | bytes accessed | tf_op | source)
XLA Modules:
  0.0 91.0 jit_solution(6158721937438387342)
XLA Ops:
  0.0 0.0 copy-start
  0.0 0.9 convert_element_type.2
  0.9 0.1 fusion.3
  0.9 1.1 %slice_multiply_fusion.2 = (bf16[48,6,128]{2,1,0:T(8,128)(2,1)S(1)}, bf16[48,6,128]{2,1,0:T(8,128)(2,1)S(1)}) fusion(bf16[48,128,128]{2,1,0:T(8,128)(2,1)} %param.11, bf16[48,6]{1,0:T(8,128)(2,1)S(1)} %get-tuple-element.17, bf16[48,6]{1,0:T(8,128)(2,1)S(1)} %get-tuple-element.18), kind=kLoop, calls=%fused_computation.7 | loop fusion | flops 73728 | bytes 296064 | tf_op jit(solution)/shard_map/mul | solution.py:39
  2.1 4.2 %collective-permute-start.1 = (bf16[48,6,128]{2,1,0:T(8,128)(2,1)S(1)}, bf16[48,6,128]{2,1,0:T(8,128)(2,1)S(1)}, u32[]{:S(2)}, u32[]{:S(2)}) collective-permute-start(bf16[48,6,128]{2,1,0:T(8,128)(2,1)S(1)} %get-tuple-element.7), channel_id=1, source_target_pairs={{1,0},{2,1},{3,2},{0,3},{5,4},{6,5},{7,6},{4,7},{9,8},{10,9},{11,1... | collective-permute-start | bytes 221192 | tf_op jit(solution)/shard_map/ppermute | solution.py:44
  6.3 0.0 collective-permute-start
  6.3 1.3 %slice_multiply_fusion.1 = (bf16[6,128,128]{2,1,0:T(8,128)(2,1)S(1)}, bf16[6,128,128]{2,1,0:T(8,128)(2,1)S(1)}) fusion(bf16[48,128,128]{2,1,0:T(8,128)(2,1)} %param.11, bf16[6,128]{1,0:T(8,128)(2,1)S(1)} %get-tuple-element.15, bf16[6,128]{1,0:T(8,128)(2,1)S(1)} %get-tuple-element.16), kind=kLoop, calls=%fused_computation.6 | loop fusion | flops 196608 | bytes 789504 | tf_op jit(solution)/shard_map/mul | solution.py:39
  7.6 1.4 %copy.12.k_ref = f32[2,49,128]{2,1,0:T(8,128)} copy(f32[2,49,128]{2,0,1:T(2,128)} %param.13) | data formatting | bytes 100352 | tf_op args[2]
  9.0 0.0 collective-permute-done.1.right_ref
  9.0 0.0 copy-start.1
  9.0 2.5 %collective-permute-done.left_ref = bf16[48,6,128]{2,1,0:T(8,128)(2,1)S(1)} collective-permute-done((bf16[48,6,128]{2,1,0:T(8,128)(2,1)S(1)}, bf16[48,6,128]{2,1,0:T(8,128)(2,1)S(1)}, u32[]{:S(2)}, u32[]{:S(2)}) %collective-permute-start) | collective-permute-done | bytes 73760 | tf_op jit(solution)/shard_map/ppermute | solution.py:43
  11.5 0.0 copy-start.2
  11.5 0.2 broadcast_select_fusion
  11.7 5.1 %collective-permute-start.3 = (bf16[6,140,128]{2,1,0:T(8,128)(2,1)S(1)}, bf16[6,140,128]{2,1,0:T(8,128)(2,1)S(1)}, u32[]{:S(2)}, u32[]{:S(2)}) collective-permute-start(bf16[6,140,128]{2,1,0:T(8,128)(2,1)S(1)} %get-tuple-element.9), channel_id=1, source_target_pairs={{4,8},{5,9},{6,10},{7,11},{8,4},{9,5},{10,6},{11,7},{12,16},{13,17... | collective-permute-start | bytes 645128 | tf_op jit(solution)/shard_map/ppermute | solution.py:49
  16.8 0.1 collective-permute-start.2
  16.9 0.0 copy-done
  16.9 1.9 %broadcast_multiply_fusion.x_ref = bf16[48,128,128]{2,1,0:T(8,128)(2,1)} fusion(bf16[48,128,128]{2,1,0:T(8,128)(2,1)S(1)} %copy-done, bf16[48,128]{1,0:T(8,128)(2,1)S(1)} %convert_element_type.2), kind=kLoop, calls=%fused_computation | loop fusion | flops 786432 | bytes 3158016 | tf_op jit(solution)/shard_map/mul | solution.py:294
  18.8 0.0 copy-done.1
  18.8 0.0 copy-done.2
  18.8 3.1 %collective-permute-done.3.b_ref = bf16[6,140,128]{2,1,0:T(8,128)(2,1)S(1)} collective-permute-done((bf16[6,140,128]{2,1,0:T(8,128)(2,1)S(1)}, bf16[6,140,128]{2,1,0:T(8,128)(2,1)S(1)}, u32[]{:S(2)}, u32[]{:S(2)}) %collective-permute-start.3) | collective-permute-done | bytes 215072 | tf_op jit(solution)/shard_map/ppermute | solution.py:49
  21.9 0.0 copy-start.3
  21.9 0.0 collective-permute-done.2.a_ref
  21.9 0.0 copy-start.4
  21.9 1.9 %broadcast_in_dim.2.mask_ref = bf16[48,128,128]{2,1,0:T(8,128)(2,1)} broadcast(bf16[48,128]{1,0:T(8,128)(2,1)S(1)} %convert_element_type.2), dimensions={0,1} | broadcast | bytes 1585152 | tf_op jit(solution)/shard_map/broadcast_in_dim | solution.py:293
  23.8 0.0 copy-done.3
  23.8 0.0 copy-done.4
  23.8 67.2 %both_blocks.1 = bf16[48,128,128]{2,1,0:T(8,128)(2,1)} custom-call(bf16[48,128,128]{2,1,0:T(8,128)(2,1)} %broadcast_multiply_fusion.x_ref, bf16[48,128,128]{2,1,0:T(8,128)(2,1)} %broadcast_in_dim.2.mask_ref, bf16[48,6,128]{2,1,0:T(8,128)(2,1)} %copy-done.2, bf16[48,6,128]{2,1,0:T(8,128)(2,1)} %copy-done.1, bf16[6,140,128]{2,1,0:T(8,128)(2,1)} %copy-done.4, ...), custom_call_target="tpu_custom_call" | custom-call | flops 12884901888 | bytes 4718592 | tf_op jit(solution)/shard_map/both_blocks/pallas_call | solution.py:302
  (3 shorter events, 0.0 us)
Async XLA Ops:
  0.0 16.9 %copy-start = (bf16[48,128,128]{2,1,0:T(8,128)(2,1)S(1)}, bf16[48,128,128]{2,1,0:T(8,128)(2,1)}, u32[]{:S(2)}) copy-start(bf16[48,128,128]{2,1,0:T(8,128)(2,1)} %param.11) | copy-start | bytes 4718596
  2.1 6.9 %collective-permute-start.1 = (bf16[48,6,128]{2,1,0:T(8,128)(2,1)S(1)}, bf16[48,6,128]{2,1,0:T(8,128)(2,1)S(1)}, u32[]{:S(2)}, u32[]{:S(2)}) collective-permute-start(bf16[48,6,128]{2,1,0:T(8,128)(2,1)S(1)} %get-tuple-element.7), channel_id=1, source_target_pairs={{1,0},{2,1},{3,2},{0,3},{5,4},{6,5},{7,6},{4,7},{9,8},{10,9},{11,1... | collective-permute-start | bytes 221192 | tf_op jit(solution)/shard_map/ppermute | solution.py:44
  6.3 5.3 %collective-permute-start = (bf16[48,6,128]{2,1,0:T(8,128)(2,1)S(1)}, bf16[48,6,128]{2,1,0:T(8,128)(2,1)S(1)}, u32[]{:S(2)}, u32[]{:S(2)}) collective-permute-start(bf16[48,6,128]{2,1,0:T(8,128)(2,1)S(1)} %get-tuple-element.8), channel_id=1, source_target_pairs={{0,1},{1,2},{2,3},{3,0},{4,5},{5,6},{6,7},{7,4},{8,9},{9,10},{10,1... | collective-permute-start | bytes 221192 | tf_op jit(solution)/shard_map/ppermute | solution.py:43
  9.0 9.8 %copy-start.1 = (bf16[48,6,128]{2,1,0:T(8,128)(2,1)}, bf16[48,6,128]{2,1,0:T(8,128)(2,1)S(1)}, u32[]{:S(2)}) copy-start(bf16[48,6,128]{2,1,0:T(8,128)(2,1)S(1)} %collective-permute-done.1.right_ref) | copy-start | bytes 221188
  11.5 7.3 %copy-start.2 = (bf16[48,6,128]{2,1,0:T(8,128)(2,1)}, bf16[48,6,128]{2,1,0:T(8,128)(2,1)S(1)}, u32[]{:S(2)}) copy-start(bf16[48,6,128]{2,1,0:T(8,128)(2,1)S(1)} %collective-permute-done.left_ref) | copy-start | bytes 221188
  11.7 10.2 %collective-permute-start.3 = (bf16[6,140,128]{2,1,0:T(8,128)(2,1)S(1)}, bf16[6,140,128]{2,1,0:T(8,128)(2,1)S(1)}, u32[]{:S(2)}, u32[]{:S(2)}) collective-permute-start(bf16[6,140,128]{2,1,0:T(8,128)(2,1)S(1)} %get-tuple-element.9), channel_id=1, source_target_pairs={{4,8},{5,9},{6,10},{7,11},{8,4},{9,5},{10,6},{11,7},{12,16},{13,17... | collective-permute-start | bytes 645128 | tf_op jit(solution)/shard_map/ppermute | solution.py:49
  16.8 5.1 %collective-permute-start.2 = (bf16[6,140,128]{2,1,0:T(8,128)(2,1)S(1)}, bf16[6,140,128]{2,1,0:T(8,128)(2,1)S(1)}, u32[]{:S(2)}, u32[]{:S(2)}) collective-permute-start(bf16[6,140,128]{2,1,0:T(8,128)(2,1)S(1)} %get-tuple-element.10), channel_id=1, source_target_pairs={{0,4},{1,5},{2,6},{3,7},{4,0},{5,1},{6,2},{7,3},{8,12},{9,13},{10,... | collective-permute-start | bytes 645128 | tf_op jit(solution)/shard_map/ppermute | solution.py:48
  21.9 1.9 %copy-start.3 = (bf16[6,140,128]{2,1,0:T(8,128)(2,1)}, bf16[6,140,128]{2,1,0:T(8,128)(2,1)S(1)}, u32[]{:S(2)}) copy-start(bf16[6,140,128]{2,1,0:T(8,128)(2,1)S(1)} %collective-permute-done.3.b_ref) | copy-start | bytes 645124
  21.9 1.9 %copy-start.4 = (bf16[6,140,128]{2,1,0:T(8,128)(2,1)}, bf16[6,140,128]{2,1,0:T(8,128)(2,1)S(1)}, u32[]{:S(2)}) copy-start(bf16[6,140,128]{2,1,0:T(8,128)(2,1)S(1)} %collective-permute-done.2.a_ref) | copy-start | bytes 645124

commit v3 on v2

v3 whole, which is shorter than its diff:
```python
import jax
import jax.numpy as jnp
from jax import lax
from jax.experimental import pallas as pl
from jax.experimental.pallas import tpu as pltpu
from jax.sharding import PartitionSpec as P

BF = jnp.bfloat16
F32 = jnp.float32
TAPS = 7
HALO = 3
REACH = 2 * HALO
OUTS = 8
ROLLED = jnp.bfloat16
VMEM_LIMIT = 48 * 1024 * 1024
ERF_POLY = (0.7975078797359708, 0.03700565107996738, -0.0003515176683895368)


def partners(nlat, nlon, parity):
    route = []
    for lat in range(nlat):
        for lon in range(nlon):
            here = lat * nlon + lon
            if lat % 2 == parity:
                there = here + nlon if lat + 1 < nlat else lat * nlon + nlon - 1 - lon
            elif lat > 0:
                there = here - nlon
            else:
                continue
            route.append((here, there))
    return route


def exchange(fields, wet_mask):
    nlat, nlon = lax.axis_size("lat"), lax.axis_size("lon")
    lat = lax.axis_index("lat")
    rows, cols = wet_mask.shape

    def edge(r0, r1, c0, c1):
        return fields[r0:r1, c0:c1] * wet_mask[r0:r1, c0:c1].astype(BF)[:, :, None]

    up = [(i, (i + 1) % nlon) for i in range(nlon)]
    down = [(j, i) for i, j in up]
    left = lax.ppermute(edge(0, rows, cols - REACH, cols), "lon", up)
    right = lax.ppermute(edge(0, rows, 0, REACH), "lon", down)
    first = jnp.concatenate([left[:REACH], edge(0, REACH, 0, cols), right[:REACH]], axis=1)
    last = jnp.concatenate([left[rows - REACH :], edge(rows - REACH, rows, 0, cols), right[rows - REACH :]], axis=1)
    even = lat % 2 == 0
    got_a = lax.ppermute(jnp.where(even, last, first), ("lat", "lon"), partners(nlat, nlon, 0))
    got_b = lax.ppermute(jnp.where(even, first, last), ("lat", "lon"), partners(nlat, nlon, 1))
    return left, right, got_a, got_b


def regroup(parts, width):
    parts = list(parts)
    ch = parts[0].shape[-1]
    block = lax.broadcasted_iota(jnp.int32, parts[0].shape, parts[0].ndim - 1) // width
    step = 1
    while step < len(parts):
        low = (block & step) == 0
        for i in range(len(parts)):
            if not i & step:
                x, y = parts[i], parts[i + step]
                parts[i] = jnp.where(low, x, pltpu.roll(y, step * width, x.ndim - 1))
                parts[i + step] = jnp.where(low, pltpu.roll(x, ch - step * width, x.ndim - 1), y)
        step *= 2
    return parts


def tap_kernel(k_ref, w_ref, kv_ref):
    ch = k_ref.shape[2]
    lanes = w_ref.shape[3]
    width = lanes // OUTS
    groups = ch // width
    gr = pl.program_id(1)

    @pl.when(gr == 0)
    def _():
        down = [k_ref[0, pl.ds(s, TAPS, stride=TAPS), :] for s in range(TAPS - 1, -1, -1)]
        down.append(jnp.zeros((TAPS, ch), F32))
        halves = [regroup(down[i : i + groups], width) for i in range(0, OUTS, groups)]
        out_col = lax.broadcasted_iota(jnp.int32, (TAPS, lanes), 1) // width
        for g in range(groups):
            line = jnp.concatenate([half[g] for half in halves], axis=1)
            for p in range(2 * OUTS):
                turned = pltpu.roll(line, (p - TAPS + 1) * width % lanes, 1)
                seen = (out_col <= p) & (out_col >= p - TAPS + 1)
                kv_ref[g, p, 0:TAPS, :] = jnp.where(seen, turned, 0.0)

    lane = lax.broadcasted_iota(jnp.int32, (width, lanes), 1)
    own = (lane % width) == lax.broadcasted_iota(jnp.int32, (width, lanes), 0)
    for r in range(TAPS):
        for p in range(2 * OUTS):
            vec = kv_ref[gr, p, r : r + 1, :]
            at = (r * 2 * OUTS + p) * width
            w_ref[0, 0, at : at + width, :] = jnp.where(own, vec, 0.0).astype(BF)


def tap_matrices(conv_kernel):
    blocks, taps, ch = conv_kernel.shape
    lanes = 2 * ch
    width = lanes // OUTS
    groups = ch // width
    depth = TAPS * 2 * OUTS * width
    return pl.pallas_call(
        tap_kernel,
        grid=(blocks, groups),
        in_specs=[pl.BlockSpec((1, taps, ch), lambda b, g: (b, 0, 0))],
        out_specs=pl.BlockSpec((1, 1, depth, lanes), lambda b, g: (b, g, 0, 0)),
        out_shape=jax.ShapeDtypeStruct((blocks, groups, depth, lanes), BF),
        scratch_shapes=[pltpu.VMEM((groups, 2 * OUTS, 8, lanes), F32)],
        compiler_params=pltpu.CompilerParams(vmem_limit_bytes=24 * 1024 * 1024),
        cost_estimate=pl.CostEstimate(
            flops=0, bytes_accessed=2 * blocks * groups * depth * lanes, transcendentals=0
        ),
        name="tap_matrices",
    )(conv_kernel)


def both_blocks(
    x_ref,
    mask_ref,
    left_ref,
    right_ref,
    a_ref,
    b_ref,
    k_ref,
    w_hbm,
    cbias_ref,
    gain_ref,
    nbias_ref,
    inw_ref,
    inb_ref,
    outw_ref,
    outb_ref,
    scale_ref,
    out_ref,
    x0_ref,
    x1_ref,
    relaid_ref,
    w_ref,
    acc_ref,
    strip_ref,
    flip_ref,
    w_sem,
):
    rows, cols, ch = x_ref.shape
    width = 2 * ch // OUTS
    groups = ch // width
    octets = cols // OUTS
    base = 8
    ext = cols + 2 * REACH
    lead = base - REACH
    near = base - HALO
    pitch = cols + 24
    wide0 = cols + 16
    lat = lax.axis_index("lat")
    even, top, bottom = lat % 2 == 0, lat == lax.axis_size("lat") - 1, lat == 0

    copies = [pltpu.make_async_copy(w_hbm.at[b], w_ref.at[b], w_sem.at[b]) for b in range(2)]
    for copy in copies:
        copy.start()

    def line(row):
        return pl.multiple_of((row + REACH) * pitch, 8)

    def fill(i, carry):
        at = line(i)
        x0_ref[pl.ds(at, base), :] = jnp.zeros((base, ch), F32)
        x0_ref[pl.ds(at + lead, REACH), :] = left_ref[i].astype(F32)
        x0_ref[pl.ds(at + base, cols), :] = x_ref[i].astype(F32)
        x0_ref[pl.ds(at + base + cols, 16), :] = jnp.zeros((16, ch), F32)
        x0_ref[pl.ds(at + base + cols, REACH), :] = right_ref[i].astype(F32)
        x1_ref[pl.ds(at, base), :] = jnp.zeros((base, ch), F32)
        x1_ref[pl.ds(at + base + cols, 16), :] = jnp.zeros((16, ch), F32)
        return carry

    lax.fori_loop(0, rows, fill, 0)
    flip_ref[...] = jnp.zeros(flip_ref.shape, F32)
    at = lax.broadcasted_iota(jnp.int32, (wide0, wide0), 0)
    to = lax.broadcasted_iota(jnp.int32, (wide0, wide0), 1)
    mirror = jnp.where(to == jnp.where(top, ext - 1 - at, at), 1.0, 0.0).astype(BF)
    for i in range(REACH):
        south, north = i * pitch, (rows + REACH + i) * pitch
        x0_ref[south : south + pitch, :] = jnp.zeros((pitch, ch), F32)
        x0_ref[south + lead : south + lead + ext, :] = jnp.where(even, b_ref[i].astype(F32), a_ref[i].astype(F32))
        src = jnp.where(top, REACH - 1 - i, i)
        flip_ref[0:ext, :] = jnp.where(even, a_ref[src].astype(F32), b_ref[src].astype(F32))
        turned = jnp.dot(mirror, flip_ref[0:wide0, :].astype(BF), preferred_element_type=F32)
        x0_ref[north : north + pitch, :] = jnp.zeros((pitch, ch), F32)
        x0_ref[north + lead : north + lead + wide0, :] = turned

    def relay(src_ref):
        def one(i, carry):
            at = line(i - HALO) + near
            for a in range(4):
                parts = [
                    src_ref[pl.ds(at + 4 * a + j, octets, stride=OUTS), :].astype(ROLLED) for j in range(groups)
                ]
                for gr, part in enumerate(regroup(parts, width)):
                    relaid_ref[gr, a, pl.ds(pl.multiple_of(i * octets, 16), octets), :] = part.astype(BF)
            return carry

        lax.fori_loop(0, rows + 2 * HALO, one, 0)

    def conv(b):
        def one(gr, carry):
            parts = []
            for r in range(TAPS):
                for a in range(4):
                    parts.append(relaid_ref[gr, a, r * octets : (r + rows) * octets, :])
            acc_ref[gr] = jnp.dot(jnp.concatenate(parts, axis=1), w_ref[b, gr], preferred_element_type=F32)
            return carry

        lax.fori_loop(0, groups, one, 0)

    def gelu_twice(h):
        z = h * h
        p = jnp.full_like(z, ERF_POLY[-1])
        for coef in ERF_POLY[-2::-1]:
            p = p * z + jnp.asarray(coef, z.dtype)
        return h + h * jnp.tanh(h * p)

    def norm(b, val):
        val = val + cbias_ref[b : b + 1, :]
        cen = val - jnp.mean(val, axis=-1, keepdims=True)
        var = jnp.mean(cen * cen, axis=-1, keepdims=True)
        return (cen * lax.rsqrt(var + 1e-6) * gain_ref[b : b + 1, :] + nbias_ref[b : b + 1, :]).astype(BF)

    def mlp(b, parts):
        n = parts[0].shape[0]
        normed = jnp.concatenate([norm(b, part) for part in parts], axis=0)
        tile = 48 if n % 48 == 0 else 64
        branch = None
        half_hid = inw_ref.shape[2] // 2
        for c in range(0, 2 * half_hid, half_hid):
            hid = jnp.dot(normed, inw_ref[b, :, c : c + half_hid], preferred_element_type=F32)
            bias = inb_ref[b : b + 1, c : c + half_hid]
            act = [gelu_twice((hid[i : i + tile] + bias).astype(BF)) for i in range(0, hid.shape[0], tile)]
            part = jnp.dot(jnp.concatenate(act, axis=0), outw_ref[b, c : c + half_hid, :], preferred_element_type=F32)
            branch = part if branch is None else branch + part
        scale = scale_ref[b : b + 1, :]
        branch = branch * (0.5 * scale) + outb_ref[b : b + 1, :] * scale
        return [branch[i * n : (i + 1) * n] for i in range(len(parts))]

    def rounded(val):
        return val.astype(BF).astype(F32)

    def inner(b, src_ref):
        step = next(d for d in (8, 6, 4, 3, 2, 1) if rows % d == 0)
        n = step * octets

        def one(t, carry):
            for half in range(2):
                parts = [
                    acc_ref[gr, pl.ds(pl.multiple_of(t * n, 16), n), half * ch : (half + 1) * ch]
                    for gr in range(groups)
                ]
                for j, branch in enumerate(mlp(b, regroup(parts, width))):
                    for i in range(step):
                        at = line(t * step + i) + base + half * groups + j
                        spot = pl.ds(at, octets, stride=OUTS)
                        x1_ref[spot, :] = rounded(src_ref[spot, :] + branch[i * octets : (i + 1) * octets])
            return carry

        lax.fori_loop(0, rows // step, one, 0)

    relay(x0_ref)
    copies[0].wait()
    conv(0)
    inner(0, x0_ref)
    for side in range(2):
        first = lead if side == 0 else base + cols - HALO
        sums = [jnp.zeros((rows, ch), F32) for _ in range(HALO)]
        for r in range(TAPS):
            for c in range(TAPS + HALO - 1):
                cells = x0_ref[pl.ds((REACH - HALO + r) * pitch + first + c, rows, stride=pitch), :]
                for i in range(HALO):
                    if 0 <= c - i < TAPS:
                        tap = TAPS * r + c - i
                        sums[i] = sums[i] + cells * k_ref[0, tap : tap + 1, :]
        start = near if side == 0 else base + cols
        for i, branch in enumerate(mlp(0, sums)):
            spot = pl.ds(REACH * pitch + start + i, rows, stride=pitch)
            x1_ref[spot, :] = rounded(x0_ref[spot, :] + branch)
    piece = wide0 // 3
    for side in range(2):
        first = (0 if side == 0 else rows + HALO) * pitch
        for c in range(0, wide0, piece):
            sums = [jnp.zeros((piece, ch), F32) for _ in range(HALO)]
            for s in range(TAPS):
                at = first + lead + s + c
                lines = [x0_ref[at + i * pitch : at + i * pitch + piece, :] for i in range(TAPS + HALO - 1)]
                for r in range(TAPS):
                    tap = TAPS * r + s
                    if side == 1:
                        tap = jnp.where(top, TAPS * TAPS - 1 - tap, tap)
                    weight = k_ref[0, pl.ds(tap, 1), :]
                    for i in range(HALO):
                        sums[i] = sums[i] + lines[i + r] * weight
            for i in range(HALO):
                strip_ref[side * HALO + i, c : c + piece, :] = sums[i]
    for side in range(2):
        branches = mlp(0, [strip_ref[side * HALO + i] for i in range(HALO)])
        for i, branch in enumerate(branches):
            row = i - HALO if side == 0 else rows + i
            at = (row + REACH) * pitch + near
            new = rounded(x0_ref[at : at + wide0, :] + branch)
            if side == 0:
                new = jnp.where(bottom, 0.0, new)
            x1_ref[at : at + wide0, :] = new

    relay(x1_ref)
    copies[1].wait()
    conv(1)
    inner(1, x1_ref)

    def finish(i, carry):
        out_ref[i] = x1_ref[pl.ds(line(i) + base, cols), :].astype(BF) * mask_ref[i]
        return carry

    lax.fori_loop(0, rows, finish, 0)


def shards(
    fields,
    wet_mask,
    conv_kernel,
    conv_bias,
    norm_gain,
    norm_bias,
    in_weight,
    in_bias,
    out_weight,
    out_bias,
    layer_scale,
):
    rows, cols, ch = fields.shape
    left, right, got_a, got_b = exchange(fields, wet_mask)
    mask = jnp.broadcast_to(wet_mask.astype(BF)[:, :, None], fields.shape)
    state = fields * mask
    taps = tap_matrices(conv_kernel)
    groups, depth, lanes = taps.shape[1:]
    hid = in_weight.shape[2]
    octets = cols // OUTS
    cells = rows * cols
    whole = pltpu.VMEM(((rows + 2 * REACH) * (cols + 24), ch), F32)
    vmem = pl.BlockSpec(memory_space=pltpu.VMEM)
    return pl.pallas_call(
        both_blocks,
        in_specs=[vmem] * 7 + [pl.BlockSpec(memory_space=pl.ANY)] + [vmem] * 8,
        out_specs=vmem,
        out_shape=jax.ShapeDtypeStruct(fields.shape, BF),
        scratch_shapes=[
            whole,
            whole,
            pltpu.VMEM((groups, 4, (rows + 2 * HALO) * octets, ch), BF),
            pltpu.VMEM((2, groups, depth, lanes), BF),
            pltpu.VMEM((groups, rows * octets, lanes), F32),
            pltpu.VMEM((2 * HALO, cols + 16, ch), F32),
            pltpu.VMEM((cols + 24, ch), F32),
            pltpu.SemaphoreType.DMA((2,)),
        ],
        compiler_params=pltpu.CompilerParams(vmem_limit_bytes=VMEM_LIMIT),
        cost_estimate=pl.CostEstimate(
            flops=4 * cells * (4 * ch * hid + 8 * ch * 2 * ch), bytes_accessed=6 * cells * ch, transcendentals=2 * cells * hid
        ),
        name="both_blocks",
    )(
        state,
        mask,
        left,
        right,
        got_a,
        got_b,
        conv_kernel,
        taps,
        conv_bias,
        norm_gain,
        norm_bias,
        in_weight,
        in_bias,
        out_weight,
        out_bias,
        layer_scale,
    )


def solution(mesh):
    return jax.shard_map(
        shards,
        mesh=mesh,
        in_specs=(P("lat", "lon", None), P("lat", "lon")) + (P(),) * 9,
        out_specs=P("lat", "lon", None),
        check_vma=False,
    )
```

time: 91.3 us -> 94.1 us (1.031)
  local copies, waits for them, and re-layouts: 3.4 us -> 7.13 us
  Pallas kernels: 67.2 us -> 69.7 us
  waiting for transfers between devices: 5.61 us -> 3.92 us
  starting transfers between devices: 9.39 us -> 8.24 us
  other arithmetic: 5.32 us -> 4.28 us
    unnamed x11 -> x21, local copies, waits for them, and re-layouts: 1.45 us -> 6.08 us
    ppermute x1, waiting for transfers between devices: 2.51 us -> 0.01 us  [exchange(): left = lax.ppermute(edge(0, rows, cols - REACH, cols), 'lon', up)]
    pallas_call x1 -> x2, Pallas kernels: 67.2 us -> 69.7 us  [the longest x1 67.6 us: shards(): pl.pallas_call(both_blocks, in_specs=[vmem] * 7 + [pl.BlockSpec(memory_sp...]
    ppermute x1, starting transfers between devices: 5.11 us -> 3.96 us  [exchange(): lax.ppermute(jnp.where(even, first, last), ('lat', 'lon'), partners(nlat,...]
  transfers between devices with their start and end apart: 4 -> 4, of which waited for: 2 -> 1; matrix products, arithmetic and copies ran while one was open for 5% -> 3% of each run, Pallas kernels for 0% -> 2%
where the time goes in v3:
time: 94.1 us; the launch traced here: 93.5 us
  Pallas kernels  69.7 us (74%)
  starting transfers between devices  8.24 us (9%)
  local copies, waits for them, and re-layouts  7.13 us (8%)
  other arithmetic  4.28 us (5%)
  waiting for transfers between devices  3.92 us (4%)
    pallas_call x1, Pallas kernels, shards(): pl.pallas_call(both_blocks, in_specs=[vmem] * 7 + [pl.BlockSpec(memory_sp...  67.6 us
    unnamed x21, local copies, waits for them, and re-layouts  6.08 us
    ppermute x1, starting transfers between devices, exchange(): right = lax.ppermute(edge(0, rows, 0, REACH), 'lon', down)  4.2 us
    ppermute x1, starting transfers between devices, exchange(): lax.ppermute(jnp.where(even, first, last), ('lat', 'lon'), partners(nlat,...  3.96 us
    ppermute x1, waiting for transfers between devices, exchange(): lax.ppermute(jnp.where(even, first, last), ('lat', 'lon'), partners(nlat,...  3.91 us
    mul x2, other arithmetic, edge(): return fields[r0:r1, c0:c1] * wet_mask[r0:r1, c0:c1].astype(BF)[:, :, None]  2.4 us
    pallas_call x1, Pallas kernels, tap_matrices(): pl.pallas_call(tap_kernel, grid=(blocks, groups), in_specs=[pl.BlockSpec(...  2.07 us
  transfers between devices with their start and end apart: 4, of which 1 were waited for; matrix products, arithmetic and copies ran while one was open for 3% of the time, Pallas kernels for 2%

profile of v3, /device:TPU:1, one launch (start us, length us, event | category | flops | bytes accessed | tf_op | source)
XLA Modules:
  0.0 93.5 jit_solution(6488932129516605623)
XLA Ops:
  0.0 0.7 convert_element_type.2
  0.7 0.1 fusion.3
  0.8 1.1 %slice_multiply_fusion.2 = (bf16[48,6,128]{2,1,0:T(8,128)(2,1)S(1)}, bf16[48,6,128]{2,1,0:T(8,128)(2,1)S(1)}) fusion(bf16[48,128,128]{2,1,0:T(8,128)(2,1)} %param.11, bf16[48,6]{1,0:T(8,128)(2,1)S(1)} %get-tuple-element.17, bf16[48,6]{1,0:T(8,128)(2,1)S(1)} %get-tuple-element.18), kind=kLoop, calls=%fused_computation.7 | loop fusion | flops 73728 | bytes 296064 | tf_op jit(solution)/shard_map/mul | solution.py:40
  1.9 4.2 %collective-permute-start.1 = (bf16[48,6,128]{2,1,0:T(8,128)(2,1)S(1)}, bf16[48,6,128]{2,1,0:T(8,128)(2,1)S(1)}, u32[]{:S(2)}, u32[]{:S(2)}) collective-permute-start(bf16[48,6,128]{2,1,0:T(8,128)(2,1)S(1)} %get-tuple-element.7), channel_id=1, source_target_pairs={{1,0},{2,1},{3,2},{0,3},{5,4},{6,5},{7,6},{4,7},{9,8},{10,9},{11,1... | collective-permute-start | bytes 221192 | tf_op jit(solution)/shard_map/ppermute | solution.py:45
  6.1 0.0 collective-permute-start
  6.1 1.3 %slice_multiply_fusion.1 = (bf16[6,128,128]{2,1,0:T(8,128)(2,1)S(1)}, bf16[6,128,128]{2,1,0:T(8,128)(2,1)S(1)}) fusion(bf16[48,128,128]{2,1,0:T(8,128)(2,1)} %param.11, bf16[6,128]{1,0:T(8,128)(2,1)S(1)} %get-tuple-element.15, bf16[6,128]{1,0:T(8,128)(2,1)S(1)} %get-tuple-element.16), kind=kLoop, calls=%fused_computation.6 | loop fusion | flops 196608 | bytes 789504 | tf_op jit(solution)/shard_map/mul | solution.py:40
  7.5 0.8 copy.13.k_ref
  8.3 2.1 %tap_matrices.1.w_hbm = bf16[2,4,3584,256]{3,2,1,0:T(8,128)(2,1)S(1)} custom-call(f32[2,49,128]{2,1,0:T(8,128)S(1)} %copy.13.k_ref), custom_call_target="tpu_custom_call" | custom-call | bytes 14680064 | tf_op jit(solution)/shard_map/tap_matrices/pallas_call | solution.py:105
  10.3 0.0 copy-start
  10.3 5.2 %copy-done = bf16[2,4,3584,256]{3,2,1,0:T(8,128)(2,1)} copy-done((bf16[2,4,3584,256]{3,2,1,0:T(8,128)(2,1)}, bf16[2,4,3584,256]{3,2,1,0:T(8,128)(2,1)S(1)}, u32[]{:S(2)}) %copy-start) | copy-done | bytes 14680088
  15.6 0.0 collective-permute-done.1.right_ref
  15.6 0.0 collective-permute-done.left_ref
  15.6 0.2 broadcast_select_fusion
  15.8 4.0 %collective-permute-start.3 = (bf16[6,140,128]{2,1,0:T(8,128)(2,1)S(1)}, bf16[6,140,128]{2,1,0:T(8,128)(2,1)S(1)}, u32[]{:S(2)}, u32[]{:S(2)}) collective-permute-start(bf16[6,140,128]{2,1,0:T(8,128)(2,1)S(1)} %get-tuple-element.9), channel_id=1, source_target_pairs={{4,8},{5,9},{6,10},{7,11},{8,4},{9,5},{10,6},{11,7},{12,16},{13,17... | collective-permute-start | bytes 645128 | tf_op jit(solution)/shard_map/ppermute | solution.py:50
  19.7 0.1 collective-permute-start.2
  19.8 0.0 copy-done.9
  19.8 1.0 %broadcast_multiply_fusion.x_ref = bf16[48,128,128]{2,1,0:T(8,128)(2,1)S(1)} fusion(bf16[48,128,128]{2,1,0:T(8,128)(2,1)S(1)} %copy-done.9, bf16[48,128]{1,0:T(8,128)(2,1)S(1)} %convert_element_type.2), kind=kLoop, calls=%fused_computation | loop fusion | flops 786432 | bytes 3158016 | tf_op jit(solution)/shard_map/mul | solution.py:341
  20.8 0.0 copy-start.1
  20.8 0.0 copy-start.2
  20.8 0.0 copy-start.3
  20.8 0.0 copy-start.4
  20.8 0.0 copy-start.5
  20.9 0.0 copy-start.6
  20.9 0.0 copy-start.7
  20.9 0.0 copy-start.8
  20.9 3.9 %collective-permute-done.3.b_ref = bf16[6,140,128]{2,1,0:T(8,128)(2,1)S(1)} collective-permute-done((bf16[6,140,128]{2,1,0:T(8,128)(2,1)S(1)}, bf16[6,140,128]{2,1,0:T(8,128)(2,1)S(1)}, u32[]{:S(2)}, u32[]{:S(2)}) %collective-permute-start.3) | collective-permute-done | bytes 215072 | tf_op jit(solution)/shard_map/ppermute | solution.py:50
  24.8 0.0 collective-permute-done.2.a_ref
  24.8 1.0 %broadcast_in_dim.2.mask_ref = bf16[48,128,128]{2,1,0:T(8,128)(2,1)S(1)} broadcast(bf16[48,128]{1,0:T(8,128)(2,1)S(1)} %convert_element_type.2), dimensions={0,1} | broadcast | bytes 1585152 | tf_op jit(solution)/shard_map/broadcast_in_dim | solution.py:340
  25.8 0.0 copy-done.1
  25.8 0.0 copy-done.2
  25.8 0.0 copy-done.3
  25.9 67.6 %both_blocks.1 = bf16[48,128,128]{2,1,0:T(8,128)(2,1)} custom-call(bf16[48,128,128]{2,1,0:T(8,128)(2,1)S(1)} %broadcast_multiply_fusion.x_ref, bf16[48,128,128]{2,1,0:T(8,128)(2,1)S(1)} %broadcast_in_dim.2.mask_ref, bf16[48,6,128]{2,1,0:T(8,128)(2,1)S(1)} %collective-permute-done.left_ref, bf16[48,6,128]{2,1,0:T(8,128)(2,1)S(1)} %collective-permute-done.1.right_ref, ...), custom_call_target="tpu_custom_call" | custom-call | flops 12884901888 | bytes 4718592 | tf_op jit(solution)/shard_map/both_blocks/pallas_call | solution.py:349
  (9 shorter events, 0.0 us)
Async XLA Ops:
  1.9 13.6 %collective-permute-start.1 = (bf16[48,6,128]{2,1,0:T(8,128)(2,1)S(1)}, bf16[48,6,128]{2,1,0:T(8,128)(2,1)S(1)}, u32[]{:S(2)}, u32[]{:S(2)}) collective-permute-start(bf16[48,6,128]{2,1,0:T(8,128)(2,1)S(1)} %get-tuple-element.7), channel_id=1, source_target_pairs={{1,0},{2,1},{3,2},{0,3},{5,4},{6,5},{7,6},{4,7},{9,8},{10,9},{11,1... | collective-permute-start | bytes 221192 | tf_op jit(solution)/shard_map/ppermute | solution.py:45
  6.1 9.4 %collective-permute-start = (bf16[48,6,128]{2,1,0:T(8,128)(2,1)S(1)}, bf16[48,6,128]{2,1,0:T(8,128)(2,1)S(1)}, u32[]{:S(2)}, u32[]{:S(2)}) collective-permute-start(bf16[48,6,128]{2,1,0:T(8,128)(2,1)S(1)} %get-tuple-element.8), channel_id=1, source_target_pairs={{0,1},{1,2},{2,3},{3,0},{4,5},{5,6},{6,7},{7,4},{8,9},{9,10},{10,1... | collective-permute-start | bytes 221192 | tf_op jit(solution)/shard_map/ppermute | solution.py:44
  8.3 11.5 %copy-start.9 = (bf16[48,128,128]{2,1,0:T(8,128)(2,1)S(1)}, bf16[48,128,128]{2,1,0:T(8,128)(2,1)}, u32[]{:S(2)}) copy-start(bf16[48,128,128]{2,1,0:T(8,128)(2,1)} %param.11) | copy-start | bytes 4718596
  10.3 5.2 %copy-start = (bf16[2,4,3584,256]{3,2,1,0:T(8,128)(2,1)}, bf16[2,4,3584,256]{3,2,1,0:T(8,128)(2,1)S(1)}, u32[]{:S(2)}) copy-start(bf16[2,4,3584,256]{3,2,1,0:T(8,128)(2,1)S(1)} %tap_matrices.1.w_hbm) | copy-start | bytes 44040196
  15.8 9.1 %collective-permute-start.3 = (bf16[6,140,128]{2,1,0:T(8,128)(2,1)S(1)}, bf16[6,140,128]{2,1,0:T(8,128)(2,1)S(1)}, u32[]{:S(2)}, u32[]{:S(2)}) collective-permute-start(bf16[6,140,128]{2,1,0:T(8,128)(2,1)S(1)} %get-tuple-element.9), channel_id=1, source_target_pairs={{4,8},{5,9},{6,10},{7,11},{8,4},{9,5},{10,6},{11,7},{12,16},{13,17... | collective-permute-start | bytes 645128 | tf_op jit(solution)/shard_map/ppermute | solution.py:50
  19.7 5.1 %collective-permute-start.2 = (bf16[6,140,128]{2,1,0:T(8,128)(2,1)S(1)}, bf16[6,140,128]{2,1,0:T(8,128)(2,1)S(1)}, u32[]{:S(2)}, u32[]{:S(2)}) collective-permute-start(bf16[6,140,128]{2,1,0:T(8,128)(2,1)S(1)} %get-tuple-element.10), channel_id=1, source_target_pairs={{0,4},{1,5},{2,6},{3,7},{4,0},{5,1},{6,2},{7,3},{8,12},{9,13},{10,... | collective-permute-start | bytes 645128 | tf_op jit(solution)/shard_map/ppermute | solution.py:49
  20.8 5.0 %copy-start.1 = (bf16[2,128,512]{2,1,0:T(8,128)(2,1)S(1)}, bf16[2,128,512]{2,1,0:T(8,128)(2,1)}, u32[]{:S(2)}) copy-start(bf16[2,128,512]{2,1,0:T(8,128)(2,1)} %inw_ref.1) | copy-start | bytes 786436
  20.8 5.0 %copy-start.2 = (bf16[2,512,128]{2,1,0:T(8,128)(2,1)S(1)}, bf16[2,512,128]{2,1,0:T(8,128)(2,1)}, u32[]{:S(2)}) copy-start(bf16[2,512,128]{2,1,0:T(8,128)(2,1)} %outw_ref.1) | copy-start | bytes 786436
  20.8 5.0 %copy-start.3 = (f32[2,512]{1,0:T(2,128)S(1)}, f32[2,512]{1,0:T(2,128)}, u32[]{:S(2)}) copy-start(f32[2,512]{1,0:T(2,128)} %inb_ref.1) | copy-start | bytes 12292
  20.8 5.0 %copy-start.4 = (f32[2,128]{1,0:T(2,128)S(1)}, f32[2,128]{1,0:T(2,128)}, u32[]{:S(2)}) copy-start(f32[2,128]{1,0:T(2,128)} %cbias_ref.1) | copy-start | bytes 3076
  20.8 5.0 %copy-start.5 = (f32[2,128]{1,0:T(2,128)S(1)}, f32[2,128]{1,0:T(2,128)}, u32[]{:S(2)}) copy-start(f32[2,128]{1,0:T(2,128)} %gain_ref.1) | copy-start | bytes 3076
  20.9 5.0 %copy-start.6 = (f32[2,128]{1,0:T(2,128)S(1)}, f32[2,128]{1,0:T(2,128)}, u32[]{:S(2)}) copy-start(f32[2,128]{1,0:T(2,128)} %nbias_ref.1) | copy-start | bytes 3076
  20.9 5.0 %copy-start.7 = (f32[2,128]{1,0:T(2,128)S(1)}, f32[2,128]{1,0:T(2,128)}, u32[]{:S(2)}) copy-start(f32[2,128]{1,0:T(2,128)} %outb_ref.1) | copy-start | bytes 3076
  20.9 5.0 %copy-start.8 = (f32[2,128]{1,0:T(2,128)S(1)}, f32[2,128]{1,0:T(2,128)}, u32[]{:S(2)}) copy-start(f32[2,128]{1,0:T(2,128)} %scale_ref.1) | copy-start | bytes 3076

commit v4 on v3

--- a/solution.py
+++ b/solution.py
@@ -1,3 +1,5 @@
+import functools
+
 import jax
 import jax.numpy as jnp
 from jax import lax
@@ -11,8 +13,8 @@
 HALO = 3
 REACH = 2 * HALO
 OUTS = 8
-ROLLED = jnp.bfloat16
-VMEM_LIMIT = 48 * 1024 * 1024
+BASE = 8
+VMEM_LIMIT = 30 * 1024 * 1024
 ERF_POLY = (0.7975078797359708, 0.03700565107996738, -0.0003515176683895368)
 
 
@@ -117,52 +119,58 @@
     )(conv_kernel)
 
 
-def both_blocks(
-    x_ref,
-    mask_ref,
-    left_ref,
-    right_ref,
-    a_ref,
-    b_ref,
-    k_ref,
-    w_hbm,
-    cbias_ref,
-    gain_ref,
-    nbias_ref,
-    inw_ref,
-    inb_ref,
-    outw_ref,
-    outb_ref,
-    scale_ref,
-    out_ref,
-    x0_ref,
-    x1_ref,
-    relaid_ref,
-    w_ref,
-    acc_ref,
-    strip_ref,
-    flip_ref,
-    w_sem,
-):
-    rows, cols, ch = x_ref.shape
-    width = 2 * ch // OUTS
-    groups = ch // width
-    octets = cols // OUTS
-    base = 8
-    ext = cols + 2 * REACH
-    lead = base - REACH
-    near = base - HALO
-    pitch = cols + 24
-    wide0 = cols + 16
+class Sizes:
+    def __init__(self, rows, cols, ch):
+        self.rows, self.cols, self.ch = rows, cols, ch
+        self.width = 2 * ch // OUTS
+        self.groups = ch // self.width
+        self.octets = cols // OUTS
+        self.pitch = cols + 24
+        self.lines = (rows + 2 * REACH) * self.pitch
+        self.wide0 = cols + 16
+
+    def line(self, row):
+        return pl.multiple_of((row + REACH) * self.pitch, 8)
+
+
+def place():
     lat = lax.axis_index("lat")
-    even, top, bottom = lat % 2 == 0, lat == lax.axis_size("lat") - 1, lat == 0
-
-    copies = [pltpu.make_async_copy(w_hbm.at[b], w_ref.at[b], w_sem.at[b]) for b in range(2)]
-    for copy in copies:
-        copy.start()
-
-    def line(row):
-        return pl.multiple_of((row + REACH) * pitch, 8)
+    return lat % 2 == 0, lat == lax.axis_size("lat") - 1, lat == 0
+
+
+def relay(size, src_ref, relaid_ref):
+    def one(i, carry):
+        at = size.line(i - HALO) + BASE - HALO
+        for a in range(4):
+            parts = [
+                src_ref[pl.ds(at + 4 * a + j, size.octets, stride=OUTS), :].astype(BF) for j in range(size.groups)
+            ]
+            for gr, part in enumerate(regroup(parts, size.width)):
+                relaid_ref[gr, a, pl.ds(pl.multiple_of(i * size.octets, 16), size.octets), :] = part
+        return carry
+
+    lax.fori_loop(0, size.rows + 2 * HALO, one, 0)
+
+
+def conv(size, relaid_ref, w_ref, acc_ref):
+    octets, rows = size.octets, size.rows
+
+    def one(gr, carry):
+        parts = []
+        for r in range(TAPS):
+            for a in range(4):
+                parts.append(relaid_ref[gr, a, r * octets : (r + rows) * octets, :])
+        acc_ref[gr] = jnp.dot(jnp.concatenate(parts, axis=1), w_ref[0, gr], preferred_element_type=F32)
+        return carry
+
+    lax.fori_loop(0, size.groups, one, 0)
+
+
+def conv0_kernel(size, x_ref, left_ref, right_ref, a_ref, b_ref, w_ref, x0_ref, acc_ref, relaid_ref, flip_ref):
+    rows, cols, ch, pitch, wide0 = size.rows, size.cols, size.ch, size.pitch, size.wide0
+    base, ext, lead = BASE, cols + 2 * REACH, BASE - REACH
+    line = size.line
+    even, top, _ = place()
 
     def fill(i, carry):
         at = line(i)
@@ -171,8 +179,6 @@
         x0_ref[pl.ds(at + base, cols), :] = x_ref[i].astype(F32)
         x0_ref[pl.ds(at + base + cols, 16), :] = jnp.zeros((16, ch), F32)
         x0_ref[pl.ds(at + base + cols, REACH), :] = right_ref[i].astype(F32)
-        x1_ref[pl.ds(at, base), :] = jnp.zeros((base, ch), F32)
-        x1_ref[pl.ds(at + base + cols, 16), :] = jnp.zeros((16, ch), F32)
         return carry
 
     lax.fori_loop(0, rows, fill, 0)
@@ -189,86 +195,90 @@
         turned = jnp.dot(mirror, flip_ref[0:wide0, :].astype(BF), preferred_element_type=F32)
         x0_ref[north : north + pitch, :] = jnp.zeros((pitch, ch), F32)
         x0_ref[north + lead : north + lead + wide0, :] = turned
-
-    def relay(src_ref):
-        def one(i, carry):
-            at = line(i - HALO) + near
-            for a in range(4):
-                parts = [
-                    src_ref[pl.ds(at + 4 * a + j, octets, stride=OUTS), :].astype(ROLLED) for j in range(groups)
-                ]
-                for gr, part in enumerate(regroup(parts, width)):
-                    relaid_ref[gr, a, pl.ds(pl.multiple_of(i * octets, 16), octets), :] = part.astype(BF)
-            return carry
-
-        lax.fori_loop(0, rows + 2 * HALO, one, 0)
-
-    def conv(b):
-        def one(gr, carry):
-            parts = []
-            for r in range(TAPS):
-                for a in range(4):
-                    parts.append(relaid_ref[gr, a, r * octets : (r + rows) * octets, :])
-            acc_ref[gr] = jnp.dot(jnp.concatenate(parts, axis=1), w_ref[b, gr], preferred_element_type=F32)
-            return carry
-
-        lax.fori_loop(0, groups, one, 0)
-
-    def gelu_twice(h):
-        z = h * h
-        p = jnp.full_like(z, ERF_POLY[-1])
-        for coef in ERF_POLY[-2::-1]:
-            p = p * z + jnp.asarray(coef, z.dtype)
-        return h + h * jnp.tanh(h * p)
-
-    def norm(b, val):
-        val = val + cbias_ref[b : b + 1, :]
-        cen = val - jnp.mean(val, axis=-1, keepdims=True)
-        var = jnp.mean(cen * cen, axis=-1, keepdims=True)
-        return (cen * lax.rsqrt(var + 1e-6) * gain_ref[b : b + 1, :] + nbias_ref[b : b + 1, :]).astype(BF)
-
-    def mlp(b, parts):
-        n = parts[0].shape[0]
-        normed = jnp.concatenate([norm(b, part) for part in parts], axis=0)
-        tile = 48 if n % 48 == 0 else 64
-        branch = None
-        half_hid = inw_ref.shape[2] // 2
-        for c in range(0, 2 * half_hid, half_hid):
-            hid = jnp.dot(normed, inw_ref[b, :, c : c + half_hid], preferred_element_type=F32)
-            bias = inb_ref[b : b + 1, c : c + half_hid]
-            act = [gelu_twice((hid[i : i + tile] + bias).astype(BF)) for i in range(0, hid.shape[0], tile)]
-            part = jnp.dot(jnp.concatenate(act, axis=0), outw_ref[b, c : c + half_hid, :], preferred_element_type=F32)
-            branch = part if branch is None else branch + part
-        scale = scale_ref[b : b + 1, :]
-        branch = branch * (0.5 * scale) + outb_ref[b : b + 1, :] * scale
-        return [branch[i * n : (i + 1) * n] for i in range(len(parts))]
-
-    def rounded(val):
-        return val.astype(BF).astype(F32)
-
-    def inner(b, src_ref):
-        step = next(d for d in (8, 6, 4, 3, 2, 1) if rows % d == 0)
-        n = step * octets
-
-        def one(t, carry):
-            for half in range(2):
-                parts = [
-                    acc_ref[gr, pl.ds(pl.multiple_of(t * n, 16), n), half * ch : (half + 1) * ch]
-                    for gr in range(groups)
-                ]
-                for j, branch in enumerate(mlp(b, regroup(parts, width))):
-                    for i in range(step):
-                        at = line(t * step + i) + base + half * groups + j
-                        spot = pl.ds(at, octets, stride=OUTS)
-                        x1_ref[spot, :] = rounded(src_ref[spot, :] + branch[i * octets : (i + 1) * octets])
-            return carry
-
-        lax.fori_loop(0, rows // step, one, 0)
-
-    relay(x0_ref)
-    copies[0].wait()
-    conv(0)
-    inner(0, x0_ref)
+    relay(size, x0_ref, relaid_ref)
+    conv(size, relaid_ref, w_ref, acc_ref)
+
+
+def conv1_kernel(size, x1_ref, w_ref, acc_ref, relaid_ref):
+    relay(size, x1_ref, relaid_ref)
+    conv(size, relaid_ref, w_ref, acc_ref)
+
+
+def gelu_twice(h):
+    z = h * h
+    p = jnp.full_like(z, ERF_POLY[-1])
+    for coef in ERF_POLY[-2::-1]:
+        p = p * z + jnp.asarray(coef, z.dtype)
+    return h + h * jnp.tanh(h * p)
+
+
+def norm(b, params, val):
+    cbias_ref, gain_ref, nbias_ref = params[:3]
+    val = val + cbias_ref[b : b + 1, :]
+    cen = val - jnp.mean(val, axis=-1, keepdims=True)
+    var = jnp.mean(cen * cen, axis=-1, keepdims=True)
+    return (cen * lax.rsqrt(var + 1e-6) * gain_ref[b : b + 1, :] + nbias_ref[b : b + 1, :]).astype(BF)
+
+
+def mlp(b, params, parts):
+    inw_ref, inb_ref, outw_ref, outb_ref, scale_ref = params[3:]
+    n = parts[0].shape[0]
+    normed = jnp.concatenate([norm(b, params, part) for part in parts], axis=0)
+    tile = 48 if n % 48 == 0 else 64
+    branch = None
+    half_hid = inw_ref.shape[2] // 2
+    for c in range(0, 2 * half_hid, half_hid):
+        hid = jnp.dot(normed, inw_ref[b, :, c : c + half_hid], preferred_element_type=F32)
+        bias = inb_ref[b : b + 1, c : c + half_hid]
+        act = [gelu_twice((hid[i : i + tile] + bias).astype(BF)) for i in range(0, hid.shape[0], tile)]
+        part = jnp.dot(jnp.concatenate(act, axis=0), outw_ref[b, c : c + half_hid, :], preferred_element_type=F32)
+        branch = part if branch is None else branch + part
+    scale = scale_ref[b : b + 1, :]
+    branch = branch * (0.5 * scale) + outb_ref[b : b + 1, :] * scale
+    return [branch[i * n : (i + 1) * n] for i in range(len(parts))]
+
+def rounded(val):
+    return val.astype(BF).astype(F32)
+
+
+def rounded(val):
+    return val.astype(BF).astype(F32)
+
+
+def inner(size, b, params, acc_ref, src_ref, dst_ref):
+    rows, octets, groups, ch = size.rows, size.octets, size.groups, size.ch
+    step = next(d for d in (8, 6, 4, 3, 2, 1) if rows % d == 0)
+    n = step * octets
+
+    def one(t, carry):
+        for half in range(2):
+            parts = [
+                acc_ref[gr, pl.ds(pl.multiple_of(t * n, 16), n), half * ch : (half + 1) * ch] for gr in range(groups)
+            ]
+            for j, branch in enumerate(mlp(b, params, regroup(parts, size.width))):
+                for i in range(step):
+                    at = size.line(t * step + i) + BASE + half * groups + j
+                    spot = pl.ds(at, octets, stride=OUTS)
+                    dst_ref[spot, :] = rounded(src_ref[spot, :] + branch[i * octets : (i + 1) * octets])
+        return carry
+
+    lax.fori_loop(0, rows // step, one, 0)
+
+
+def mlp0_kernel(size, acc_ref, x0_ref, k_ref, *refs):
+    params, (x1_ref, strip_ref) = refs[:8], refs[8:]
+    rows, cols, ch, pitch, wide0 = size.rows, size.cols, size.ch, size.pitch, size.wide0
+    base, lead, near = BASE, BASE - REACH, BASE - HALO
+    _, top, bottom = place()
+
+    def clear(i, carry):
+        at = size.line(i)
+        x1_ref[pl.ds(at, base), :] = jnp.zeros((base, ch), F32)
+        x1_ref[pl.ds(at + base + cols, 16), :] = jnp.zeros((16, ch), F32)
+        return carry
+
+    lax.fori_loop(0, rows, clear, 0)
+    inner(size, 0, params, acc_ref, x0_ref, x1_ref)
     for side in range(2):
         first = lead if side == 0 else base + cols - HALO
         sums = [jnp.zeros((rows, ch), F32) for _ in range(HALO)]
@@ -280,7 +290,7 @@
                         tap = TAPS * r + c - i
                         sums[i] = sums[i] + cells * k_ref[0, tap : tap + 1, :]
         start = near if side == 0 else base + cols
-        for i, branch in enumerate(mlp(0, sums)):
+        for i, branch in enumerate(mlp(0, params, sums)):
             spot = pl.ds(REACH * pitch + start + i, rows, stride=pitch)
             x1_ref[spot, :] = rounded(x0_ref[spot, :] + branch)
     piece = wide0 // 3
@@ -301,7 +311,7 @@
             for i in range(HALO):
                 strip_ref[side * HALO + i, c : c + piece, :] = sums[i]
     for side in range(2):
-        branches = mlp(0, [strip_ref[side * HALO + i] for i in range(HALO)])
+        branches = mlp(0, params, [strip_ref[side * HALO + i] for i in range(HALO)])
         for i, branch in enumerate(branches):
             row = i - HALO if side == 0 else rows + i
             at = (row + REACH) * pitch + near
@@ -310,16 +320,16 @@
                 new = jnp.where(bottom, 0.0, new)
             x1_ref[at : at + wide0, :] = new
 
-    relay(x1_ref)
-    copies[1].wait()
-    conv(1)
-    inner(1, x1_ref)
+
+def mlp1_kernel(size, acc_ref, x1_ref, mask_ref, *refs):
+    params, (out_ref, x2_ref) = refs[:8], refs[8:]
+    inner(size, 1, params, acc_ref, x1_ref, x2_ref)
 
     def finish(i, carry):
-        out_ref[i] = x1_ref[pl.ds(line(i) + base, cols), :].astype(BF) * mask_ref[i]
-        return carry
-
-    lax.fori_loop(0, rows, finish, 0)
+        out_ref[i] = x2_ref[pl.ds(size.line(i) + BASE, size.cols), :].astype(BF) * mask_ref[i]
+        return carry
+
+    lax.fori_loop(0, size.rows, finish, 0)
 
 
 def shards(
@@ -342,48 +352,48 @@
     taps = tap_matrices(conv_kernel)
     groups, depth, lanes = taps.shape[1:]
     hid = in_weight.shape[2]
-    octets = cols // OUTS
+    size = Sizes(rows, cols, ch)
     cells = rows * cols
-    whole = pltpu.VMEM(((rows + 2 * REACH) * (cols + 24), ch), F32)
     vmem = pl.BlockSpec(memory_space=pltpu.VMEM)
-    return pl.pallas_call(
-        both_blocks,
-        in_specs=[vmem] * 7 + [pl.BlockSpec(memory_space=pl.ANY)] + [vmem] * 8,
-        out_specs=vmem,
-        out_shape=jax.ShapeDtypeStruct(fields.shape, BF),
-        scratch_shapes=[
-            whole,
-            whole,
-            pltpu.VMEM((groups, 4, (rows + 2 * HALO) * octets, ch), BF),
-            pltpu.VMEM((2, groups, depth, lanes), BF),
-            pltpu.VMEM((groups, rows * octets, lanes), F32),
-            pltpu.VMEM((2 * HALO, cols + 16, ch), F32),
-            pltpu.VMEM((cols + 24, ch), F32),
-            pltpu.SemaphoreType.DMA((2,)),
-        ],
-        compiler_params=pltpu.CompilerParams(vmem_limit_bytes=VMEM_LIMIT),
-        cost_estimate=pl.CostEstimate(
-            flops=4 * cells * (4 * ch * hid + 8 * ch * 2 * ch), bytes_accessed=6 * cells * ch, transcendentals=2 * cells * hid
-        ),
-        name="both_blocks",
-    )(
-        state,
-        mask,
-        left,
-        right,
-        got_a,
-        got_b,
-        conv_kernel,
-        taps,
-        conv_bias,
-        norm_gain,
-        norm_bias,
-        in_weight,
-        in_bias,
-        out_weight,
-        out_bias,
-        layer_scale,
+    relaid = pltpu.VMEM((groups, 4, (rows + 2 * HALO) * size.octets, ch), BF)
+    padded = jax.ShapeDtypeStruct((size.lines, ch), F32)
+    sums = jax.ShapeDtypeStruct((groups, rows * size.octets, lanes), F32)
+
+    def call(kernel, ins, out_shape, scratch, flops):
+        def spec(value):
+            if value is not taps:
+                return vmem
+            block = 0 if kernel is conv0_kernel else 1
+            return pl.BlockSpec((1, groups, depth, lanes), lambda i: (block, 0, 0, 0))
+
+        several = isinstance(out_shape, tuple)
+        return pl.pallas_call(
+            functools.partial(kernel, size),
+            grid=(1,),
+            in_specs=[spec(value) for value in ins],
+            out_specs=(vmem,) * len(out_shape) if several else vmem,
+            out_shape=out_shape,
+            scratch_shapes=scratch,
+            compiler_params=pltpu.CompilerParams(vmem_limit_bytes=VMEM_LIMIT),
+            cost_estimate=pl.CostEstimate(flops=flops, bytes_accessed=6 * cells * ch, transcendentals=cells * hid),
+            name=kernel.__name__,
+        )(*ins)
+
+    conv_flops = 2 * cells * ch * depth // OUTS * 2
+    mlp_flops = 4 * cells * ch * hid
+    params = (conv_bias, norm_gain, norm_bias, in_weight, in_bias, out_weight, out_bias, layer_scale)
+    x0, acc = call(
+        conv0_kernel,
+        (state, left, right, got_a, got_b, taps),
+        (padded, sums),
+        [relaid, pltpu.VMEM((cols + 24, ch), F32)],
+        conv_flops,
     )
+    strips = pltpu.VMEM((2 * HALO, cols + 16, ch), F32)
+    x1 = call(mlp0_kernel, (acc, x0, conv_kernel) + params, padded, [strips], mlp_flops)
+    acc = call(conv1_kernel, (x1, taps), sums, [relaid], conv_flops)
+    whole = pltpu.VMEM((size.lines, ch), F32)
+    return call(mlp1_kernel, (acc, x1, mask) + params, jax.ShapeDtypeStruct(fields.shape, BF), [whole], mlp_flops)
 
 
 def solution(mesh):

time: 94.1 us -> 101 us (1.073)
  local copies, waits for them, and re-layouts: 7.13 us -> 12.3 us
  waiting for transfers between devices: 3.92 us -> 5.02 us
    unnamed x21 -> x23, local copies, waits for them, and re-layouts: 6.08 us -> 11.2 us
    ppermute x1, starting transfers between devices: 0.01 us -> 2.18 us  [exchange(): left = lax.ppermute(edge(0, rows, cols - REACH, cols), 'lon', up)]
    ppermute x1, starting transfers between devices: 4.2 us -> 2.09 us  [exchange(): right = lax.ppermute(edge(0, rows, 0, REACH), 'lon', down)]
    ppermute x1, waiting for transfers between devices: 3.91 us -> 5.01 us  [exchange(): lax.ppermute(jnp.where(even, first, last), ('lat', 'lon'), partners(nlat,...]
    pallas_call x1 -> x4, Pallas kernels: 67.6 us -> 68.1 us  [call(): pl.pallas_call(functools.partial(kernel, size), grid=(1,), in_specs=[spec...]
where the time goes in v4:
time: 101 us; the launch traced here: 100 us
  Pallas kernels  70.1 us (69%)
  local copies, waits for them, and re-layouts  12.3 us (12%)
  starting transfers between devices  8.46 us (8%)
  waiting for transfers between devices  5.02 us (5%)
  other arithmetic  4.28 us (4%)
    pallas_call x4, Pallas kernels, call(): pl.pallas_call(functools.partial(kernel, size), grid=(1,), in_specs=[spec...  68.1 us
    unnamed x23, local copies, waits for them, and re-layouts  11.2 us
    ppermute x1, waiting for transfers between devices, exchange(): lax.ppermute(jnp.where(even, first, last), ('lat', 'lon'), partners(nlat,...  5.01 us
    ppermute x1, starting transfers between devices, exchange(): lax.ppermute(jnp.where(even, first, last), ('lat', 'lon'), partners(nlat,...  3.14 us
    mul x2, other arithmetic, edge(): return fields[r0:r1, c0:c1] * wet_mask[r0:r1, c0:c1].astype(BF)[:, :, None]  2.4 us
    ppermute x1, starting transfers between devices, exchange(): left = lax.ppermute(edge(0, rows, cols - REACH, cols), 'lon', up)  2.18 us
    ppermute x1, starting transfers between devices, exchange(): right = lax.ppermute(edge(0, rows, 0, REACH), 'lon', down)  2.09 us
    pallas_call x1, Pallas kernels, tap_matrices(): pl.pallas_call(tap_kernel, grid=(blocks, groups), in_specs=[pl.BlockSpec(...  2.07 us
  transfers between devices with their start and end apart: 4, of which 1 were waited for; matrix products, arithmetic and copies ran while one was open for 3% of the time, Pallas kernels for 2%

profile of v4, /device:TPU:1, one launch (start us, length us, event | category | flops | bytes accessed | tf_op | source)
XLA Modules:
  0.0 100.4 jit_solution(12190580055785102579)
XLA Ops:
  0.0 0.7 convert_element_type.2
  0.7 0.1 fusion.3
  0.8 1.1 %slice_multiply_fusion.2 = (bf16[48,6,128]{2,1,0:T(8,128)(2,1)S(1)}, bf16[48,6,128]{2,1,0:T(8,128)(2,1)S(1)}) fusion(bf16[48,128,128]{2,1,0:T(8,128)(2,1)} %param.11, bf16[48,6]{1,0:T(8,128)(2,1)S(1)} %get-tuple-element.21, bf16[48,6]{1,0:T(8,128)(2,1)S(1)} %get-tuple-element.22), kind=kLoop, calls=%fused_computation.7 | loop fusion | flops 73728 | bytes 296064 | tf_op jit(solution)/shard_map/mul | solution.py:42
  1.9 2.2 %collective-permute-start = (bf16[48,6,128]{2,1,0:T(8,128)(2,1)S(1)}, bf16[48,6,128]{2,1,0:T(8,128)(2,1)S(1)}, u32[]{:S(2)}, u32[]{:S(2)}) collective-permute-start(bf16[48,6,128]{2,1,0:T(8,128)(2,1)S(1)} %get-tuple-element.12), channel_id=1, source_target_pairs={{0,1},{1,2},{2,3},{3,0},{4,5},{5,6},{6,7},{7,4},{8,9},{9,10},{10,1... | collective-permute-start | bytes 221192 | tf_op jit(solution)/shard_map/ppermute | solution.py:46
  4.1 2.1 %collective-permute-start.1 = (bf16[48,6,128]{2,1,0:T(8,128)(2,1)S(1)}, bf16[48,6,128]{2,1,0:T(8,128)(2,1)S(1)}, u32[]{:S(2)}, u32[]{:S(2)}) collective-permute-start(bf16[48,6,128]{2,1,0:T(8,128)(2,1)S(1)} %get-tuple-element.11), channel_id=1, source_target_pairs={{1,0},{2,1},{3,2},{0,3},{5,4},{6,5},{7,6},{4,7},{9,8},{10,9},{11,1... | collective-permute-start | bytes 221192 | tf_op jit(solution)/shard_map/ppermute | solution.py:47
  6.2 1.3 %slice_multiply_fusion.1 = (bf16[6,128,128]{2,1,0:T(8,128)(2,1)S(1)}, bf16[6,128,128]{2,1,0:T(8,128)(2,1)S(1)}) fusion(bf16[48,128,128]{2,1,0:T(8,128)(2,1)} %param.11, bf16[6,128]{1,0:T(8,128)(2,1)S(1)} %get-tuple-element.19, bf16[6,128]{1,0:T(8,128)(2,1)S(1)} %get-tuple-element.20), kind=kLoop, calls=%fused_computation.6 | loop fusion | flops 196608 | bytes 789504 | tf_op jit(solution)/shard_map/mul | solution.py:42
  7.5 0.8 copy.12.k_ref
  8.3 2.1 %tap_matrices.1.w_ref = bf16[2,4,3584,256]{3,2,1,0:T(8,128)(2,1)S(1)} custom-call(f32[2,49,128]{2,1,0:T(8,128)S(1)} %copy.12.k_ref), custom_call_target="tpu_custom_call" | custom-call | bytes 14680064 | tf_op jit(solution)/shard_map/tap_matrices/pallas_call | solution.py:107
  10.4 0.0 collective-permute-done.left_ref
  10.4 0.0 collective-permute-done.1.right_ref
  10.4 0.2 broadcast_select_fusion
  10.6 1.1 %collective-permute-start.2 = (bf16[6,140,128]{2,1,0:T(8,128)(2,1)S(1)}, bf16[6,140,128]{2,1,0:T(8,128)(2,1)S(1)}, u32[]{:S(2)}, u32[]{:S(2)}) collective-permute-start(bf16[6,140,128]{2,1,0:T(8,128)(2,1)S(1)} %get-tuple-element.14), channel_id=1, source_target_pairs={{0,4},{1,5},{2,6},{3,7},{4,0},{5,1},{6,2},{7,3},{8,12},{9,13},{10,... | collective-permute-start | bytes 645128 | tf_op jit(solution)/shard_map/ppermute | solution.py:51
  11.7 3.1 %collective-permute-start.3 = (bf16[6,140,128]{2,1,0:T(8,128)(2,1)S(1)}, bf16[6,140,128]{2,1,0:T(8,128)(2,1)S(1)}, u32[]{:S(2)}, u32[]{:S(2)}) collective-permute-start(bf16[6,140,128]{2,1,0:T(8,128)(2,1)S(1)} %get-tuple-element.13), channel_id=1, source_target_pairs={{4,8},{5,9},{6,10},{7,11},{8,4},{9,5},{10,6},{11,7},{12,16},{13,17... | collective-permute-start | bytes 645128 | tf_op jit(solution)/shard_map/ppermute | solution.py:52
  14.8 1.0 broadcast_multiply_fusion.x_ref
  15.8 0.0 copy-start.2
  15.8 0.0 copy-start.3
  15.8 0.0 copy-start.4
  15.8 0.0 copy-start.5
  15.9 0.0 copy-start.6
  15.9 0.0 copy-start.7
  15.9 0.0 copy-start.8
  15.9 0.0 copy-start.9
  15.9 0.0 collective-permute-done.2.a_ref
  15.9 5.0 %collective-permute-done.3.b_ref = bf16[6,140,128]{2,1,0:T(8,128)(2,1)S(1)} collective-permute-done((bf16[6,140,128]{2,1,0:T(8,128)(2,1)S(1)}, bf16[6,140,128]{2,1,0:T(8,128)(2,1)S(1)}, u32[]{:S(2)}, u32[]{:S(2)}) %collective-permute-start.3) | collective-permute-done | bytes 215072 | tf_op jit(solution)/shard_map/ppermute | solution.py:52
  20.9 15.7 %conv0_kernel.1 = (f32[9120,128]{1,0:T(8,128)S(1)}, f32[4,768,256]{2,1,0:T(8,128)S(1)}) custom-call(bf16[48,128,128]{2,1,0:T(8,128)(2,1)S(1)} %broadcast_multiply_fusion.x_ref, bf16[48,6,128]{2,1,0:T(8,128)(2,1)S(1)} %collective-permute-done.left_ref, bf16[48,6,128]{2,1,0:T(8,128)(2,1)S(1)} %collective-permute-done.1.right_ref, ...), custom_call_target="tpu_custom_call" | custom-call | flops 1409286144 | bytes 4718592 | tf_op jit(solution)/shard_map/conv0_kernel/pallas_call | solution.py:370
  36.6 5.2 %copy-done = bf16[2,4,3584,256]{3,2,1,0:T(8,128)(2,1)} copy-done((bf16[2,4,3584,256]{3,2,1,0:T(8,128)(2,1)}, bf16[2,4,3584,256]{3,2,1,0:T(8,128)(2,1)S(1)}, u32[]{:S(2)}) %copy-start) | copy-done | bytes 14680088
  41.9 0.0 copy-done.4
  41.9 20.1 %mlp0_kernel.1.x1_ref = f32[9120,128]{1,0:T(8,128)S(1)} custom-call(f32[4,768,256]{2,1,0:T(8,128)S(1)} %get-tuple-element.7.acc_ref, f32[9120,128]{1,0:T(8,128)S(1)} %get-tuple-element.8.x0_ref, f32[2,49,128]{2,1,0:T(8,128)S(1)} %copy.12.k_ref, f32[2,128]{1,0:T(2,128)S(1)} %copy-done.5, f32[2,128]{1,0:T(2,128)S(1)} %copy-done.6, f32[2,128]{1,0:T(2,128)S(1)} %copy-done.7, ...), custom_call_target="tpu_custom_call" | custom-call | flops 1610612736 | bytes 4718592 | tf_op jit(solution)/shard_map/mlp0_kernel/pallas_call | solution.py:370
  62.0 5.2 %copy-done.1 = bf16[2,4,3584,256]{3,2,1,0:T(8,128)(2,1)S(1)} copy-done((bf16[2,4,3584,256]{3,2,1,0:T(8,128)(2,1)S(1)}, bf16[2,4,3584,256]{3,2,1,0:T(8,128)(2,1)}, u32[]{:S(2)}) %copy-start.1) | copy-done | bytes 14680088
  67.2 15.0 %conv1_kernel.1.acc_ref = f32[4,768,256]{2,1,0:T(8,128)S(1)} custom-call(f32[9120,128]{1,0:T(8,128)S(1)} %mlp0_kernel.1.x1_ref, bf16[2,4,3584,256]{3,2,1,0:T(8,128)(2,1)S(1)} %copy-done.1), custom_call_target="tpu_custom_call" | custom-call | flops 1409286144 | bytes 4718592 | tf_op jit(solution)/shard_map/conv1_kernel/pallas_call | solution.py:370
  82.2 1.0 broadcast_in_dim.2.mask_ref
  83.2 17.2 %mlp1_kernel.1 = bf16[48,128,128]{2,1,0:T(8,128)(2,1)} custom-call(f32[4,768,256]{2,1,0:T(8,128)S(1)} %conv1_kernel.1.acc_ref, f32[9120,128]{1,0:T(8,128)S(1)} %mlp0_kernel.1.x1_ref, bf16[48,128,128]{2,1,0:T(8,128)(2,1)S(1)} %broadcast_in_dim.2.mask_ref, f32[2,128]{1,0:T(2,128)S(1)} %copy-done.5, f32[2,128]{1,0:T(2,128)S(1)} %copy-done.6, ...), custom_call_target="tpu_custom_call" | custom-call | flops 1610612736 | bytes 4718592 | tf_op jit(solution)/shard_map/mlp1_kernel/pallas_call | solution.py:370
  (14 shorter events, 0.0 us)
Async XLA Ops:
  1.9 8.5 %collective-permute-start = (bf16[48,6,128]{2,1,0:T(8,128)(2,1)S(1)}, bf16[48,6,128]{2,1,0:T(8,128)(2,1)S(1)}, u32[]{:S(2)}, u32[]{:S(2)}) collective-permute-start(bf16[48,6,128]{2,1,0:T(8,128)(2,1)S(1)} %get-tuple-element.12), channel_id=1, source_target_pairs={{0,1},{1,2},{2,3},{3,0},{4,5},{5,6},{6,7},{7,4},{8,9},{9,10},{10,1... | collective-permute-start | bytes 221192 | tf_op jit(solution)/shard_map/ppermute | solution.py:46
  4.1 6.3 %collective-permute-start.1 = (bf16[48,6,128]{2,1,0:T(8,128)(2,1)S(1)}, bf16[48,6,128]{2,1,0:T(8,128)(2,1)S(1)}, u32[]{:S(2)}, u32[]{:S(2)}) collective-permute-start(bf16[48,6,128]{2,1,0:T(8,128)(2,1)S(1)} %get-tuple-element.11), channel_id=1, source_target_pairs={{1,0},{2,1},{3,2},{0,3},{5,4},{6,5},{7,6},{4,7},{9,8},{10,9},{11,1... | collective-permute-start | bytes 221192 | tf_op jit(solution)/shard_map/ppermute | solution.py:47
  8.3 6.5 %copy-start.10 = (bf16[48,128,128]{2,1,0:T(8,128)(2,1)S(1)}, bf16[48,128,128]{2,1,0:T(8,128)(2,1)}, u32[]{:S(2)}) copy-start(bf16[48,128,128]{2,1,0:T(8,128)(2,1)} %param.11) | copy-start | bytes 4718596
  10.6 5.3 %collective-permute-start.2 = (bf16[6,140,128]{2,1,0:T(8,128)(2,1)S(1)}, bf16[6,140,128]{2,1,0:T(8,128)(2,1)S(1)}, u32[]{:S(2)}, u32[]{:S(2)}) collective-permute-start(bf16[6,140,128]{2,1,0:T(8,128)(2,1)S(1)} %get-tuple-element.14), channel_id=1, source_target_pairs={{0,4},{1,5},{2,6},{3,7},{4,0},{5,1},{6,2},{7,3},{8,12},{9,13},{10,... | collective-permute-start | bytes 645128 | tf_op jit(solution)/shard_map/ppermute | solution.py:51
  11.7 9.3 %collective-permute-start.3 = (bf16[6,140,128]{2,1,0:T(8,128)(2,1)S(1)}, bf16[6,140,128]{2,1,0:T(8,128)(2,1)S(1)}, u32[]{:S(2)}, u32[]{:S(2)}) collective-permute-start(bf16[6,140,128]{2,1,0:T(8,128)(2,1)S(1)} %get-tuple-element.13), channel_id=1, source_target_pairs={{4,8},{5,9},{6,10},{7,11},{8,4},{9,5},{10,6},{11,7},{12,16},{13,17... | collective-permute-start | bytes 645128 | tf_op jit(solution)/shard_map/ppermute | solution.py:52
  15.8 26.0 %copy-start.2 = (bf16[2,128,512]{2,1,0:T(8,128)(2,1)S(1)}, bf16[2,128,512]{2,1,0:T(8,128)(2,1)}, u32[]{:S(2)}) copy-start(bf16[2,128,512]{2,1,0:T(8,128)(2,1)} %refs_3_.3) | copy-start | bytes 786436
  15.8 26.0 %copy-start.3 = (bf16[2,512,128]{2,1,0:T(8,128)(2,1)S(1)}, bf16[2,512,128]{2,1,0:T(8,128)(2,1)}, u32[]{:S(2)}) copy-start(bf16[2,512,128]{2,1,0:T(8,128)(2,1)} %refs_5_.3) | copy-start | bytes 786436
  15.8 26.0 %copy-start.4 = (f32[2,512]{1,0:T(2,128)S(1)}, f32[2,512]{1,0:T(2,128)}, u32[]{:S(2)}) copy-start(f32[2,512]{1,0:T(2,128)} %refs_4_.3) | copy-start | bytes 12292
  15.8 26.0 %copy-start.5 = (f32[2,128]{1,0:T(2,128)S(1)}, f32[2,128]{1,0:T(2,128)}, u32[]{:S(2)}) copy-start(f32[2,128]{1,0:T(2,128)} %refs_0_.3) | copy-start | bytes 3076
  15.9 26.0 %copy-start.6 = (f32[2,128]{1,0:T(2,128)S(1)}, f32[2,128]{1,0:T(2,128)}, u32[]{:S(2)}) copy-start(f32[2,128]{1,0:T(2,128)} %refs_1_.3) | copy-start | bytes 3076
  15.9 26.0 %copy-start.7 = (f32[2,128]{1,0:T(2,128)S(1)}, f32[2,128]{1,0:T(2,128)}, u32[]{:S(2)}) copy-start(f32[2,128]{1,0:T(2,128)} %refs_2_.3) | copy-start | bytes 3076
  15.9 26.0 %copy-start.8 = (f32[2,128]{1,0:T(2,128)S(1)}, f32[2,128]{1,0:T(2,128)}, u32[]{:S(2)}) copy-start(f32[2,128]{1,0:T(2,128)} %refs_6_.3) | copy-start | bytes 3076
  15.9 26.0 %copy-start.9 = (f32[2,128]{1,0:T(2,128)S(1)}, f32[2,128]{1,0:T(2,128)}, u32[]{:S(2)}) copy-start(f32[2,128]{1,0:T(2,128)} %refs_7_.3) | copy-start | bytes 3076
  36.6 5.2 %copy-start = (bf16[2,4,3584,256]{3,2,1,0:T(8,128)(2,1)}, bf16[2,4,3584,256]{3,2,1,0:T(8,128)(2,1)S(1)}, u32[]{:S(2)}) copy-start(bf16[2,4,3584,256]{3,2,1,0:T(8,128)(2,1)S(1)} %tap_matrices.1.w_ref) | copy-start | bytes 44040196
  62.0 5.2 %copy-start.1 = (bf16[2,4,3584,256]{3,2,1,0:T(8,128)(2,1)S(1)}, bf16[2,4,3584,256]{3,2,1,0:T(8,128)(2,1)}, u32[]{:S(2)}) copy-start(bf16[2,4,3584,256]{3,2,1,0:T(8,128)(2,1)} %copy-done) | copy-start | bytes 44040196

commit v5 on v4

--- a/solution.py
+++ b/solution.py
@@ -14,7 +14,7 @@
 REACH = 2 * HALO
 OUTS = 8
 BASE = 8
-VMEM_LIMIT = 30 * 1024 * 1024
+VMEM_LIMIT = 16 * 1024 * 1024
 ERF_POLY = (0.7975078797359708, 0.03700565107996738, -0.0003515176683895368)
 
 
@@ -155,15 +155,12 @@
 def conv(size, relaid_ref, w_ref, acc_ref):
     octets, rows = size.octets, size.rows
 
-    def one(gr, carry):
+    for gr in range(size.groups):
         parts = []
         for r in range(TAPS):
             for a in range(4):
                 parts.append(relaid_ref[gr, a, r * octets : (r + rows) * octets, :])
         acc_ref[gr] = jnp.dot(jnp.concatenate(parts, axis=1), w_ref[0, gr], preferred_element_type=F32)
-        return carry
-
-    lax.fori_loop(0, size.groups, one, 0)
 
 
 def conv0_kernel(size, x_ref, left_ref, right_ref, a_ref, b_ref, w_ref, x0_ref, acc_ref, relaid_ref, flip_ref):

time: 101 us -> 89.6 us (0.89)
  local copies, waits for them, and re-layouts: 12.3 us -> 1.93 us
    unnamed x23 -> x19, local copies, waits for them, and re-layouts: 11.2 us -> 0.86 us
where the time goes in v5:
time: 89.6 us; the launch traced here: 89.4 us
  Pallas kernels  69.4 us (77%)
  starting transfers between devices  8.46 us (9%)
  waiting for transfers between devices  5.02 us (6%)
  other arithmetic  4.28 us (5%)
  local copies, waits for them, and re-layouts  1.93 us (2%)
    pallas_call x4, Pallas kernels, call(): pl.pallas_call(functools.partial(kernel, size), grid=(1,), in_specs=[spec...  67.3 us
    ppermute x1, waiting for transfers between devices, exchange(): lax.ppermute(jnp.where(even, first, last), ('lat', 'lon'), partners(nlat,...  5.01 us
    ppermute x1, starting transfers between devices, exchange(): lax.ppermute(jnp.where(even, first, last), ('lat', 'lon'), partners(nlat,...  3.14 us
    mul x2, other arithmetic, edge(): return fields[r0:r1, c0:c1] * wet_mask[r0:r1, c0:c1].astype(BF)[:, :, None]  2.4 us
    ppermute x1, starting transfers between devices, exchange(): left = lax.ppermute(edge(0, rows, cols - REACH, cols), 'lon', up)  2.18 us
    ppermute x1, starting transfers between devices, exchange(): right = lax.ppermute(edge(0, rows, 0, REACH), 'lon', down)  2.09 us
    pallas_call x1, Pallas kernels, tap_matrices(): pl.pallas_call(tap_kernel, grid=(blocks, groups), in_specs=[pl.BlockSpec(...  2.07 us
  transfers between devices with their start and end apart: 4, of which 1 were waited for; matrix products, arithmetic and copies ran while one was open for 3% of the time, Pallas kernels for 2%

profile of v5, /device:TPU:1, one launch (start us, length us, event | category | flops | bytes accessed | tf_op | source)
XLA Modules:
  0.0 89.4 jit_solution(8261923342285701939)
XLA Ops:
  0.0 0.7 convert_element_type.2
  0.7 0.1 fusion.3
  0.8 1.1 %slice_multiply_fusion.2 = (bf16[48,6,128]{2,1,0:T(8,128)(2,1)S(1)}, bf16[48,6,128]{2,1,0:T(8,128)(2,1)S(1)}) fusion(bf16[48,128,128]{2,1,0:T(8,128)(2,1)} %param.11, bf16[48,6]{1,0:T(8,128)(2,1)S(1)} %get-tuple-element.21, bf16[48,6]{1,0:T(8,128)(2,1)S(1)} %get-tuple-element.22), kind=kLoop, calls=%fused_computation.7 | loop fusion | flops 73728 | bytes 296064 | tf_op jit(solution)/shard_map/mul | solution.py:42
  1.9 2.2 %collective-permute-start = (bf16[48,6,128]{2,1,0:T(8,128)(2,1)S(1)}, bf16[48,6,128]{2,1,0:T(8,128)(2,1)S(1)}, u32[]{:S(2)}, u32[]{:S(2)}) collective-permute-start(bf16[48,6,128]{2,1,0:T(8,128)(2,1)S(1)} %get-tuple-element.12), channel_id=1, source_target_pairs={{0,1},{1,2},{2,3},{3,0},{4,5},{5,6},{6,7},{7,4},{8,9},{9,10},{10,1... | collective-permute-start | bytes 221192 | tf_op jit(solution)/shard_map/ppermute | solution.py:46
  4.1 2.1 %collective-permute-start.1 = (bf16[48,6,128]{2,1,0:T(8,128)(2,1)S(1)}, bf16[48,6,128]{2,1,0:T(8,128)(2,1)S(1)}, u32[]{:S(2)}, u32[]{:S(2)}) collective-permute-start(bf16[48,6,128]{2,1,0:T(8,128)(2,1)S(1)} %get-tuple-element.11), channel_id=1, source_target_pairs={{1,0},{2,1},{3,2},{0,3},{5,4},{6,5},{7,6},{4,7},{9,8},{10,9},{11,1... | collective-permute-start | bytes 221192 | tf_op jit(solution)/shard_map/ppermute | solution.py:47
  6.2 1.3 %slice_multiply_fusion.1 = (bf16[6,128,128]{2,1,0:T(8,128)(2,1)S(1)}, bf16[6,128,128]{2,1,0:T(8,128)(2,1)S(1)}) fusion(bf16[48,128,128]{2,1,0:T(8,128)(2,1)} %param.11, bf16[6,128]{1,0:T(8,128)(2,1)S(1)} %get-tuple-element.19, bf16[6,128]{1,0:T(8,128)(2,1)S(1)} %get-tuple-element.20), kind=kLoop, calls=%fused_computation.6 | loop fusion | flops 196608 | bytes 789504 | tf_op jit(solution)/shard_map/mul | solution.py:42
  7.5 0.8 copy.12.k_ref
  8.3 2.1 %tap_matrices.1.w_ref = bf16[2,4,3584,256]{3,2,1,0:T(8,128)(2,1)S(1)} custom-call(f32[2,49,128]{2,1,0:T(8,128)S(1)} %copy.12.k_ref), custom_call_target="tpu_custom_call" | custom-call | bytes 14680064 | tf_op jit(solution)/shard_map/tap_matrices/pallas_call | solution.py:107
  10.4 0.0 collective-permute-done.left_ref
  10.4 0.0 collective-permute-done.1.right_ref
  10.4 0.2 broadcast_select_fusion
  10.6 1.1 %collective-permute-start.2 = (bf16[6,140,128]{2,1,0:T(8,128)(2,1)S(1)}, bf16[6,140,128]{2,1,0:T(8,128)(2,1)S(1)}, u32[]{:S(2)}, u32[]{:S(2)}) collective-permute-start(bf16[6,140,128]{2,1,0:T(8,128)(2,1)S(1)} %get-tuple-element.14), channel_id=1, source_target_pairs={{0,4},{1,5},{2,6},{3,7},{4,0},{5,1},{6,2},{7,3},{8,12},{9,13},{10,... | collective-permute-start | bytes 645128 | tf_op jit(solution)/shard_map/ppermute | solution.py:51
  11.7 3.1 %collective-permute-start.3 = (bf16[6,140,128]{2,1,0:T(8,128)(2,1)S(1)}, bf16[6,140,128]{2,1,0:T(8,128)(2,1)S(1)}, u32[]{:S(2)}, u32[]{:S(2)}) collective-permute-start(bf16[6,140,128]{2,1,0:T(8,128)(2,1)S(1)} %get-tuple-element.13), channel_id=1, source_target_pairs={{4,8},{5,9},{6,10},{7,11},{8,4},{9,5},{10,6},{11,7},{12,16},{13,17... | collective-permute-start | bytes 645128 | tf_op jit(solution)/shard_map/ppermute | solution.py:52
  14.8 0.0 copy-done.8
  14.8 1.0 %broadcast_multiply_fusion.x_ref = bf16[48,128,128]{2,1,0:T(8,128)(2,1)S(1)} fusion(bf16[48,128,128]{2,1,0:T(8,128)(2,1)S(1)} %copy-done.8, bf16[48,128]{1,0:T(8,128)(2,1)S(1)} %convert_element_type.2), kind=kLoop, calls=%fused_computation | loop fusion | flops 786432 | bytes 3158016 | tf_op jit(solution)/shard_map/mul | solution.py:348
  15.8 0.0 copy-start
  15.8 0.0 copy-start.1
  15.8 0.0 copy-start.2
  15.8 0.0 copy-start.3
  15.9 0.0 copy-start.4
  15.9 0.0 copy-start.5
  15.9 0.0 copy-start.6
  15.9 0.0 copy-start.7
  15.9 0.0 collective-permute-done.2.a_ref
  15.9 5.0 %collective-permute-done.3.b_ref = bf16[6,140,128]{2,1,0:T(8,128)(2,1)S(1)} collective-permute-done((bf16[6,140,128]{2,1,0:T(8,128)(2,1)S(1)}, bf16[6,140,128]{2,1,0:T(8,128)(2,1)S(1)}, u32[]{:S(2)}, u32[]{:S(2)}) %collective-permute-start.3) | collective-permute-done | bytes 215072 | tf_op jit(solution)/shard_map/ppermute | solution.py:52
  20.9 15.2 %conv0_kernel.1 = (f32[9120,128]{1,0:T(8,128)S(1)}, f32[4,768,256]{2,1,0:T(8,128)S(1)}) custom-call(bf16[48,128,128]{2,1,0:T(8,128)(2,1)S(1)} %broadcast_multiply_fusion.x_ref, bf16[48,6,128]{2,1,0:T(8,128)(2,1)S(1)} %collective-permute-done.left_ref, bf16[48,6,128]{2,1,0:T(8,128)(2,1)S(1)} %collective-permute-done.1.right_ref, ...), custom_call_target="tpu_custom_call" | custom-call | flops 1409286144 | bytes 4718592 | tf_op jit(solution)/shard_map/conv0_kernel/pallas_call | solution.py:367
  36.1 0.0 copy-done
  36.1 0.0 copy-done.1
  36.2 20.2 %mlp0_kernel.1.x1_ref = f32[9120,128]{1,0:T(8,128)S(1)} custom-call(f32[4,768,256]{2,1,0:T(8,128)S(1)} %get-tuple-element.7.acc_ref, f32[9120,128]{1,0:T(8,128)S(1)} %get-tuple-element.8.x0_ref, f32[2,49,128]{2,1,0:T(8,128)S(1)} %copy.12.k_ref, f32[2,128]{1,0:T(2,128)S(1)} %copy-done.3, f32[2,128]{1,0:T(2,128)S(1)} %copy-done.4, f32[2,128]{1,0:T(2,128)S(1)} %copy-done.5, ...), custom_call_target="tpu_custom_call" | custom-call | flops 1610612736 | bytes 4718592 | tf_op jit(solution)/shard_map/mlp0_kernel/pallas_call | solution.py:367
  56.4 14.7 %conv1_kernel.1.acc_ref = f32[4,768,256]{2,1,0:T(8,128)S(1)} custom-call(f32[9120,128]{1,0:T(8,128)S(1)} %mlp0_kernel.1.x1_ref, bf16[2,4,3584,256]{3,2,1,0:T(8,128)(2,1)S(1)} %tap_matrices.1.w_ref), custom_call_target="tpu_custom_call" | custom-call | flops 1409286144 | bytes 4718592 | tf_op jit(solution)/shard_map/conv1_kernel/pallas_call | solution.py:367
  71.1 1.0 %broadcast_in_dim.2.mask_ref = bf16[48,128,128]{2,1,0:T(8,128)(2,1)S(1)} broadcast(bf16[48,128]{1,0:T(8,128)(2,1)S(1)} %convert_element_type.2), dimensions={0,1} | broadcast | bytes 1585152 | tf_op jit(solution)/shard_map/broadcast_in_dim | solution.py:347
  72.1 17.3 %mlp1_kernel.1 = bf16[48,128,128]{2,1,0:T(8,128)(2,1)} custom-call(f32[4,768,256]{2,1,0:T(8,128)S(1)} %conv1_kernel.1.acc_ref, f32[9120,128]{1,0:T(8,128)S(1)} %mlp0_kernel.1.x1_ref, bf16[48,128,128]{2,1,0:T(8,128)(2,1)S(1)} %broadcast_in_dim.2.mask_ref, f32[2,128]{1,0:T(2,128)S(1)} %copy-done.3, f32[2,128]{1,0:T(2,128)S(1)} %copy-done.4, ...), custom_call_target="tpu_custom_call" | custom-call | flops 1610612736 | bytes 4718592 | tf_op jit(solution)/shard_map/mlp1_kernel/pallas_call | solution.py:367
  (10 shorter events, 0.0 us)
Async XLA Ops:
  1.9 8.5 %collective-permute-start = (bf16[48,6,128]{2,1,0:T(8,128)(2,1)S(1)}, bf16[48,6,128]{2,1,0:T(8,128)(2,1)S(1)}, u32[]{:S(2)}, u32[]{:S(2)}) collective-permute-start(bf16[48,6,128]{2,1,0:T(8,128)(2,1)S(1)} %get-tuple-element.12), channel_id=1, source_target_pairs={{0,1},{1,2},{2,3},{3,0},{4,5},{5,6},{6,7},{7,4},{8,9},{9,10},{10,1... | collective-permute-start | bytes 221192 | tf_op jit(solution)/shard_map/ppermute | solution.py:46
  4.1 6.3 %collective-permute-start.1 = (bf16[48,6,128]{2,1,0:T(8,128)(2,1)S(1)}, bf16[48,6,128]{2,1,0:T(8,128)(2,1)S(1)}, u32[]{:S(2)}, u32[]{:S(2)}) collective-permute-start(bf16[48,6,128]{2,1,0:T(8,128)(2,1)S(1)} %get-tuple-element.11), channel_id=1, source_target_pairs={{1,0},{2,1},{3,2},{0,3},{5,4},{6,5},{7,6},{4,7},{9,8},{10,9},{11,1... | collective-permute-start | bytes 221192 | tf_op jit(solution)/shard_map/ppermute | solution.py:47
  8.3 6.5 %copy-start.8 = (bf16[48,128,128]{2,1,0:T(8,128)(2,1)S(1)}, bf16[48,128,128]{2,1,0:T(8,128)(2,1)}, u32[]{:S(2)}) copy-start(bf16[48,128,128]{2,1,0:T(8,128)(2,1)} %param.11) | copy-start | bytes 4718596
  10.6 5.3 %collective-permute-start.2 = (bf16[6,140,128]{2,1,0:T(8,128)(2,1)S(1)}, bf16[6,140,128]{2,1,0:T(8,128)(2,1)S(1)}, u32[]{:S(2)}, u32[]{:S(2)}) collective-permute-start(bf16[6,140,128]{2,1,0:T(8,128)(2,1)S(1)} %get-tuple-element.14), channel_id=1, source_target_pairs={{0,4},{1,5},{2,6},{3,7},{4,0},{5,1},{6,2},{7,3},{8,12},{9,13},{10,... | collective-permute-start | bytes 645128 | tf_op jit(solution)/shard_map/ppermute | solution.py:51
  11.7 9.3 %collective-permute-start.3 = (bf16[6,140,128]{2,1,0:T(8,128)(2,1)S(1)}, bf16[6,140,128]{2,1,0:T(8,128)(2,1)S(1)}, u32[]{:S(2)}, u32[]{:S(2)}) collective-permute-start(bf16[6,140,128]{2,1,0:T(8,128)(2,1)S(1)} %get-tuple-element.13), channel_id=1, source_target_pairs={{4,8},{5,9},{6,10},{7,11},{8,4},{9,5},{10,6},{11,7},{12,16},{13,17... | collective-permute-start | bytes 645128 | tf_op jit(solution)/shard_map/ppermute | solution.py:52
  15.8 20.3 %copy-start = (bf16[2,128,512]{2,1,0:T(8,128)(2,1)S(1)}, bf16[2,128,512]{2,1,0:T(8,128)(2,1)}, u32[]{:S(2)}) copy-start(bf16[2,128,512]{2,1,0:T(8,128)(2,1)} %refs_3_.3) | copy-start | bytes 786436
  15.8 20.3 %copy-start.1 = (bf16[2,512,128]{2,1,0:T(8,128)(2,1)S(1)}, bf16[2,512,128]{2,1,0:T(8,128)(2,1)}, u32[]{:S(2)}) copy-start(bf16[2,512,128]{2,1,0:T(8,128)(2,1)} %refs_5_.3) | copy-start | bytes 786436
  15.8 20.3 %copy-start.2 = (f32[2,512]{1,0:T(2,128)S(1)}, f32[2,512]{1,0:T(2,128)}, u32[]{:S(2)}) copy-start(f32[2,512]{1,0:T(2,128)} %refs_4_.3) | copy-start | bytes 12292
  15.8 20.3 %copy-start.3 = (f32[2,128]{1,0:T(2,128)S(1)}, f32[2,128]{1,0:T(2,128)}, u32[]{:S(2)}) copy-start(f32[2,128]{1,0:T(2,128)} %refs_0_.3) | copy-start | bytes 3076
  15.9 20.3 %copy-start.4 = (f32[2,128]{1,0:T(2,128)S(1)}, f32[2,128]{1,0:T(2,128)}, u32[]{:S(2)}) copy-start(f32[2,128]{1,0:T(2,128)} %refs_1_.3) | copy-start | bytes 3076
  15.9 20.3 %copy-start.5 = (f32[2,128]{1,0:T(2,128)S(1)}, f32[2,128]{1,0:T(2,128)}, u32[]{:S(2)}) copy-start(f32[2,128]{1,0:T(2,128)} %refs_2_.3) | copy-start | bytes 3076
  15.9 20.3 %copy-start.6 = (f32[2,128]{1,0:T(2,128)S(1)}, f32[2,128]{1,0:T(2,128)}, u32[]{:S(2)}) copy-start(f32[2,128]{1,0:T(2,128)} %refs_6_.3) | copy-start | bytes 3076
  15.9 20.3 %copy-start.7 = (f32[2,128]{1,0:T(2,128)S(1)}, f32[2,128]{1,0:T(2,128)}, u32[]{:S(2)}) copy-start(f32[2,128]{1,0:T(2,128)} %refs_7_.3) | copy-start | bytes 3076

commit v6 on v5

--- a/solution.py
+++ b/solution.py
@@ -125,12 +125,33 @@
         self.width = 2 * ch // OUTS
         self.groups = ch // self.width
         self.octets = cols // OUTS
-        self.pitch = cols + 24
-        self.lines = (rows + 2 * REACH) * self.pitch
+        self.each = self.octets + 8
+        self.pitch = OUTS * self.each
+        self.lines = (rows + 2 * REACH) * self.pitch + 8
         self.wide0 = cols + 16
-
-    def line(self, row):
-        return pl.multiple_of((row + REACH) * self.pitch, 8)
+        self.plain = cols + 24
+
+    def spot(self, row, o):
+        return pl.multiple_of((row + REACH) * self.pitch, 8) + o * self.each + 8
+
+
+def ordering(size, undo=False):
+    shape = (size.cols, size.cols)
+    by_octet = lax.broadcasted_iota(jnp.int32, shape, 1 if undo else 0)
+    plain = lax.broadcasted_iota(jnp.int32, shape, 0 if undo else 1)
+    same = plain == by_octet % size.octets * OUTS + by_octet // size.octets
+    return jnp.where(same, 1.0, 0.0).astype(BF)
+
+
+def put_row(size, dst_ref, row, val):
+    for o in range(OUTS):
+        dst_ref[pl.ds(size.spot(row, o), size.octets), :] = val[o * size.octets : (o + 1) * size.octets]
+
+
+def put_ends(size, dst_ref, row, before, after):
+    n = before.shape[0]
+    dst_ref[pl.ds(size.spot(row, OUTS - n) - 1, n, stride=size.each), :] = before
+    dst_ref[pl.ds(size.spot(row, 0) + size.octets, n, stride=size.each), :] = after
 
 
 def place():
@@ -139,12 +160,17 @@
 
 
 def relay(size, src_ref, relaid_ref):
+    blank = jnp.zeros((size.octets, size.ch), BF)
+
     def one(i, carry):
-        at = size.line(i - HALO) + BASE - HALO
         for a in range(4):
-            parts = [
-                src_ref[pl.ds(at + 4 * a + j, size.octets, stride=OUTS), :].astype(BF) for j in range(size.groups)
-            ]
+            parts = []
+            for col in range(4 * a - HALO, 4 * a - HALO + 4):
+                if col < OUTS + HALO:
+                    at = size.spot(i - HALO, col % OUTS) + col // OUTS
+                    parts.append(src_ref[pl.ds(at, size.octets), :].astype(BF))
+                else:
+                    parts.append(blank)
             for gr, part in enumerate(regroup(parts, size.width)):
                 relaid_ref[gr, a, pl.ds(pl.multiple_of(i * size.octets, 16), size.octets), :] = part
         return carry
@@ -163,35 +189,51 @@
         acc_ref[gr] = jnp.dot(jnp.concatenate(parts, axis=1), w_ref[0, gr], preferred_element_type=F32)
 
 
-def conv0_kernel(size, x_ref, left_ref, right_ref, a_ref, b_ref, w_ref, x0_ref, acc_ref, relaid_ref, flip_ref):
-    rows, cols, ch, pitch, wide0 = size.rows, size.cols, size.ch, size.pitch, size.wide0
-    base, ext, lead = BASE, cols + 2 * REACH, BASE - REACH
-    line = size.line
+def conv0_kernel(size, x_ref, left_ref, right_ref, a_ref, b_ref, w_ref, x0_ref, edge_ref, acc_ref, relaid_ref, flip_ref):
+    rows, cols, ch, wide0 = size.rows, size.cols, size.ch, size.wide0
+    ext, lead = cols + 2 * REACH, BASE - REACH
     even, top, _ = place()
+    order = ordering(size)
 
     def fill(i, carry):
-        at = line(i)
-        x0_ref[pl.ds(at, base), :] = jnp.zeros((base, ch), F32)
-        x0_ref[pl.ds(at + lead, REACH), :] = left_ref[i].astype(F32)
-        x0_ref[pl.ds(at + base, cols), :] = x_ref[i].astype(F32)
-        x0_ref[pl.ds(at + base + cols, 16), :] = jnp.zeros((16, ch), F32)
-        x0_ref[pl.ds(at + base + cols, REACH), :] = right_ref[i].astype(F32)
+        both = jnp.concatenate([x_ref[2 * i], x_ref[2 * i + 1]], axis=1)
+        both = jnp.dot(order, both, preferred_element_type=F32)
+        for h in range(2):
+            put_row(size, x0_ref, 2 * i + h, both[:, h * ch : (h + 1) * ch])
+            put_ends(size, x0_ref, 2 * i + h, left_ref[2 * i + h].astype(F32), right_ref[2 * i + h].astype(F32))
         return carry
 
-    lax.fori_loop(0, rows, fill, 0)
+    lax.fori_loop(0, rows // 2, fill, 0)
+
+    edge_ref[...] = jnp.zeros(edge_ref.shape, F32)
     flip_ref[...] = jnp.zeros(flip_ref.shape, F32)
     at = lax.broadcasted_iota(jnp.int32, (wide0, wide0), 0)
     to = lax.broadcasted_iota(jnp.int32, (wide0, wide0), 1)
     mirror = jnp.where(to == jnp.where(top, ext - 1 - at, at), 1.0, 0.0).astype(BF)
     for i in range(REACH):
-        south, north = i * pitch, (rows + REACH + i) * pitch
-        x0_ref[south : south + pitch, :] = jnp.zeros((pitch, ch), F32)
-        x0_ref[south + lead : south + lead + ext, :] = jnp.where(even, b_ref[i].astype(F32), a_ref[i].astype(F32))
+        edge_ref[0, i, lead : lead + ext, :] = jnp.where(even, b_ref[i].astype(F32), a_ref[i].astype(F32))
         src = jnp.where(top, REACH - 1 - i, i)
         flip_ref[0:ext, :] = jnp.where(even, a_ref[src].astype(F32), b_ref[src].astype(F32))
         turned = jnp.dot(mirror, flip_ref[0:wide0, :].astype(BF), preferred_element_type=F32)
-        x0_ref[north : north + pitch, :] = jnp.zeros((pitch, ch), F32)
-        x0_ref[north + lead : north + lead + wide0, :] = turned
+        edge_ref[1, HALO + i, lead : lead + wide0, :] = turned
+    for i in range(HALO):
+        for side, slot, row in ((0, REACH + i, i), (1, i, rows - HALO + i)):
+            edge_ref[side, slot, lead:BASE, :] = left_ref[row].astype(F32)
+            edge_ref[side, slot, BASE : BASE + cols, :] = x_ref[row].astype(F32)
+            edge_ref[side, slot, BASE + cols : BASE + cols + REACH, :] = right_ref[row].astype(F32)
+    for i in range(HALO):
+        lines = [edge_ref[0, HALO + i], edge_ref[1, HALO + i]]
+        both = jnp.concatenate([line[BASE : BASE + cols].astype(BF) for line in lines], axis=1)
+        both = jnp.dot(order, both, preferred_element_type=F32)
+        for side, row in ((0, i - HALO), (1, rows + i)):
+            put_row(size, x0_ref, row, both[:, side * ch : (side + 1) * ch])
+            put_ends(
+                size,
+                x0_ref,
+                row,
+                edge_ref[side, HALO + i, lead:BASE, :],
+                edge_ref[side, HALO + i, BASE + cols : BASE + cols + REACH, :],
+            )
     relay(size, x0_ref, relaid_ref)
     conv(size, relaid_ref, w_ref, acc_ref)
 
@@ -212,8 +254,9 @@
 def norm(b, params, val):
     cbias_ref, gain_ref, nbias_ref = params[:3]
     val = val + cbias_ref[b : b + 1, :]
-    cen = val - jnp.mean(val, axis=-1, keepdims=True)
-    var = jnp.mean(cen * cen, axis=-1, keepdims=True)
+    share = 1.0 / val.shape[-1]
+    cen = val - jnp.sum(val, axis=-1, keepdims=True) * share
+    var = jnp.sum(cen * cen, axis=-1, keepdims=True) * share
     return (cen * lax.rsqrt(var + 1e-6) * gain_ref[b : b + 1, :] + nbias_ref[b : b + 1, :]).astype(BF)
 
 
@@ -242,7 +285,7 @@
     return val.astype(BF).astype(F32)
 
 
-def inner(size, b, params, acc_ref, src_ref, dst_ref):
+def inner(size, b, params, acc_ref, src_ref, keep):
     rows, octets, groups, ch = size.rows, size.octets, size.groups, size.ch
     step = next(d for d in (8, 6, 4, 3, 2, 1) if rows % d == 0)
     n = step * octets
@@ -254,50 +297,50 @@
             ]
             for j, branch in enumerate(mlp(b, params, regroup(parts, size.width))):
                 for i in range(step):
-                    at = size.line(t * step + i) + BASE + half * groups + j
-                    spot = pl.ds(at, octets, stride=OUTS)
-                    dst_ref[spot, :] = rounded(src_ref[spot, :] + branch[i * octets : (i + 1) * octets])
+                    row, o = t * step + i, half * groups + j
+                    old = src_ref[pl.ds(size.spot(row, o), octets), :]
+                    keep(row, o, old + branch[i * octets : (i + 1) * octets])
         return carry
 
     lax.fori_loop(0, rows // step, one, 0)
 
 
-def mlp0_kernel(size, acc_ref, x0_ref, k_ref, *refs):
-    params, (x1_ref, strip_ref) = refs[:8], refs[8:]
-    rows, cols, ch, pitch, wide0 = size.rows, size.cols, size.ch, size.pitch, size.wide0
-    base, lead, near = BASE, BASE - REACH, BASE - HALO
+def mlp0_kernel(size, acc_ref, x0_ref, edge_ref, k_ref, *refs):
+    params, (x1_ref, strip_ref, side_ref) = refs[:8], refs[8:]
+    rows, cols, ch, wide0, octets = size.rows, size.cols, size.ch, size.wide0, size.octets
+    lead, near = BASE - REACH, BASE - HALO
     _, top, bottom = place()
 
-    def clear(i, carry):
-        at = size.line(i)
-        x1_ref[pl.ds(at, base), :] = jnp.zeros((base, ch), F32)
-        x1_ref[pl.ds(at + base + cols, 16), :] = jnp.zeros((16, ch), F32)
-        return carry
-
-    lax.fori_loop(0, rows, clear, 0)
-    inner(size, 0, params, acc_ref, x0_ref, x1_ref)
-    for side in range(2):
-        first = lead if side == 0 else base + cols - HALO
+    def keep(row, o, new):
+        x1_ref[pl.ds(size.spot(row, o), octets), :] = rounded(new)
+
+    inner(size, 0, params, acc_ref, x0_ref, keep)
+
+    def column(col, first, count):
+        return pl.ds(size.spot(first, col % OUTS) + col // OUTS, count, stride=size.pitch)
+
+    for start in (-HALO, cols):
+        for c in range(TAPS + HALO - 1):
+            side_ref[c, 0 : rows + 2 * HALO, :] = x0_ref[column(start - HALO + c, -HALO, rows + 2 * HALO), :]
         sums = [jnp.zeros((rows, ch), F32) for _ in range(HALO)]
         for r in range(TAPS):
             for c in range(TAPS + HALO - 1):
-                cells = x0_ref[pl.ds((REACH - HALO + r) * pitch + first + c, rows, stride=pitch), :]
+                cells = side_ref[c, r : r + rows, :]
                 for i in range(HALO):
                     if 0 <= c - i < TAPS:
                         tap = TAPS * r + c - i
                         sums[i] = sums[i] + cells * k_ref[0, tap : tap + 1, :]
-        start = near if side == 0 else base + cols
         for i, branch in enumerate(mlp(0, params, sums)):
-            spot = pl.ds(REACH * pitch + start + i, rows, stride=pitch)
-            x1_ref[spot, :] = rounded(x0_ref[spot, :] + branch)
+            at = column(start + i, 0, rows)
+            x1_ref[at, :] = rounded(x0_ref[at, :] + branch)
+
     piece = wide0 // 3
     for side in range(2):
-        first = (0 if side == 0 else rows + HALO) * pitch
         for c in range(0, wide0, piece):
             sums = [jnp.zeros((piece, ch), F32) for _ in range(HALO)]
             for s in range(TAPS):
-                at = first + lead + s + c
-                lines = [x0_ref[at + i * pitch : at + i * pitch + piece, :] for i in range(TAPS + HALO - 1)]
+                at = lead + s + c
+                lines = [edge_ref[side, i, at : at + piece, :] for i in range(TAPS + HALO - 1)]
                 for r in range(TAPS):
                     tap = TAPS * r + s
                     if side == 1:
@@ -306,27 +349,47 @@
                     for i in range(HALO):
                         sums[i] = sums[i] + lines[i + r] * weight
             for i in range(HALO):
-                strip_ref[side * HALO + i, c : c + piece, :] = sums[i]
+                strip_ref[side, i, c : c + piece, :] = sums[i]
     for side in range(2):
-        branches = mlp(0, params, [strip_ref[side * HALO + i] for i in range(HALO)])
+        branches = mlp(0, params, [strip_ref[side, i] for i in range(HALO)])
         for i, branch in enumerate(branches):
-            row = i - HALO if side == 0 else rows + i
-            at = (row + REACH) * pitch + near
-            new = rounded(x0_ref[at : at + wide0, :] + branch)
+            new = rounded(edge_ref[side, HALO + i, near : near + wide0, :] + branch)
             if side == 0:
                 new = jnp.where(bottom, 0.0, new)
-            x1_ref[at : at + wide0, :] = new
+            strip_ref[side, i] = new
+    order = ordering(size)
+    for i in range(HALO):
+        both = jnp.concatenate([strip_ref[side, i, HALO : HALO + cols, :].astype(BF) for side in range(2)], axis=1)
+        both = jnp.dot(order, both, preferred_element_type=F32)
+        for side, row in ((0, i - HALO), (1, rows + i)):
+            put_row(size, x1_ref, row, both[:, side * ch : (side + 1) * ch])
+            put_ends(
+                size,
+                x1_ref,
+                row,
+                strip_ref[side, i, 0:HALO, :],
+                strip_ref[side, i, HALO + cols : 2 * HALO + cols, :],
+            )
 
 
 def mlp1_kernel(size, acc_ref, x1_ref, mask_ref, *refs):
     params, (out_ref, x2_ref) = refs[:8], refs[8:]
-    inner(size, 1, params, acc_ref, x1_ref, x2_ref)
+    ch, octets = size.ch, size.octets
+
+    def keep(row, o, new):
+        x2_ref[row, o * octets : (o + 1) * octets, :] = new.astype(BF)
+
+    inner(size, 1, params, acc_ref, x1_ref, keep)
+    back = ordering(size, undo=True)
 
     def finish(i, carry):
-        out_ref[i] = x2_ref[pl.ds(size.line(i) + BASE, size.cols), :].astype(BF) * mask_ref[i]
+        both = jnp.concatenate([x2_ref[2 * i], x2_ref[2 * i + 1]], axis=1)
+        both = jnp.dot(back, both, preferred_element_type=F32).astype(BF)
+        for h in range(2):
+            out_ref[2 * i + h] = both[:, h * ch : (h + 1) * ch] * mask_ref[2 * i + h]
         return carry
 
-    lax.fori_loop(0, size.rows, finish, 0)
+    lax.fori_loop(0, size.rows // 2, finish, 0)
 
 
 def shards(
@@ -379,18 +442,20 @@
     conv_flops = 2 * cells * ch * depth // OUTS * 2
     mlp_flops = 4 * cells * ch * hid
     params = (conv_bias, norm_gain, norm_bias, in_weight, in_bias, out_weight, out_bias, layer_scale)
-    x0, acc = call(
+    edges = jax.ShapeDtypeStruct((2, TAPS + HALO - 1, size.plain, ch), F32)
+    x0, edge, acc = call(
         conv0_kernel,
         (state, left, right, got_a, got_b, taps),
-        (padded, sums),
-        [relaid, pltpu.VMEM((cols + 24, ch), F32)],
+        (padded, edges, sums),
+        [relaid, pltpu.VMEM((size.plain, ch), F32)],
         conv_flops,
     )
-    strips = pltpu.VMEM((2 * HALO, cols + 16, ch), F32)
-    x1 = call(mlp0_kernel, (acc, x0, conv_kernel) + params, padded, [strips], mlp_flops)
+    strips = pltpu.VMEM((2, HALO, size.wide0, ch), F32)
+    sides = pltpu.VMEM((TAPS + HALO - 1, rows + 8, ch), F32)
+    x1 = call(mlp0_kernel, (acc, x0, edge, conv_kernel) + params, padded, [strips, sides], mlp_flops)
     acc = call(conv1_kernel, (x1, taps), sums, [relaid], conv_flops)
-    whole = pltpu.VMEM((size.lines, ch), F32)
-    return call(mlp1_kernel, (acc, x1, mask) + params, jax.ShapeDtypeStruct(fields.shape, BF), [whole], mlp_flops)
+    last = pltpu.VMEM(fields.shape, BF)
+    return call(mlp1_kernel, (acc, x1, mask) + params, jax.ShapeDtypeStruct(fields.shape, BF), [last], mlp_flops)
 
 
 def solution(mesh):

time: 89.6 us -> 97.9 us (1.093)
  Pallas kernels: 69.4 us -> 77.7 us
    pallas_call x4, Pallas kernels: 67.3 us -> 75.6 us  [call(): pl.pallas_call(functools.partial(kernel, size), grid=(1,), in_specs=[spec...]
where the time goes in v6:
time: 97.9 us; the launch traced here: 97.6 us
  Pallas kernels  77.7 us (79%)
  starting transfers between devices  8.46 us (9%)
  waiting for transfers between devices  5.02 us (5%)
  other arithmetic  4.28 us (4%)
  local copies, waits for them, and re-layouts  1.93 us (2%)
    pallas_call x4, Pallas kernels, call(): pl.pallas_call(functools.partial(kernel, size), grid=(1,), in_specs=[spec...  75.6 us
    ppermute x1, waiting for transfers between devices, exchange(): lax.ppermute(jnp.where(even, first, last), ('lat', 'lon'), partners(nlat,...  5.01 us
    ppermute x1, starting transfers between devices, exchange(): lax.ppermute(jnp.where(even, first, last), ('lat', 'lon'), partners(nlat,...  3.14 us
    mul x2, other arithmetic, edge(): return fields[r0:r1, c0:c1] * wet_mask[r0:r1, c0:c1].astype(BF)[:, :, None]  2.4 us
    ppermute x1, starting transfers between devices, exchange(): left = lax.ppermute(edge(0, rows, cols - REACH, cols), 'lon', up)  2.18 us
    ppermute x1, starting transfers between devices, exchange(): right = lax.ppermute(edge(0, rows, 0, REACH), 'lon', down)  2.09 us
    pallas_call x1, Pallas kernels, tap_matrices(): pl.pallas_call(tap_kernel, grid=(blocks, groups), in_specs=[pl.BlockSpec(...  2.07 us
  transfers between devices with their start and end apart: 4, of which 1 were waited for; matrix products, arithmetic and copies ran while one was open for 3% of the time, Pallas kernels for 2%

profile of v6, /device:TPU:1, one launch (start us, length us, event | category | flops | bytes accessed | tf_op | source)
XLA Modules:
  0.0 97.6 jit_solution(10577676730943152014)
XLA Ops:
  0.0 0.7 convert_element_type.2
  0.7 0.1 fusion.3
  0.8 1.1 %slice_multiply_fusion.2 = (bf16[48,6,128]{2,1,0:T(8,128)(2,1)S(1)}, bf16[48,6,128]{2,1,0:T(8,128)(2,1)S(1)}) fusion(bf16[48,128,128]{2,1,0:T(8,128)(2,1)} %param.11, bf16[48,6]{1,0:T(8,128)(2,1)S(1)} %get-tuple-element.23, bf16[48,6]{1,0:T(8,128)(2,1)S(1)} %get-tuple-element.24), kind=kLoop, calls=%fused_computation.7 | loop fusion | flops 73728 | bytes 296064 | tf_op jit(solution)/shard_map/mul | solution.py:42
  1.9 2.2 %collective-permute-start = (bf16[48,6,128]{2,1,0:T(8,128)(2,1)S(1)}, bf16[48,6,128]{2,1,0:T(8,128)(2,1)S(1)}, u32[]{:S(2)}, u32[]{:S(2)}) collective-permute-start(bf16[48,6,128]{2,1,0:T(8,128)(2,1)S(1)} %get-tuple-element.14), channel_id=1, source_target_pairs={{0,1},{1,2},{2,3},{3,0},{4,5},{5,6},{6,7},{7,4},{8,9},{9,10},{10,1... | collective-permute-start | bytes 221192 | tf_op jit(solution)/shard_map/ppermute | solution.py:46
  4.1 2.1 %collective-permute-start.1 = (bf16[48,6,128]{2,1,0:T(8,128)(2,1)S(1)}, bf16[48,6,128]{2,1,0:T(8,128)(2,1)S(1)}, u32[]{:S(2)}, u32[]{:S(2)}) collective-permute-start(bf16[48,6,128]{2,1,0:T(8,128)(2,1)S(1)} %get-tuple-element.13), channel_id=1, source_target_pairs={{1,0},{2,1},{3,2},{0,3},{5,4},{6,5},{7,6},{4,7},{9,8},{10,9},{11,1... | collective-permute-start | bytes 221192 | tf_op jit(solution)/shard_map/ppermute | solution.py:47
  6.2 1.3 %slice_multiply_fusion.1 = (bf16[6,128,128]{2,1,0:T(8,128)(2,1)S(1)}, bf16[6,128,128]{2,1,0:T(8,128)(2,1)S(1)}) fusion(bf16[48,128,128]{2,1,0:T(8,128)(2,1)} %param.11, bf16[6,128]{1,0:T(8,128)(2,1)S(1)} %get-tuple-element.21, bf16[6,128]{1,0:T(8,128)(2,1)S(1)} %get-tuple-element.22), kind=kLoop, calls=%fused_computation.6 | loop fusion | flops 196608 | bytes 789504 | tf_op jit(solution)/shard_map/mul | solution.py:42
  7.5 0.8 copy.12.k_ref
  8.3 2.1 %tap_matrices.1.w_ref = bf16[2,4,3584,256]{3,2,1,0:T(8,128)(2,1)S(1)} custom-call(f32[2,49,128]{2,1,0:T(8,128)S(1)} %copy.12.k_ref), custom_call_target="tpu_custom_call" | custom-call | bytes 14680064 | tf_op jit(solution)/shard_map/tap_matrices/pallas_call | solution.py:107
  10.4 0.0 collective-permute-done.left_ref
  10.4 0.0 collective-permute-done.1.right_ref
  10.4 0.2 broadcast_select_fusion
  10.6 1.1 %collective-permute-start.2 = (bf16[6,140,128]{2,1,0:T(8,128)(2,1)S(1)}, bf16[6,140,128]{2,1,0:T(8,128)(2,1)S(1)}, u32[]{:S(2)}, u32[]{:S(2)}) collective-permute-start(bf16[6,140,128]{2,1,0:T(8,128)(2,1)S(1)} %get-tuple-element.16), channel_id=1, source_target_pairs={{0,4},{1,5},{2,6},{3,7},{4,0},{5,1},{6,2},{7,3},{8,12},{9,13},{10,... | collective-permute-start | bytes 645128 | tf_op jit(solution)/shard_map/ppermute | solution.py:51
  11.7 3.1 %collective-permute-start.3 = (bf16[6,140,128]{2,1,0:T(8,128)(2,1)S(1)}, bf16[6,140,128]{2,1,0:T(8,128)(2,1)S(1)}, u32[]{:S(2)}, u32[]{:S(2)}) collective-permute-start(bf16[6,140,128]{2,1,0:T(8,128)(2,1)S(1)} %get-tuple-element.15), channel_id=1, source_target_pairs={{4,8},{5,9},{6,10},{7,11},{8,4},{9,5},{10,6},{11,7},{12,16},{13,17... | collective-permute-start | bytes 645128 | tf_op jit(solution)/shard_map/ppermute | solution.py:52
  14.8 0.0 copy-done.8
  14.8 1.0 %broadcast_multiply_fusion.x_ref = bf16[48,128,128]{2,1,0:T(8,128)(2,1)S(1)} fusion(bf16[48,128,128]{2,1,0:T(8,128)(2,1)S(1)} %copy-done.8, bf16[48,128]{1,0:T(8,128)(2,1)S(1)} %convert_element_type.2), kind=kLoop, calls=%fused_computation | loop fusion | flops 786432 | bytes 3158016 | tf_op jit(solution)/shard_map/mul | solution.py:411
  15.8 0.0 copy-start
  15.8 0.0 copy-start.1
  15.8 0.0 copy-start.2
  15.9 0.0 copy-start.3
  15.9 0.0 copy-start.4
  15.9 0.0 copy-start.5
  15.9 0.0 copy-start.6
  15.9 0.0 copy-start.7
  15.9 0.0 collective-permute-done.2.a_ref
  15.9 5.0 %collective-permute-done.3.b_ref = bf16[6,140,128]{2,1,0:T(8,128)(2,1)S(1)} collective-permute-done((bf16[6,140,128]{2,1,0:T(8,128)(2,1)S(1)}, bf16[6,140,128]{2,1,0:T(8,128)(2,1)S(1)}, u32[]{:S(2)}, u32[]{:S(2)}) %collective-permute-start.3) | collective-permute-done | bytes 215072 | tf_op jit(solution)/shard_map/ppermute | solution.py:52
  20.9 19.3 %conv0_kernel.1 = (f32[11528,128]{1,0:T(8,128)S(1)}, f32[2,9,152,128]{3,2,1,0:T(8,128)S(1)}, f32[4,768,256]{2,1,0:T(8,128)S(1)}) custom-call(bf16[48,128,128]{2,1,0:T(8,128)(2,1)S(1)} %broadcast_multiply_fusion.x_ref, bf16[48,6,128]{2,1,0:T(8,128)(2,1)S(1)} %collective-permute-done.left_ref, bf16[48,6,128]{2,1,0:T(8,128)(2,1)S(1)} %collective-permute-done.1.right_ref, ...), custom_call_target="tpu_custom_call" | custom-call | flops 1409286144 | bytes 4718592 | tf_op jit(solution)/shard_map/conv0_kernel/pallas_call | solution.py:430
  40.3 0.0 copy-done
  40.3 0.0 copy-done.1
  40.3 20.6 %mlp0_kernel.1.x1_ref = f32[11528,128]{1,0:T(8,128)S(1)} custom-call(f32[4,768,256]{2,1,0:T(8,128)S(1)} %get-tuple-element.8.acc_ref, f32[11528,128]{1,0:T(8,128)S(1)} %get-tuple-element.9.x0_ref, f32[2,9,152,128]{3,2,1,0:T(8,128)S(1)} %get-tuple-element.10.edge_ref, f32[2,49,128]{2,1,0:T(8,128)S(1)} %copy.12.k_ref, f32[2,128]{1,0:T(2,128)S(1)} %copy-done.3, ...), custom_call_target="tpu_custom_call" | custom-call | flops 1610612736 | bytes 4718592 | tf_op jit(solution)/shard_map/mlp0_kernel/pallas_call | solution.py:430
  61.0 15.3 %conv1_kernel.1.acc_ref = f32[4,768,256]{2,1,0:T(8,128)S(1)} custom-call(f32[11528,128]{1,0:T(8,128)S(1)} %mlp0_kernel.1.x1_ref, bf16[2,4,3584,256]{3,2,1,0:T(8,128)(2,1)S(1)} %tap_matrices.1.w_ref), custom_call_target="tpu_custom_call" | custom-call | flops 1409286144 | bytes 4718592 | tf_op jit(solution)/shard_map/conv1_kernel/pallas_call | solution.py:430
  76.3 1.0 %broadcast_in_dim.2.mask_ref = bf16[48,128,128]{2,1,0:T(8,128)(2,1)S(1)} broadcast(bf16[48,128]{1,0:T(8,128)(2,1)S(1)} %convert_element_type.2), dimensions={0,1} | broadcast | bytes 1585152 | tf_op jit(solution)/shard_map/broadcast_in_dim | solution.py:410
  77.3 20.3 %mlp1_kernel.1 = bf16[48,128,128]{2,1,0:T(8,128)(2,1)} custom-call(f32[4,768,256]{2,1,0:T(8,128)S(1)} %conv1_kernel.1.acc_ref, f32[11528,128]{1,0:T(8,128)S(1)} %mlp0_kernel.1.x1_ref, bf16[48,128,128]{2,1,0:T(8,128)(2,1)S(1)} %broadcast_in_dim.2.mask_ref, f32[2,128]{1,0:T(2,128)S(1)} %copy-done.3, f32[2,128]{1,0:T(2,128)S(1)} %copy-done.4, ...), custom_call_target="tpu_custom_call" | custom-call | flops 1610612736 | bytes 4718592 | tf_op jit(solution)/shard_map/mlp1_kernel/pallas_call | solution.py:430
  (10 shorter events, 0.0 us)
Async XLA Ops:
  1.9 8.5 %collective-permute-start = (bf16[48,6,128]{2,1,0:T(8,128)(2,1)S(1)}, bf16[48,6,128]{2,1,0:T(8,128)(2,1)S(1)}, u32[]{:S(2)}, u32[]{:S(2)}) collective-permute-start(bf16[48,6,128]{2,1,0:T(8,128)(2,1)S(1)} %get-tuple-element.14), channel_id=1, source_target_pairs={{0,1},{1,2},{2,3},{3,0},{4,5},{5,6},{6,7},{7,4},{8,9},{9,10},{10,1... | collective-permute-start | bytes 221192 | tf_op jit(solution)/shard_map/ppermute | solution.py:46
  4.1 6.3 %collective-permute-start.1 = (bf16[48,6,128]{2,1,0:T(8,128)(2,1)S(1)}, bf16[48,6,128]{2,1,0:T(8,128)(2,1)S(1)}, u32[]{:S(2)}, u32[]{:S(2)}) collective-permute-start(bf16[48,6,128]{2,1,0:T(8,128)(2,1)S(1)} %get-tuple-element.13), channel_id=1, source_target_pairs={{1,0},{2,1},{3,2},{0,3},{5,4},{6,5},{7,6},{4,7},{9,8},{10,9},{11,1... | collective-permute-start | bytes 221192 | tf_op jit(solution)/shard_map/ppermute | solution.py:47
  8.3 6.5 %copy-start.8 = (bf16[48,128,128]{2,1,0:T(8,128)(2,1)S(1)}, bf16[48,128,128]{2,1,0:T(8,128)(2,1)}, u32[]{:S(2)}) copy-start(bf16[48,128,128]{2,1,0:T(8,128)(2,1)} %param.11) | copy-start | bytes 4718596
  10.6 5.3 %collective-permute-start.2 = (bf16[6,140,128]{2,1,0:T(8,128)(2,1)S(1)}, bf16[6,140,128]{2,1,0:T(8,128)(2,1)S(1)}, u32[]{:S(2)}, u32[]{:S(2)}) collective-permute-start(bf16[6,140,128]{2,1,0:T(8,128)(2,1)S(1)} %get-tuple-element.16), channel_id=1, source_target_pairs={{0,4},{1,5},{2,6},{3,7},{4,0},{5,1},{6,2},{7,3},{8,12},{9,13},{10,... | collective-permute-start | bytes 645128 | tf_op jit(solution)/shard_map/ppermute | solution.py:51
  11.7 9.3 %collective-permute-start.3 = (bf16[6,140,128]{2,1,0:T(8,128)(2,1)S(1)}, bf16[6,140,128]{2,1,0:T(8,128)(2,1)S(1)}, u32[]{:S(2)}, u32[]{:S(2)}) collective-permute-start(bf16[6,140,128]{2,1,0:T(8,128)(2,1)S(1)} %get-tuple-element.15), channel_id=1, source_target_pairs={{4,8},{5,9},{6,10},{7,11},{8,4},{9,5},{10,6},{11,7},{12,16},{13,17... | collective-permute-start | bytes 645128 | tf_op jit(solution)/shard_map/ppermute | solution.py:52
  15.8 24.5 %copy-start = (bf16[2,128,512]{2,1,0:T(8,128)(2,1)S(1)}, bf16[2,128,512]{2,1,0:T(8,128)(2,1)}, u32[]{:S(2)}) copy-start(bf16[2,128,512]{2,1,0:T(8,128)(2,1)} %refs_3_.3) | copy-start | bytes 786436
  15.8 24.5 %copy-start.1 = (bf16[2,512,128]{2,1,0:T(8,128)(2,1)S(1)}, bf16[2,512,128]{2,1,0:T(8,128)(2,1)}, u32[]{:S(2)}) copy-start(bf16[2,512,128]{2,1,0:T(8,128)(2,1)} %refs_5_.3) | copy-start | bytes 786436
  15.8 24.5 %copy-start.2 = (f32[2,512]{1,0:T(2,128)S(1)}, f32[2,512]{1,0:T(2,128)}, u32[]{:S(2)}) copy-start(f32[2,512]{1,0:T(2,128)} %refs_4_.3) | copy-start | bytes 12292
  15.9 24.4 %copy-start.3 = (f32[2,128]{1,0:T(2,128)S(1)}, f32[2,128]{1,0:T(2,128)}, u32[]{:S(2)}) copy-start(f32[2,128]{1,0:T(2,128)} %refs_0_.3) | copy-start | bytes 3076
  15.9 24.4 %copy-start.4 = (f32[2,128]{1,0:T(2,128)S(1)}, f32[2,128]{1,0:T(2,128)}, u32[]{:S(2)}) copy-start(f32[2,128]{1,0:T(2,128)} %refs_1_.3) | copy-start | bytes 3076
  15.9 24.4 %copy-start.5 = (f32[2,128]{1,0:T(2,128)S(1)}, f32[2,128]{1,0:T(2,128)}, u32[]{:S(2)}) copy-start(f32[2,128]{1,0:T(2,128)} %refs_2_.3) | copy-start | bytes 3076
  15.9 24.4 %copy-start.6 = (f32[2,128]{1,0:T(2,128)S(1)}, f32[2,128]{1,0:T(2,128)}, u32[]{:S(2)}) copy-start(f32[2,128]{1,0:T(2,128)} %refs_6_.3) | copy-start | bytes 3076
  15.9 24.4 %copy-start.7 = (f32[2,128]{1,0:T(2,128)S(1)}, f32[2,128]{1,0:T(2,128)}, u32[]{:S(2)}) copy-start(f32[2,128]{1,0:T(2,128)} %refs_7_.3) | copy-start | bytes 3076

commit v7 on v5

--- a/solution.py
+++ b/solution.py
@@ -69,7 +69,7 @@
     return parts
 
 
-def tap_kernel(k_ref, w_ref, kv_ref):
+def tap_kernel(k_ref, inw_ref, cbias_ref, gain_ref, nbias_ref, w_ref, spread_ref, lines_ref, kv_ref):
     ch = k_ref.shape[2]
     lanes = w_ref.shape[3]
     width = lanes // OUTS
@@ -78,6 +78,13 @@
 
     @pl.when(gr == 0)
     def _():
+        block = lax.broadcasted_iota(jnp.int32, (1, ch), 1) // width
+        for n, ref in enumerate((cbias_ref, gain_ref, nbias_ref)):
+            for g in range(groups):
+                line = jnp.zeros((1, ch), F32)
+                for j in range(groups):
+                    line = jnp.where(block == j, pltpu.roll(ref[0], (j - g) * width % ch, 1), line)
+                lines_ref[0, n * groups + g : n * groups + g + 1, :] = line
         down = [k_ref[0, pl.ds(s, TAPS, stride=TAPS), :] for s in range(TAPS - 1, -1, -1)]
         down.append(jnp.zeros((TAPS, ch), F32))
         halves = [regroup(down[i : i + groups], width) for i in range(0, OUTS, groups)]
@@ -96,10 +103,15 @@
             vec = kv_ref[gr, p, r : r + 1, :]
             at = (r * 2 * OUTS + p) * width
             w_ref[0, 0, at : at + width, :] = jnp.where(own, vec, 0.0).astype(BF)
-
-
-def tap_matrices(conv_kernel):
+    mine = inw_ref[0]
+    for o in range(groups):
+        for j in range(groups):
+            spread_ref[0, o, j * width : (j + 1) * width, :] = mine if j == o else jnp.zeros_like(mine)
+
+
+def tap_matrices(conv_kernel, in_weight, conv_bias, norm_gain, norm_bias):
     blocks, taps, ch = conv_kernel.shape
+    hid = in_weight.shape[2]
     lanes = 2 * ch
     width = lanes // OUTS
     groups = ch // width
@@ -107,16 +119,28 @@
     return pl.pallas_call(
         tap_kernel,
         grid=(blocks, groups),
-        in_specs=[pl.BlockSpec((1, taps, ch), lambda b, g: (b, 0, 0))],
-        out_specs=pl.BlockSpec((1, 1, depth, lanes), lambda b, g: (b, g, 0, 0)),
-        out_shape=jax.ShapeDtypeStruct((blocks, groups, depth, lanes), BF),
+        in_specs=[
+            pl.BlockSpec((1, taps, ch), lambda b, g: (b, 0, 0)),
+            pl.BlockSpec((1, width, hid), lambda b, g: (b, g, 0)),
+        ]
+        + [pl.BlockSpec((1, 1, ch), lambda b, g: (b, 0, 0))] * 3,
+        out_specs=(
+            pl.BlockSpec((1, 1, depth, lanes), lambda b, g: (b, g, 0, 0)),
+            pl.BlockSpec((1, groups, ch, hid), lambda b, g: (b, 0, g, 0)),
+            pl.BlockSpec((1, 3 * groups, ch), lambda b, g: (b, 0, 0)),
+        ),
+        out_shape=(
+            jax.ShapeDtypeStruct((blocks, groups, depth, lanes), BF),
+            jax.ShapeDtypeStruct((blocks, groups, groups * ch, hid), BF),
+            jax.ShapeDtypeStruct((blocks, 3 * groups, ch), F32),
+        ),
         scratch_shapes=[pltpu.VMEM((groups, 2 * OUTS, 8, lanes), F32)],
         compiler_params=pltpu.CompilerParams(vmem_limit_bytes=24 * 1024 * 1024),
         cost_estimate=pl.CostEstimate(
             flops=0, bytes_accessed=2 * blocks * groups * depth * lanes, transcendentals=0
         ),
         name="tap_matrices",
-    )(conv_kernel)
+    )(conv_kernel, in_weight, conv_bias[:, None], norm_gain[:, None], norm_bias[:, None])
 
 
 class Sizes:
@@ -139,17 +163,31 @@
 
 
 def relay(size, src_ref, relaid_ref):
-    def one(i, carry):
-        at = size.line(i - HALO) + BASE - HALO
+    octets, groups, width, ch = size.octets, size.groups, size.width, size.ch
+    lines = size.rows + 2 * HALO
+    step = next(d for d in (6, 4, 3, 2, 1) if lines % d == 0)
+    shape = (groups * ch, groups * ch)
+    old = lax.broadcasted_iota(jnp.int32, shape, 0)
+    new = lax.broadcasted_iota(jnp.int32, shape, 1)
+    order = jnp.where(new == old % ch // width * ch + old // ch * width + old % width, 1.0, 0.0).astype(BF)
+
+    def one(q, carry):
+        cells = []
         for a in range(4):
-            parts = [
-                src_ref[pl.ds(at + 4 * a + j, size.octets, stride=OUTS), :].astype(BF) for j in range(size.groups)
-            ]
-            for gr, part in enumerate(regroup(parts, size.width)):
-                relaid_ref[gr, a, pl.ds(pl.multiple_of(i * size.octets, 16), size.octets), :] = part
+            for i in range(step):
+                at = size.line(q * step + i - HALO) + BASE - HALO + 4 * a
+                parts = [src_ref[pl.ds(at + j, octets, stride=OUTS), :].astype(BF) for j in range(groups)]
+                cells.append(jnp.concatenate(parts, axis=1))
+        moved = jnp.dot(jnp.concatenate(cells, axis=0), order, preferred_element_type=F32).astype(BF)
+        n = step * octets
+        for a in range(4):
+            for gr in range(groups):
+                relaid_ref[gr, a, pl.ds(pl.multiple_of(q * n, 16), n), :] = moved[
+                    a * n : (a + 1) * n, gr * ch : (gr + 1) * ch
+                ]
         return carry
 
-    lax.fori_loop(0, size.rows + 2 * HALO, one, 0)
+    lax.fori_loop(0, lines // step, one, 0)
 
 
 def conv(size, relaid_ref, w_ref, acc_ref):
@@ -217,22 +255,54 @@
     return (cen * lax.rsqrt(var + 1e-6) * gain_ref[b : b + 1, :] + nbias_ref[b : b + 1, :]).astype(BF)
 
 
-def mlp(b, params, parts):
-    inw_ref, inb_ref, outw_ref, outb_ref, scale_ref = params[3:]
-    n = parts[0].shape[0]
-    normed = jnp.concatenate([norm(b, params, part) for part in parts], axis=0)
-    tile = 48 if n % 48 == 0 else 64
+def project(b, params, normed, weight_ref, index):
+    inb_ref, outw_ref, outb_ref, scale_ref = params[4:8]
+    rows = normed.shape[0]
+    tile = 48 if rows % 48 == 0 else 64
     branch = None
-    half_hid = inw_ref.shape[2] // 2
+    half_hid = outw_ref.shape[1] // 2
     for c in range(0, 2 * half_hid, half_hid):
-        hid = jnp.dot(normed, inw_ref[b, :, c : c + half_hid], preferred_element_type=F32)
+        hid = jnp.dot(normed, weight_ref[index + (slice(None), slice(c, c + half_hid))], preferred_element_type=F32)
         bias = inb_ref[b : b + 1, c : c + half_hid]
-        act = [gelu_twice((hid[i : i + tile] + bias).astype(BF)) for i in range(0, hid.shape[0], tile)]
+        act = [gelu_twice((hid[i : i + tile] + bias).astype(BF)) for i in range(0, rows, tile)]
         part = jnp.dot(jnp.concatenate(act, axis=0), outw_ref[b, c : c + half_hid, :], preferred_element_type=F32)
         branch = part if branch is None else branch + part
     scale = scale_ref[b : b + 1, :]
-    branch = branch * (0.5 * scale) + outb_ref[b : b + 1, :] * scale
+    return branch * (0.5 * scale) + outb_ref[b : b + 1, :] * scale
+
+
+def mlp(b, params, parts):
+    n = parts[0].shape[0]
+    normed = jnp.concatenate([norm(b, params, part) for part in parts], axis=0)
+    branch = project(b, params, normed, params[3], (b,))
     return [branch[i * n : (i + 1) * n] for i in range(len(parts))]
+
+
+def block_sums(size, val):
+    ch = size.ch
+    row = lax.broadcasted_iota(jnp.int32, (2 * ch, ch), 0) % ch
+    col = lax.broadcasted_iota(jnp.int32, (2 * ch, ch), 1)
+    ones = jnp.where(row // size.width == col // size.width, 1.0, 0.0).astype(BF)
+    high = val.astype(BF)
+    low = (val - high.astype(F32)).astype(BF)
+    return jnp.dot(jnp.concatenate([high, low], axis=1), ones, preferred_element_type=F32)
+
+
+def norm_grouped(size, lines_ref, parts):
+    groups = size.groups
+    share = 1.0 / size.ch
+
+    def line(n, gr):
+        return lines_ref[0, n * groups + gr : n * groups + gr + 1, :]
+
+    vals = [part + line(0, gr) for gr, part in enumerate(parts)]
+    mean = block_sums(size, sum(vals[1:], vals[0])) * share
+    cens = [val - mean for val in vals]
+    squares = [cen * cen for cen in cens]
+    inv = lax.rsqrt(block_sums(size, sum(squares[1:], squares[0])) * share + 1e-6)
+    normed = [(cen * inv * line(1, gr) + line(2, gr)).astype(BF) for gr, cen in enumerate(cens)]
+    return jnp.concatenate(normed, axis=1)
+
 
 def rounded(val):
     return val.astype(BF).astype(F32)
@@ -244,7 +314,8 @@
 
 def inner(size, b, params, acc_ref, src_ref, dst_ref):
     rows, octets, groups, ch = size.rows, size.octets, size.groups, size.ch
-    step = next(d for d in (8, 6, 4, 3, 2, 1) if rows % d == 0)
+    spread_ref, lines_ref = params[8:]
+    step = next(d for d in (24, 16, 12, 8, 6, 4, 3, 2, 1) if rows % d == 0)
     n = step * octets
 
     def one(t, carry):
@@ -252,7 +323,9 @@
             parts = [
                 acc_ref[gr, pl.ds(pl.multiple_of(t * n, 16), n), half * ch : (half + 1) * ch] for gr in range(groups)
             ]
-            for j, branch in enumerate(mlp(b, params, regroup(parts, size.width))):
+            normed = norm_grouped(size, lines_ref, parts)
+            for j in range(groups):
+                branch = project(b, params, normed, spread_ref, (0, j))
                 for i in range(step):
                     at = size.line(t * step + i) + BASE + half * groups + j
                     spot = pl.ds(at, octets, stride=OUTS)
@@ -263,7 +336,7 @@
 
 
 def mlp0_kernel(size, acc_ref, x0_ref, k_ref, *refs):
-    params, (x1_ref, strip_ref) = refs[:8], refs[8:]
+    params, (x1_ref, strip_ref) = refs[:10], refs[10:]
     rows, cols, ch, pitch, wide0 = size.rows, size.cols, size.ch, size.pitch, size.wide0
     base, lead, near = BASE, BASE - REACH, BASE - HALO
     _, top, bottom = place()
@@ -319,7 +392,7 @@
 
 
 def mlp1_kernel(size, acc_ref, x1_ref, mask_ref, *refs):
-    params, (out_ref, x2_ref) = refs[:8], refs[8:]
+    params, (out_ref, x2_ref) = refs[:10], refs[10:]
     inner(size, 1, params, acc_ref, x1_ref, x2_ref)
 
     def finish(i, carry):
@@ -346,22 +419,22 @@
     left, right, got_a, got_b = exchange(fields, wet_mask)
     mask = jnp.broadcast_to(wet_mask.astype(BF)[:, :, None], fields.shape)
     state = fields * mask
-    taps = tap_matrices(conv_kernel)
-    groups, depth, lanes = taps.shape[1:]
+    taps, spread, lines = tap_matrices(conv_kernel, in_weight, conv_bias, norm_gain, norm_bias)
+    groups, depth, width = taps.shape[1:]
     hid = in_weight.shape[2]
     size = Sizes(rows, cols, ch)
     cells = rows * cols
     vmem = pl.BlockSpec(memory_space=pltpu.VMEM)
     relaid = pltpu.VMEM((groups, 4, (rows + 2 * HALO) * size.octets, ch), BF)
     padded = jax.ShapeDtypeStruct((size.lines, ch), F32)
-    sums = jax.ShapeDtypeStruct((groups, rows * size.octets, lanes), F32)
+    sums = jax.ShapeDtypeStruct((groups, rows * size.octets, width), F32)
 
     def call(kernel, ins, out_shape, scratch, flops):
         def spec(value):
-            if value is not taps:
+            if value is not taps and value is not spread and value is not lines:
                 return vmem
-            block = 0 if kernel is conv0_kernel else 1
-            return pl.BlockSpec((1, groups, depth, lanes), lambda i: (block, 0, 0, 0))
+            block = 0 if kernel in (conv0_kernel, mlp0_kernel) else 1
+            return pl.BlockSpec((1,) + value.shape[1:], lambda i: (block,) + (0,) * (value.ndim - 1))
 
         several = isinstance(out_shape, tuple)
         return pl.pallas_call(
@@ -378,7 +451,7 @@
 
     conv_flops = 2 * cells * ch * depth // OUTS * 2
     mlp_flops = 4 * cells * ch * hid
-    params = (conv_bias, norm_gain, norm_bias, in_weight, in_bias, out_weight, out_bias, layer_scale)
+    params = (conv_bias, norm_gain, norm_bias, in_weight, in_bias, out_weight, out_bias, layer_scale, spread, lines)
     x0, acc = call(
         conv0_kernel,
         (state, left, right, got_a, got_b, taps),

time: 89.6 us -> 69.2 us (0.77)
  Pallas kernels: 69.4 us -> 46.9 us
  local copies, waits for them, and re-layouts: 1.93 us -> 3.93 us
  other arithmetic: 4.28 us -> 5.45 us
  waiting for transfers between devices: 5.02 us -> 3.93 us
    pallas_call x4, Pallas kernels: 67.3 us -> 44.3 us  [call(): pl.pallas_call(functools.partial(kernel, size), grid=(1,), in_specs=[spec...]
    unnamed x19 -> x17, local copies, waits for them, and re-layouts: 0.86 us -> 2.86 us
    mul x1, other arithmetic: 0.98 us -> 2.11 us  [shards(): state = fields * mask]
    ppermute x1, waiting for transfers between devices: 5.01 us -> 3.93 us  [exchange(): lax.ppermute(jnp.where(even, first, last), ('lat', 'lon'), partners(nlat,...]
  transfers between devices with their start and end apart: 4 -> 4, of which waited for: 1 -> 1; matrix products, arithmetic and copies ran while one was open for 3% -> 6% of each run, Pallas kernels for 2% -> 4%
where the time goes in v7:
time: 69.2 us; the launch traced here: 68.9 us
  Pallas kernels  46.9 us (68%)
  starting transfers between devices  8.46 us (12%)
  other arithmetic  5.45 us (8%)
  local copies, waits for them, and re-layouts  3.93 us (6%)
  waiting for transfers between devices  3.93 us (6%)
    pallas_call x4, Pallas kernels, call(): pl.pallas_call(functools.partial(kernel, size), grid=(1,), in_specs=[spec...  44.3 us
    ppermute x1, waiting for transfers between devices, exchange(): lax.ppermute(jnp.where(even, first, last), ('lat', 'lon'), partners(nlat,...  3.93 us
    ppermute x1, starting transfers between devices, exchange(): lax.ppermute(jnp.where(even, first, last), ('lat', 'lon'), partners(nlat,...  3.17 us
    unnamed x17, local copies, waits for them, and re-layouts  2.86 us
    pallas_call x1, Pallas kernels, tap_matrices(): pl.pallas_call(tap_kernel, grid=(blocks, groups), in_specs=[pl.BlockSpec(...  2.66 us
    mul x2, other arithmetic, edge(): return fields[r0:r1, c0:c1] * wet_mask[r0:r1, c0:c1].astype(BF)[:, :, None]  2.4 us
    ppermute x1, starting transfers between devices, exchange(): left = lax.ppermute(edge(0, rows, cols - REACH, cols), 'lon', up)  2.18 us
    mul x1, other arithmetic, shards(): state = fields * mask  2.11 us
  transfers between devices with their start and end apart: 4, of which 1 were waited for; matrix products, arithmetic and copies ran while one was open for 6% of the time, Pallas kernels for 4%

profile of v7, /device:TPU:1, one launch (start us, length us, event | category | flops | bytes accessed | tf_op | source)
XLA Modules:
  0.0 68.9 jit_solution(12250444693555379217)
XLA Ops:
  0.0 0.0 copy-start
  0.0 0.8 %convert_element_type.2 = bf16[48,128]{1,0:T(8,128)(2,1)S(1)} convert(s32[48,128]{1,0:T(8,128)} %param.12) | non-fusion elementwise | flops 6144 | bytes 36864 | tf_op jit(solution)/shard_map/convert_element_type | solution.py:420
  0.8 0.1 fusion.3
  0.9 1.1 %slice_multiply_fusion.2 = (bf16[48,6,128]{2,1,0:T(8,128)(2,1)S(1)}, bf16[48,6,128]{2,1,0:T(8,128)(2,1)S(1)}) fusion(bf16[48,128,128]{2,1,0:T(8,128)(2,1)} %param.11, bf16[48,6]{1,0:T(8,128)(2,1)S(1)} %get-tuple-element.27, bf16[48,6]{1,0:T(8,128)(2,1)S(1)} %get-tuple-element.28), kind=kLoop, calls=%fused_computation.7 | loop fusion | flops 73728 | bytes 296064 | tf_op jit(solution)/shard_map/mul | solution.py:42
  2.0 2.2 %collective-permute-start = (bf16[48,6,128]{2,1,0:T(8,128)(2,1)S(1)}, bf16[48,6,128]{2,1,0:T(8,128)(2,1)S(1)}, u32[]{:S(2)}, u32[]{:S(2)}) collective-permute-start(bf16[48,6,128]{2,1,0:T(8,128)(2,1)S(1)} %get-tuple-element.18), channel_id=1, source_target_pairs={{0,1},{1,2},{2,3},{3,0},{4,5},{5,6},{6,7},{7,4},{8,9},{9,10},{10,1... | collective-permute-start | bytes 221192 | tf_op jit(solution)/shard_map/ppermute | solution.py:46
  4.2 2.1 %collective-permute-start.1 = (bf16[48,6,128]{2,1,0:T(8,128)(2,1)S(1)}, bf16[48,6,128]{2,1,0:T(8,128)(2,1)S(1)}, u32[]{:S(2)}, u32[]{:S(2)}) collective-permute-start(bf16[48,6,128]{2,1,0:T(8,128)(2,1)S(1)} %get-tuple-element.17), channel_id=1, source_target_pairs={{1,0},{2,1},{3,2},{0,3},{5,4},{6,5},{7,6},{4,7},{9,8},{10,9},{11,1... | collective-permute-start | bytes 221192 | tf_op jit(solution)/shard_map/ppermute | solution.py:47
  6.3 1.3 %slice_multiply_fusion.1 = (bf16[6,128,128]{2,1,0:T(8,128)(2,1)S(1)}, bf16[6,128,128]{2,1,0:T(8,128)(2,1)S(1)}) fusion(bf16[48,128,128]{2,1,0:T(8,128)(2,1)} %param.11, bf16[6,128]{1,0:T(8,128)(2,1)S(1)} %get-tuple-element.25, bf16[6,128]{1,0:T(8,128)(2,1)S(1)} %get-tuple-element.26), kind=kLoop, calls=%fused_computation.6 | loop fusion | flops 196608 | bytes 789504 | tf_op jit(solution)/shard_map/mul | solution.py:42
  7.6 0.8 %copy.12.k_ref = f32[2,49,128]{2,1,0:T(8,128)S(1)} copy(f32[2,49,128]{2,0,1:T(2,128)} %param.13) | data formatting | bytes 100352 | tf_op args[2]
  8.4 0.0 copy-done
  8.4 0.0 copy-start.3
  8.4 0.7 copy-done.3
  9.1 0.0 copy-start.4
  9.1 0.7 copy-done.4
  9.7 0.7 copy-done.5
  10.4 2.7 %tap_matrices.1 = (bf16[2,4,3584,256]{3,2,1,0:T(8,128)(2,1)S(1)}, bf16[2,4,512,512]{3,2,1,0:T(8,128)(2,1)S(1)}, f32[2,12,128]{2,1,0:T(8,128)S(1)}) custom-call(f32[2,49,128]{2,1,0:T(8,128)S(1)} %copy.12.k_ref, bf16[2,128,512]{2,1,0:T(8,128)(2,1)S(1)} %copy-done, f32[2,1,128]{2,1,0:T(1,128)S(1)} %bitcast.3, f32[2,1,128]{2,1,0:T(1,128)S(1)} %bitcast.4, ...), custom_call_target="tpu_custom_call" | custom-call | bytes 14680064 | tf_op jit(solution)/shard_map/tap_matrices/pallas_call | solution.py:119
  13.1 0.0 collective-permute-done.left_ref
  13.1 0.0 collective-permute-done.1.right_ref
  13.1 0.2 broadcast_select_fusion
  13.3 1.0 %collective-permute-start.2 = (bf16[6,140,128]{2,1,0:T(8,128)(2,1)S(1)}, bf16[6,140,128]{2,1,0:T(8,128)(2,1)S(1)}, u32[]{:S(2)}, u32[]{:S(2)}) collective-permute-start(bf16[6,140,128]{2,1,0:T(8,128)(2,1)S(1)} %get-tuple-element.20), channel_id=1, source_target_pairs={{0,4},{1,5},{2,6},{3,7},{4,0},{5,1},{6,2},{7,3},{8,12},{9,13},{10,... | collective-permute-start | bytes 645128 | tf_op jit(solution)/shard_map/ppermute | solution.py:51
  14.3 3.2 %collective-permute-start.3 = (bf16[6,140,128]{2,1,0:T(8,128)(2,1)S(1)}, bf16[6,140,128]{2,1,0:T(8,128)(2,1)S(1)}, u32[]{:S(2)}, u32[]{:S(2)}) collective-permute-start(bf16[6,140,128]{2,1,0:T(8,128)(2,1)S(1)} %get-tuple-element.19), channel_id=1, source_target_pairs={{4,8},{5,9},{6,10},{7,11},{8,4},{9,5},{10,6},{11,7},{12,16},{13,17... | collective-permute-start | bytes 645128 | tf_op jit(solution)/shard_map/ppermute | solution.py:52
  17.5 2.1 %broadcast_multiply_fusion.x_ref = bf16[48,128,128]{2,1,0:T(8,128)(2,1)S(1)} fusion(bf16[48,128,128]{2,1,0:T(8,128)(2,1)} %param.11, bf16[48,128]{1,0:T(8,128)(2,1)S(1)} %convert_element_type.2), kind=kLoop, calls=%fused_computation | loop fusion | flops 786432 | bytes 3158016 | tf_op jit(solution)/shard_map/mul | solution.py:421
  19.6 0.0 collective-permute-done.2.a_ref
  19.6 3.9 %collective-permute-done.3.b_ref = bf16[6,140,128]{2,1,0:T(8,128)(2,1)S(1)} collective-permute-done((bf16[6,140,128]{2,1,0:T(8,128)(2,1)S(1)}, bf16[6,140,128]{2,1,0:T(8,128)(2,1)S(1)}, u32[]{:S(2)}, u32[]{:S(2)}) %collective-permute-start.3) | collective-permute-done | bytes 215072 | tf_op jit(solution)/shard_map/ppermute | solution.py:52
  23.6 10.3 %conv0_kernel.1 = (f32[9120,128]{1,0:T(8,128)S(1)}, f32[4,768,256]{2,1,0:T(8,128)S(1)}) custom-call(bf16[48,128,128]{2,1,0:T(8,128)(2,1)S(1)} %broadcast_multiply_fusion.x_ref, bf16[48,6,128]{2,1,0:T(8,128)(2,1)S(1)} %collective-permute-done.left_ref, bf16[48,6,128]{2,1,0:T(8,128)(2,1)S(1)} %collective-permute-done.1.right_ref, ...), custom_call_target="tpu_custom_call" | custom-call | flops 1409286144 | bytes 4718592 | tf_op jit(solution)/shard_map/conv0_kernel/pallas_call | solution.py:440
  33.8 0.0 copy-done.1
  33.9 0.0 copy-done.2
  33.9 0.0 copy-done.6
  33.9 0.0 copy-done.7
  33.9 14.0 %mlp0_kernel.1.x1_ref = f32[9120,128]{1,0:T(8,128)S(1)} custom-call(f32[4,768,256]{2,1,0:T(8,128)S(1)} %get-tuple-element.11.acc_ref, f32[9120,128]{1,0:T(8,128)S(1)} %get-tuple-element.12.x0_ref, f32[2,49,128]{2,1,0:T(8,128)S(1)} %copy.12.k_ref, f32[2,128]{1,0:T(2,128)S(1)} %copy-done.3, f32[2,128]{1,0:T(2,128)S(1)} %copy-done.4, f32[2,128]{1,0:T(2,128)S(1)} %copy-done.5, ...), custom_call_target="tpu_custom_call" | custom-call | flops 1610612736 | bytes 4718592 | tf_op jit(solution)/shard_map/mlp0_kernel/pallas_call | solution.py:440
  47.9 9.6 %conv1_kernel.1.acc_ref = f32[4,768,256]{2,1,0:T(8,128)S(1)} custom-call(f32[9120,128]{1,0:T(8,128)S(1)} %mlp0_kernel.1.x1_ref, bf16[2,4,3584,256]{3,2,1,0:T(8,128)(2,1)S(1)} %get-tuple-element.10.w_ref), custom_call_target="tpu_custom_call" | custom-call | flops 1409286144 | bytes 4718592 | tf_op jit(solution)/shard_map/conv1_kernel/pallas_call | solution.py:440
  57.4 1.0 %broadcast_in_dim.8.mask_ref = bf16[48,128,128]{2,1,0:T(8,128)(2,1)S(1)} broadcast(bf16[48,128]{1,0:T(8,128)(2,1)S(1)} %convert_element_type.2), dimensions={0,1} | broadcast | bytes 1585152 | tf_op jit(solution)/shard_map/broadcast_in_dim | solution.py:420
  58.4 10.4 %mlp1_kernel.1 = bf16[48,128,128]{2,1,0:T(8,128)(2,1)} custom-call(f32[4,768,256]{2,1,0:T(8,128)S(1)} %conv1_kernel.1.acc_ref, f32[9120,128]{1,0:T(8,128)S(1)} %mlp0_kernel.1.x1_ref, bf16[48,128,128]{2,1,0:T(8,128)(2,1)S(1)} %broadcast_in_dim.8.mask_ref, f32[2,128]{1,0:T(2,128)S(1)} %copy-done.3, f32[2,128]{1,0:T(2,128)S(1)} %copy-done.4, ...), custom_call_target="tpu_custom_call" | custom-call | flops 1610612736 | bytes 4718592 | tf_op jit(solution)/shard_map/mlp1_kernel/pallas_call | solution.py:440
  (8 shorter events, 0.0 us)
Async XLA Ops:
  0.0 8.4 %copy-start = (bf16[2,128,512]{2,1,0:T(8,128)(2,1)S(1)}, bf16[2,128,512]{2,1,0:T(8,128)(2,1)}, u32[]{:S(2)}) copy-start(bf16[2,128,512]{2,1,0:T(8,128)(2,1)} %refs_3_.3) | copy-start | bytes 786436
  2.0 11.1 %collective-permute-start = (bf16[48,6,128]{2,1,0:T(8,128)(2,1)S(1)}, bf16[48,6,128]{2,1,0:T(8,128)(2,1)S(1)}, u32[]{:S(2)}, u32[]{:S(2)}) collective-permute-start(bf16[48,6,128]{2,1,0:T(8,128)(2,1)S(1)} %get-tuple-element.18), channel_id=1, source_target_pairs={{0,1},{1,2},{2,3},{3,0},{4,5},{5,6},{6,7},{7,4},{8,9},{9,10},{10,1... | collective-permute-start | bytes 221192 | tf_op jit(solution)/shard_map/ppermute | solution.py:46
  4.2 8.9 %collective-permute-start.1 = (bf16[48,6,128]{2,1,0:T(8,128)(2,1)S(1)}, bf16[48,6,128]{2,1,0:T(8,128)(2,1)S(1)}, u32[]{:S(2)}, u32[]{:S(2)}) collective-permute-start(bf16[48,6,128]{2,1,0:T(8,128)(2,1)S(1)} %get-tuple-element.17), channel_id=1, source_target_pairs={{1,0},{2,1},{3,2},{0,3},{5,4},{6,5},{7,6},{4,7},{9,8},{10,9},{11,1... | collective-permute-start | bytes 221192 | tf_op jit(solution)/shard_map/ppermute | solution.py:47
  8.4 0.7 copy-start.3
  9.1 0.7 copy-start.4
  9.7 0.7 copy-start.5
  13.3 6.3 %collective-permute-start.2 = (bf16[6,140,128]{2,1,0:T(8,128)(2,1)S(1)}, bf16[6,140,128]{2,1,0:T(8,128)(2,1)S(1)}, u32[]{:S(2)}, u32[]{:S(2)}) collective-permute-start(bf16[6,140,128]{2,1,0:T(8,128)(2,1)S(1)} %get-tuple-element.20), channel_id=1, source_target_pairs={{0,4},{1,5},{2,6},{3,7},{4,0},{5,1},{6,2},{7,3},{8,12},{9,13},{10,... | collective-permute-start | bytes 645128 | tf_op jit(solution)/shard_map/ppermute | solution.py:51
  14.3 9.2 %collective-permute-start.3 = (bf16[6,140,128]{2,1,0:T(8,128)(2,1)S(1)}, bf16[6,140,128]{2,1,0:T(8,128)(2,1)S(1)}, u32[]{:S(2)}, u32[]{:S(2)}) collective-permute-start(bf16[6,140,128]{2,1,0:T(8,128)(2,1)S(1)} %get-tuple-element.19), channel_id=1, source_target_pairs={{4,8},{5,9},{6,10},{7,11},{8,4},{9,5},{10,6},{11,7},{12,16},{13,17... | collective-permute-start | bytes 645128 | tf_op jit(solution)/shard_map/ppermute | solution.py:52
  23.6 10.3 %copy-start.1 = (bf16[2,512,128]{2,1,0:T(8,128)(2,1)S(1)}, bf16[2,512,128]{2,1,0:T(8,128)(2,1)}, u32[]{:S(2)}) copy-start(bf16[2,512,128]{2,1,0:T(8,128)(2,1)} %refs_5_.3) | copy-start | bytes 786436
  23.6 10.3 %copy-start.2 = (f32[2,512]{1,0:T(2,128)S(1)}, f32[2,512]{1,0:T(2,128)}, u32[]{:S(2)}) copy-start(f32[2,512]{1,0:T(2,128)} %refs_4_.3) | copy-start | bytes 12292
  23.6 10.3 %copy-start.6 = (f32[2,128]{1,0:T(2,128)S(1)}, f32[2,128]{1,0:T(2,128)}, u32[]{:S(2)}) copy-start(f32[2,128]{1,0:T(2,128)} %refs_6_.3) | copy-start | bytes 3076
  23.6 10.3 %copy-start.7 = (f32[2,128]{1,0:T(2,128)S(1)}, f32[2,128]{1,0:T(2,128)}, u32[]{:S(2)}) copy-start(f32[2,128]{1,0:T(2,128)} %refs_7_.3) | copy-start | bytes 3076

commit v8 on v7

--- a/solution.py
+++ b/solution.py
@@ -83,7 +83,7 @@
             for g in range(groups):
                 line = jnp.zeros((1, ch), F32)
                 for j in range(groups):
-                    line = jnp.where(block == j, pltpu.roll(ref[0], (j - g) * width % ch, 1), line)
+                    line = jnp.where(block == j, pltpu.roll(ref[pl.ds(pl.program_id(0), 1), :], (j - g) * width % ch, 1), line)
                 lines_ref[0, n * groups + g : n * groups + g + 1, :] = line
         down = [k_ref[0, pl.ds(s, TAPS, stride=TAPS), :] for s in range(TAPS - 1, -1, -1)]
         down.append(jnp.zeros((TAPS, ch), F32))
@@ -123,7 +123,7 @@
             pl.BlockSpec((1, taps, ch), lambda b, g: (b, 0, 0)),
             pl.BlockSpec((1, width, hid), lambda b, g: (b, g, 0)),
         ]
-        + [pl.BlockSpec((1, 1, ch), lambda b, g: (b, 0, 0))] * 3,
+        + [pl.BlockSpec((blocks, ch), lambda b, g: (0, 0))] * 3,
         out_specs=(
             pl.BlockSpec((1, 1, depth, lanes), lambda b, g: (b, g, 0, 0)),
             pl.BlockSpec((1, groups, ch, hid), lambda b, g: (b, 0, g, 0)),
@@ -140,7 +140,7 @@
             flops=0, bytes_accessed=2 * blocks * groups * depth * lanes, transcendentals=0
         ),
         name="tap_matrices",
-    )(conv_kernel, in_weight, conv_bias[:, None], norm_gain[:, None], norm_bias[:, None])
+    )(conv_kernel, in_weight, conv_bias, norm_gain, norm_bias)
 
 
 class Sizes:
@@ -190,7 +190,7 @@
     lax.fori_loop(0, lines // step, one, 0)
 
 
-def conv(size, relaid_ref, w_ref, acc_ref):
+def conv(size, relaid_ref, w_ref, acc_ref, beside=()):
     octets, rows = size.octets, size.rows
 
     for gr in range(size.groups):
@@ -199,9 +199,46 @@
             for a in range(4):
                 parts.append(relaid_ref[gr, a, r * octets : (r + rows) * octets, :])
         acc_ref[gr] = jnp.dot(jnp.concatenate(parts, axis=1), w_ref[0, gr], preferred_element_type=F32)
-
-
-def conv0_kernel(size, x_ref, left_ref, right_ref, a_ref, b_ref, w_ref, x0_ref, acc_ref, relaid_ref, flip_ref):
+        for work in beside[gr :: size.groups]:
+            work()
+
+
+def column_strip(size, start, x0_ref, k_ref, strip_ref):
+    rows, pitch = size.rows, size.pitch
+    sums = [jnp.zeros((rows, size.ch), F32) for _ in range(HALO)]
+    for r in range(TAPS):
+        for c in range(TAPS + HALO - 1):
+            at = (REACH - HALO + r) * pitch + BASE + start - HALO + c
+            cells = x0_ref[pl.ds(at, rows, stride=pitch), :]
+            for i in range(HALO):
+                if 0 <= c - i < TAPS:
+                    tap = TAPS * r + c - i
+                    sums[i] = sums[i] + cells * k_ref[0, tap : tap + 1, :]
+    for i in range(HALO):
+        strip_ref[i] = sums[i]
+
+
+def row_strip(size, side, c, piece, top, x0_ref, k_ref, strip_ref):
+    pitch, lead = size.pitch, BASE - REACH
+    first = (0 if side == 0 else size.rows + HALO) * pitch
+    sums = [jnp.zeros((piece, size.ch), F32) for _ in range(HALO)]
+    for s in range(TAPS):
+        at = first + lead + s + c
+        lines = [x0_ref[at + i * pitch : at + i * pitch + piece, :] for i in range(TAPS + HALO - 1)]
+        for r in range(TAPS):
+            tap = TAPS * r + s
+            if side == 1:
+                tap = jnp.where(top, TAPS * TAPS - 1 - tap, tap)
+            weight = k_ref[0, pl.ds(tap, 1), :]
+            for i in range(HALO):
+                sums[i] = sums[i] + lines[i + r] * weight
+    for i in range(HALO):
+        strip_ref[side * HALO + i, c : c + piece, :] = sums[i]
+
+
+def conv0_kernel(size, *refs):
+    x_ref, mask_ref, left_ref, right_ref, a_ref, b_ref, w_ref, k_ref = refs[:8]
+    x0_ref, acc_ref, row_ref, col_ref, relaid_ref, flip_ref = refs[8:]
     rows, cols, ch, pitch, wide0 = size.rows, size.cols, size.ch, size.pitch, size.wide0
     base, ext, lead = BASE, cols + 2 * REACH, BASE - REACH
     line = size.line
@@ -211,7 +248,7 @@
         at = line(i)
         x0_ref[pl.ds(at, base), :] = jnp.zeros((base, ch), F32)
         x0_ref[pl.ds(at + lead, REACH), :] = left_ref[i].astype(F32)
-        x0_ref[pl.ds(at + base, cols), :] = x_ref[i].astype(F32)
+        x0_ref[pl.ds(at + base, cols), :] = (x_ref[i] * mask_ref[i]).astype(F32)
         x0_ref[pl.ds(at + base + cols, 16), :] = jnp.zeros((16, ch), F32)
         x0_ref[pl.ds(at + base + cols, REACH), :] = right_ref[i].astype(F32)
         return carry
@@ -231,7 +268,13 @@
         x0_ref[north : north + pitch, :] = jnp.zeros((pitch, ch), F32)
         x0_ref[north + lead : north + lead + wide0, :] = turned
     relay(size, x0_ref, relaid_ref)
-    conv(size, relaid_ref, w_ref, acc_ref)
+    piece = wide0 // 3
+    beside = [functools.partial(column_strip, size, -HALO, x0_ref, k_ref, col_ref.at[0])]
+    beside.append(functools.partial(column_strip, size, cols, x0_ref, k_ref, col_ref.at[1]))
+    for side in range(2):
+        for c in range(0, wide0, piece):
+            beside.append(functools.partial(row_strip, size, side, c, piece, top, x0_ref, k_ref, row_ref))
+    conv(size, relaid_ref, w_ref, acc_ref, beside)
 
 
 def conv1_kernel(size, x1_ref, w_ref, acc_ref, relaid_ref):
@@ -335,11 +378,11 @@
     lax.fori_loop(0, rows // step, one, 0)
 
 
-def mlp0_kernel(size, acc_ref, x0_ref, k_ref, *refs):
-    params, (x1_ref, strip_ref) = refs[:10], refs[10:]
+def mlp0_kernel(size, acc_ref, x0_ref, row_ref, col_ref, *refs):
+    params, x1_ref = refs[:10], refs[10]
     rows, cols, ch, pitch, wide0 = size.rows, size.cols, size.ch, size.pitch, size.wide0
-    base, lead, near = BASE, BASE - REACH, BASE - HALO
-    _, top, bottom = place()
+    base, near = BASE, BASE - HALO
+    _, _, bottom = place()
 
     def clear(i, carry):
         at = size.line(i)
@@ -349,39 +392,12 @@
 
     lax.fori_loop(0, rows, clear, 0)
     inner(size, 0, params, acc_ref, x0_ref, x1_ref)
+    for side, start in enumerate((-HALO, cols)):
+        for i, branch in enumerate(mlp(0, params, [col_ref[side, i] for i in range(HALO)])):
+            spot = pl.ds(REACH * pitch + BASE + start + i, rows, stride=pitch)
+            x1_ref[spot, :] = rounded(x0_ref[spot, :] + branch)
     for side in range(2):
-        first = lead if side == 0 else base + cols - HALO
-        sums = [jnp.zeros((rows, ch), F32) for _ in range(HALO)]
-        for r in range(TAPS):
-            for c in range(TAPS + HALO - 1):
-                cells = x0_ref[pl.ds((REACH - HALO + r) * pitch + first + c, rows, stride=pitch), :]
-                for i in range(HALO):
-                    if 0 <= c - i < TAPS:
-                        tap = TAPS * r + c - i
-                        sums[i] = sums[i] + cells * k_ref[0, tap : tap + 1, :]
-        start = near if side == 0 else base + cols
-        for i, branch in enumerate(mlp(0, params, sums)):
-            spot = pl.ds(REACH * pitch + start + i, rows, stride=pitch)
-            x1_ref[spot, :] = rounded(x0_ref[spot, :] + branch)
-    piece = wide0 // 3
-    for side in range(2):
-        first = (0 if side == 0 else rows + HALO) * pitch
-        for c in range(0, wide0, piece):
-            sums = [jnp.zeros((piece, ch), F32) for _ in range(HALO)]
-            for s in range(TAPS):
-                at = first + lead + s + c
-                lines = [x0_ref[at + i * pitch : at + i * pitch + piece, :] for i in range(TAPS + HALO - 1)]
-                for r in range(TAPS):
-                    tap = TAPS * r + s
-                    if side == 1:
-                        tap = jnp.where(top, TAPS * TAPS - 1 - tap, tap)
-                    weight = k_ref[0, pl.ds(tap, 1), :]
-                    for i in range(HALO):
-                        sums[i] = sums[i] + lines[i + r] * weight
-            for i in range(HALO):
-                strip_ref[side * HALO + i, c : c + piece, :] = sums[i]
-    for side in range(2):
-        branches = mlp(0, params, [strip_ref[side * HALO + i] for i in range(HALO)])
+        branches = mlp(0, params, [row_ref[side * HALO + i] for i in range(HALO)])
         for i, branch in enumerate(branches):
             row = i - HALO if side == 0 else rows + i
             at = (row + REACH) * pitch + near
@@ -417,8 +433,8 @@
 ):
     rows, cols, ch = fields.shape
     left, right, got_a, got_b = exchange(fields, wet_mask)
-    mask = jnp.broadcast_to(wet_mask.astype(BF)[:, :, None], fields.shape)
-    state = fields * mask
+    conv_kernel, whole_mask, left, right = lax.optimization_barrier((conv_kernel, wet_mask, left, right))
+    mask = jnp.broadcast_to(whole_mask.astype(BF)[:, :, None], fields.shape)
     taps, spread, lines = tap_matrices(conv_kernel, in_weight, conv_bias, norm_gain, norm_bias)
     groups, depth, width = taps.shape[1:]
     hid = in_weight.shape[2]
@@ -452,15 +468,16 @@
     conv_flops = 2 * cells * ch * depth // OUTS * 2
     mlp_flops = 4 * cells * ch * hid
     params = (conv_bias, norm_gain, norm_bias, in_weight, in_bias, out_weight, out_bias, layer_scale, spread, lines)
-    x0, acc = call(
+    row_strips = jax.ShapeDtypeStruct((2 * HALO, size.wide0, ch), F32)
+    col_strips = jax.ShapeDtypeStruct((2, HALO, rows, ch), F32)
+    x0, acc, row_sums, col_sums = call(
         conv0_kernel,
-        (state, left, right, got_a, got_b, taps),
-        (padded, sums),
+        (fields, mask, left, right, got_a, got_b, taps, conv_kernel),
+        (padded, sums, row_strips, col_strips),
         [relaid, pltpu.VMEM((cols + 24, ch), F32)],
         conv_flops,
     )
-    strips = pltpu.VMEM((2 * HALO, cols + 16, ch), F32)
-    x1 = call(mlp0_kernel, (acc, x0, conv_kernel) + params, padded, [strips], mlp_flops)
+    x1 = call(mlp0_kernel, (acc, x0, row_sums, col_sums) + params, padded, [], mlp_flops)
     acc = call(conv1_kernel, (x1, taps), sums, [relaid], conv_flops)
     whole = pltpu.VMEM((size.lines, ch), F32)
     return call(mlp1_kernel, (acc, x1, mask) + params, jax.ShapeDtypeStruct(fields.shape, BF), [whole], mlp_flops)

time: 69.2 us -> 68.3 us (0.987)
  Pallas kernels: 46.9 us -> 44.9 us
  other arithmetic: 5.45 us -> 4.16 us
  local copies, waits for them, and re-layouts: 3.93 us -> 4.91 us
  starting transfers between devices: 8.46 us -> 9.39 us
    ppermute x1, waiting for transfers between devices: 3.93 us -> 0.01 us  [exchange(): lax.ppermute(jnp.where(even, first, last), ('lat', 'lon'), partners(nlat,...]
    ppermute x1, waiting for transfers between devices: 0.01 us -> 3.62 us  [exchange(): left = lax.ppermute(edge(0, rows, cols - REACH, cols), 'lon', up)]
    ppermute x1, starting transfers between devices: 2.18 us -> 0.01 us  [exchange(): left = lax.ppermute(edge(0, rows, cols - REACH, cols), 'lon', up)]
    ppermute x1, starting transfers between devices: 2.09 us -> 4.2 us  [exchange(): right = lax.ppermute(edge(0, rows, 0, REACH), 'lon', down)]
    mul x1 -> x0, other arithmetic: 2.11 us -> none  [shards(): state = fields * mask]
    pallas_call x4, Pallas kernels: 44.3 us -> 42.2 us  [call(): pl.pallas_call(functools.partial(kernel, size), grid=(1,), in_specs=[spec...]
    ppermute x1, starting transfers between devices: 3.17 us -> 5.11 us  [exchange(): lax.ppermute(jnp.where(even, first, last), ('lat', 'lon'), partners(nlat,...]
    ppermute x1, starting transfers between devices: 1.02 us -> 0.07 us  [exchange(): lax.ppermute(jnp.where(even, last, first), ('lat', 'lon'), partners(nlat,...]
  transfers between devices with their start and end apart: 4 -> 4, of which waited for: 1 -> 2; matrix products, arithmetic and copies ran while one was open for 6% -> 4% of each run, Pallas kernels for 4% -> 4%
where the time goes in v8:
time: 68.3 us; the launch traced here: 67.5 us
  Pallas kernels  44.9 us (66%)
  starting transfers between devices  9.39 us (14%)
  local copies, waits for them, and re-layouts  4.91 us (7%)
  other arithmetic  4.16 us (6%)
  waiting for transfers between devices  3.95 us (6%)
    pallas_call x4, Pallas kernels, call(): pl.pallas_call(functools.partial(kernel, size), grid=(1,), in_specs=[spec...  42.2 us
    ppermute x1, starting transfers between devices, exchange(): lax.ppermute(jnp.where(even, first, last), ('lat', 'lon'), partners(nlat,...  5.11 us
    ppermute x1, starting transfers between devices, exchange(): right = lax.ppermute(edge(0, rows, 0, REACH), 'lon', down)  4.2 us
    ppermute x1, waiting for transfers between devices, exchange(): left = lax.ppermute(edge(0, rows, cols - REACH, cols), 'lon', up)  3.62 us
    unnamed x26, local copies, waits for them, and re-layouts  3.04 us
    pallas_call x1, Pallas kernels, tap_matrices(): pl.pallas_call(tap_kernel, grid=(blocks, groups), in_specs=[pl.BlockSpec(...  2.7 us
    mul x2, other arithmetic, edge(): return fields[r0:r1, c0:c1] * wet_mask[r0:r1, c0:c1].astype(BF)[:, :, None]  2.4 us
  transfers between devices with their start and end apart: 4, of which 2 were waited for; matrix products, arithmetic and copies ran while one was open for 4% of the time, Pallas kernels for 4%

profile of v8, /device:TPU:1, one launch (start us, length us, event | category | flops | bytes accessed | tf_op | source)
XLA Modules:
  0.0 67.5 jit_solution(8687512826755978527)
XLA Ops:
  0.0 0.9 %convert.6 = bf16[48,128]{1,0:T(8,128)(2,1)S(1)} convert(s32[48,128]{1,0:T(8,128)} %param.12) | non-fusion elementwise | flops 6144 | bytes 36864 | tf_op jit(solution)/shard_map/convert.3
  0.9 0.1 fusion.3
  0.9 1.1 %slice_multiply_fusion.2 = (bf16[48,6,128]{2,1,0:T(8,128)(2,1)S(1)}, bf16[48,6,128]{2,1,0:T(8,128)(2,1)S(1)}) fusion(bf16[48,128,128]{2,1,0:T(8,128)(2,1)} %refs_0_.3, bf16[48,6]{1,0:T(8,128)(2,1)S(1)} %get-tuple-element.39, bf16[48,6]{1,0:T(8,128)(2,1)S(1)} %get-tuple-element.40), kind=kLoop, calls=%fused_computation.6 | loop fusion | flops 73728 | bytes 296064 | tf_op jit(solution)/shard_map/mul | solution.py:42
  2.1 4.2 %collective-permute-start.1 = (bf16[48,6,128]{2,1,0:T(8,128)(2,1)S(1)}, bf16[48,6,128]{2,1,0:T(8,128)(2,1)S(1)}, u32[]{:S(2)}, u32[]{:S(2)}) collective-permute-start(bf16[48,6,128]{2,1,0:T(8,128)(2,1)S(1)} %get-tuple-element.29), channel_id=1, source_target_pairs={{1,0},{2,1},{3,2},{0,3},{5,4},{6,5},{7,6},{4,7},{9,8},{10,9},{11,1... | collective-permute-start | bytes 221192 | tf_op jit(solution)/shard_map/ppermute | solution.py:47
  6.3 0.0 collective-permute-start
  6.3 1.3 %slice_multiply_fusion.1 = (bf16[6,128,128]{2,1,0:T(8,128)(2,1)S(1)}, bf16[6,128,128]{2,1,0:T(8,128)(2,1)S(1)}) fusion(bf16[48,128,128]{2,1,0:T(8,128)(2,1)} %refs_0_.3, bf16[6,128]{1,0:T(8,128)(2,1)S(1)} %get-tuple-element.37, bf16[6,128]{1,0:T(8,128)(2,1)S(1)} %get-tuple-element.38), kind=kLoop, calls=%fused_computation.5 | loop fusion | flops 196608 | bytes 789504 | tf_op jit(solution)/shard_map/mul | solution.py:42
  7.6 0.3 collective-permute-done.1.refs_3_
  7.9 3.6 %collective-permute-done.refs_2_ = bf16[48,6,128]{2,1,0:T(8,128)(2,1)S(1)} collective-permute-done((bf16[48,6,128]{2,1,0:T(8,128)(2,1)S(1)}, bf16[48,6,128]{2,1,0:T(8,128)(2,1)S(1)}, u32[]{:S(2)}, u32[]{:S(2)}) %collective-permute-start) | collective-permute-done | bytes 73760 | tf_op jit(solution)/shard_map/ppermute | solution.py:46
  11.5 0.2 broadcast_select_fusion
  11.7 5.1 %collective-permute-start.3 = (bf16[6,140,128]{2,1,0:T(8,128)(2,1)S(1)}, bf16[6,140,128]{2,1,0:T(8,128)(2,1)S(1)}, u32[]{:S(2)}, u32[]{:S(2)}) collective-permute-start(bf16[6,140,128]{2,1,0:T(8,128)(2,1)S(1)} %get-tuple-element.31), channel_id=1, source_target_pairs={{4,8},{5,9},{6,10},{7,11},{8,4},{9,5},{10,6},{11,7},{12,16},{13,17... | collective-permute-start | bytes 645128 | tf_op jit(solution)/shard_map/ppermute | solution.py:52
  16.8 0.1 collective-permute-start.2
  16.9 0.7 %convert_element_type.2 = bf16[48,128]{1,0:T(8,128)(2,1)S(1)} convert(s32[48,128]{1,0:T(8,128)} %param.12) | non-fusion elementwise | flops 6144 | bytes 36864 | tf_op jit(solution)/shard_map/convert_element_type | solution.py:437
  17.6 0.8 %copy.12.k_ref.refs_7_ = f32[2,49,128]{2,1,0:T(8,128)S(1)} copy(f32[2,49,128]{2,0,1:T(2,128)} %param.13) | data formatting | bytes 100352 | tf_op jit(solution)/shard_map/optimization_barrier | solution.py:436
  18.4 0.9 %copy-done.1 = bf16[2,128,512]{2,1,0:T(8,128)(2,1)S(1)} copy-done((bf16[2,128,512]{2,1,0:T(8,128)(2,1)S(1)}, bf16[2,128,512]{2,1,0:T(8,128)(2,1)}, u32[]{:S(2)}) %copy-start.1) | copy-done | bytes 262168
  19.4 0.7 %copy-done.5 = f32[2,128]{1,0:T(2,128)S(1)} copy-done((f32[2,128]{1,0:T(2,128)S(1)}, f32[2,128]{1,0:T(2,128)}, u32[]{:S(2)}) %copy-start.5) | copy-done | bytes 1048
  20.1 0.7 %copy-done.7 = f32[2,128]{1,0:T(2,128)S(1)} copy-done((f32[2,128]{1,0:T(2,128)S(1)}, f32[2,128]{1,0:T(2,128)}, u32[]{:S(2)}) %copy-start.7) | copy-done | bytes 1048
  20.8 0.7 %copy-done.9 = f32[2,128]{1,0:T(2,128)S(1)} copy-done((f32[2,128]{1,0:T(2,128)S(1)}, f32[2,128]{1,0:T(2,128)}, u32[]{:S(2)}) %copy-start.9) | copy-done | bytes 1048
  21.4 2.7 %tap_matrices.1 = (bf16[2,4,3584,256]{3,2,1,0:T(8,128)(2,1)S(1)}, bf16[2,4,512,512]{3,2,1,0:T(8,128)(2,1)S(1)}, f32[2,12,128]{2,1,0:T(8,128)S(1)}) custom-call(f32[2,49,128]{2,1,0:T(8,128)S(1)} %copy.12.k_ref.refs_7_, bf16[2,128,512]{2,1,0:T(8,128)(2,1)S(1)} %copy-done.1, f32[2,128]{1,0:T(2,128)S(1)} %copy-done.5, f32[2,128]{1,0:T(2,128)S(1)} %copy-done.7, ...), custom_call_target="tpu_custom_call" | custom-call | bytes 14680064 | tf_op jit(solution)/shard_map/tap_matrices/pallas_call | solution.py:119
  24.1 0.0 collective-permute-done.3.refs_5_
  24.2 1.0 %broadcast_in_dim.2.refs_1_.mask_ref = bf16[48,128,128]{2,1,0:T(8,128)(2,1)S(1)} broadcast(bf16[48,128]{1,0:T(8,128)(2,1)S(1)} %convert_element_type.2), dimensions={0,1} | broadcast | bytes 1585152 | tf_op jit(solution)/shard_map/broadcast_in_dim | solution.py:437
  25.2 0.0 copy-start.2
  25.2 0.0 copy-start.3
  25.2 0.0 copy-start.4
  25.2 0.0 copy-start.6
  25.2 0.0 copy-start.8
  25.2 0.0 copy-start.10
  25.2 0.0 copy-start.11
  25.2 0.0 copy-start.12
  25.2 11.6 %conv0_kernel.1 = (f32[9120,128]{1,0:T(8,128)S(1)}, f32[4,768,256]{2,1,0:T(8,128)S(1)}, f32[6,144,128]{2,1,0:T(8,128)S(1)}, f32[2,3,48,128]{3,2,1,0:T(8,128)S(1)}) custom-call(bf16[48,128,128]{2,1,0:T(8,128)(2,1)S(1)} %copy-done, bf16[48,128,128]{2,1,0:T(8,128)(2,1)S(1)} %broadcast_in_dim.2.refs_1_.mask_ref, ...), custom_call_target="tpu_custom_call" | custom-call | flops 1409286144 | bytes 4718592 | tf_op jit(solution)/shard_map/conv0_kernel/pallas_call | solution.py:456
  36.9 10.5 %mlp0_kernel.1.x1_ref = f32[9120,128]{1,0:T(8,128)S(1)} custom-call(f32[4,768,256]{2,1,0:T(8,128)S(1)} %get-tuple-element.21.acc_ref, f32[9120,128]{1,0:T(8,128)S(1)} %get-tuple-element.22.x0_ref, f32[6,144,128]{2,1,0:T(8,128)S(1)} %get-tuple-element.23.row_ref, f32[2,3,48,128]{3,2,1,0:T(8,128)S(1)} %get-tuple-element.24.col_ref, f32[2,128]{1,0:T(2,128)S(1)} %copy-done.6, ...), custom_call_target="tpu_custom_call" | custom-call | flops 1610612736 | bytes 4718592 | tf_op jit(solution)/shard_map/mlp0_kernel/pallas_call | solution.py:456
  47.4 9.7 %conv1_kernel.1.acc_ref = f32[4,768,256]{2,1,0:T(8,128)S(1)} custom-call(f32[9120,128]{1,0:T(8,128)S(1)} %mlp0_kernel.1.x1_ref, bf16[2,4,3584,256]{3,2,1,0:T(8,128)(2,1)S(1)} %get-tuple-element.20.refs_6_.w_ref), custom_call_target="tpu_custom_call" | custom-call | flops 1409286144 | bytes 4718592 | tf_op jit(solution)/shard_map/conv1_kernel/pallas_call | solution.py:456
  57.1 10.4 %mlp1_kernel.1 = bf16[48,128,128]{2,1,0:T(8,128)(2,1)} custom-call(f32[4,768,256]{2,1,0:T(8,128)S(1)} %conv1_kernel.1.acc_ref, f32[9120,128]{1,0:T(8,128)S(1)} %mlp0_kernel.1.x1_ref, bf16[48,128,128]{2,1,0:T(8,128)(2,1)S(1)} %broadcast_in_dim.2.refs_1_.mask_ref, f32[2,128]{1,0:T(2,128)S(1)} %copy-done.6, f32[2,128]{1,0:T(2,128)S(1)} %copy-done.8, ...), custom_call_target="tpu_custom_call" | custom-call | flops 1610612736 | bytes 4718592 | tf_op jit(solution)/shard_map/mlp1_kernel/pallas_call | solution.py:456
  (18 shorter events, 0.0 us)
Async XLA Ops:
  0.0 25.1 %copy-start = (bf16[48,128,128]{2,1,0:T(8,128)(2,1)S(1)}, bf16[48,128,128]{2,1,0:T(8,128)(2,1)}, u32[]{:S(2)}) copy-start(bf16[48,128,128]{2,1,0:T(8,128)(2,1)} %refs_0_.3) | copy-start | bytes 4718596
  2.1 5.8 %collective-permute-start.1 = (bf16[48,6,128]{2,1,0:T(8,128)(2,1)S(1)}, bf16[48,6,128]{2,1,0:T(8,128)(2,1)S(1)}, u32[]{:S(2)}, u32[]{:S(2)}) collective-permute-start(bf16[48,6,128]{2,1,0:T(8,128)(2,1)S(1)} %get-tuple-element.29), channel_id=1, source_target_pairs={{1,0},{2,1},{3,2},{0,3},{5,4},{6,5},{7,6},{4,7},{9,8},{10,9},{11,1... | collective-permute-start | bytes 221192 | tf_op jit(solution)/shard_map/ppermute | solution.py:47
  6.3 5.3 %collective-permute-start = (bf16[48,6,128]{2,1,0:T(8,128)(2,1)S(1)}, bf16[48,6,128]{2,1,0:T(8,128)(2,1)S(1)}, u32[]{:S(2)}, u32[]{:S(2)}) collective-permute-start(bf16[48,6,128]{2,1,0:T(8,128)(2,1)S(1)} %get-tuple-element.30), channel_id=1, source_target_pairs={{0,1},{1,2},{2,3},{3,0},{4,5},{5,6},{6,7},{7,4},{8,9},{9,10},{10,1... | collective-permute-start | bytes 221192 | tf_op jit(solution)/shard_map/ppermute | solution.py:46
  11.7 12.4 %collective-permute-start.3 = (bf16[6,140,128]{2,1,0:T(8,128)(2,1)S(1)}, bf16[6,140,128]{2,1,0:T(8,128)(2,1)S(1)}, u32[]{:S(2)}, u32[]{:S(2)}) collective-permute-start(bf16[6,140,128]{2,1,0:T(8,128)(2,1)S(1)} %get-tuple-element.31), channel_id=1, source_target_pairs={{4,8},{5,9},{6,10},{7,11},{8,4},{9,5},{10,6},{11,7},{12,16},{13,17... | collective-permute-start | bytes 645128 | tf_op jit(solution)/shard_map/ppermute | solution.py:52
  16.8 7.3 %collective-permute-start.2 = (bf16[6,140,128]{2,1,0:T(8,128)(2,1)S(1)}, bf16[6,140,128]{2,1,0:T(8,128)(2,1)S(1)}, u32[]{:S(2)}, u32[]{:S(2)}) collective-permute-start(bf16[6,140,128]{2,1,0:T(8,128)(2,1)S(1)} %get-tuple-element.32), channel_id=1, source_target_pairs={{0,4},{1,5},{2,6},{3,7},{4,0},{5,1},{6,2},{7,3},{8,12},{9,13},{10,... | collective-permute-start | bytes 645128 | tf_op jit(solution)/shard_map/ppermute | solution.py:51
  18.4 0.9 %copy-start.1 = (bf16[2,128,512]{2,1,0:T(8,128)(2,1)S(1)}, bf16[2,128,512]{2,1,0:T(8,128)(2,1)}, u32[]{:S(2)}) copy-start(bf16[2,128,512]{2,1,0:T(8,128)(2,1)} %refs_3_.3) | copy-start | bytes 786436
  19.4 0.7 %copy-start.5 = (f32[2,128]{1,0:T(2,128)S(1)}, f32[2,128]{1,0:T(2,128)}, u32[]{:S(2)}) copy-start(f32[2,128]{1,0:T(2,128)} %refs_0_.5) | copy-start | bytes 3076
  20.1 0.7 %copy-start.7 = (f32[2,128]{1,0:T(2,128)S(1)}, f32[2,128]{1,0:T(2,128)}, u32[]{:S(2)}) copy-start(f32[2,128]{1,0:T(2,128)} %refs_1_.3) | copy-start | bytes 3076
  20.8 0.7 %copy-start.9 = (f32[2,128]{1,0:T(2,128)S(1)}, f32[2,128]{1,0:T(2,128)}, u32[]{:S(2)}) copy-start(f32[2,128]{1,0:T(2,128)} %refs_2_.3) | copy-start | bytes 3076
  25.2 11.7 %copy-start.2 = (bf16[2,128,512]{2,1,0:T(8,128)(2,1)S(1)}, bf16[2,128,512]{2,1,0:T(8,128)(2,1)}, u32[]{:S(2)}) copy-start(bf16[2,128,512]{2,1,0:T(8,128)(2,1)} %refs_3_.3) | copy-start | bytes 786436
  25.2 11.7 %copy-start.3 = (bf16[2,512,128]{2,1,0:T(8,128)(2,1)S(1)}, bf16[2,512,128]{2,1,0:T(8,128)(2,1)}, u32[]{:S(2)}) copy-start(bf16[2,512,128]{2,1,0:T(8,128)(2,1)} %refs_5_.3) | copy-start | bytes 786436
  25.2 11.7 %copy-start.4 = (f32[2,512]{1,0:T(2,128)S(1)}, f32[2,512]{1,0:T(2,128)}, u32[]{:S(2)}) copy-start(f32[2,512]{1,0:T(2,128)} %refs_4_.3) | copy-start | bytes 12292
  25.2 11.7 %copy-start.6 = (f32[2,128]{1,0:T(2,128)S(1)}, f32[2,128]{1,0:T(2,128)}, u32[]{:S(2)}) copy-start(f32[2,128]{1,0:T(2,128)} %refs_0_.5) | copy-start | bytes 3076
  25.2 11.7 %copy-start.8 = (f32[2,128]{1,0:T(2,128)S(1)}, f32[2,128]{1,0:T(2,128)}, u32[]{:S(2)}) copy-start(f32[2,128]{1,0:T(2,128)} %refs_1_.3) | copy-start | bytes 3076
  25.2 11.7 %copy-start.10 = (f32[2,128]{1,0:T(2,128)S(1)}, f32[2,128]{1,0:T(2,128)}, u32[]{:S(2)}) copy-start(f32[2,128]{1,0:T(2,128)} %refs_2_.3) | copy-start | bytes 3076
  25.2 11.7 %copy-start.11 = (f32[2,128]{1,0:T(2,128)S(1)}, f32[2,128]{1,0:T(2,128)}, u32[]{:S(2)}) copy-start(f32[2,128]{1,0:T(2,128)} %refs_6_.3) | copy-start | bytes 3076
  25.2 11.7 %copy-start.12 = (f32[2,128]{1,0:T(2,128)S(1)}, f32[2,128]{1,0:T(2,128)}, u32[]{:S(2)}) copy-start(f32[2,128]{1,0:T(2,128)} %refs_7_.3) | copy-start | bytes 3076

commit v9 on v8

--- a/solution.py
+++ b/solution.py
@@ -33,24 +33,30 @@
     return route
 
 
-def exchange(fields, wet_mask):
-    nlat, nlon = lax.axis_size("lat"), lax.axis_size("lon")
-    lat = lax.axis_index("lat")
+def edge(fields, wet_mask, r0, r1, c0, c1):
+    return fields[r0:r1, c0:c1] * wet_mask[r0:r1, c0:c1].astype(BF)[:, :, None]
+
+
+def exchange_columns(fields, wet_mask):
+    nlon = lax.axis_size("lon")
     rows, cols = wet_mask.shape
-
-    def edge(r0, r1, c0, c1):
-        return fields[r0:r1, c0:c1] * wet_mask[r0:r1, c0:c1].astype(BF)[:, :, None]
-
     up = [(i, (i + 1) % nlon) for i in range(nlon)]
     down = [(j, i) for i, j in up]
-    left = lax.ppermute(edge(0, rows, cols - REACH, cols), "lon", up)
-    right = lax.ppermute(edge(0, rows, 0, REACH), "lon", down)
-    first = jnp.concatenate([left[:REACH], edge(0, REACH, 0, cols), right[:REACH]], axis=1)
-    last = jnp.concatenate([left[rows - REACH :], edge(rows - REACH, rows, 0, cols), right[rows - REACH :]], axis=1)
-    even = lat % 2 == 0
+    left = lax.ppermute(edge(fields, wet_mask, 0, rows, cols - REACH, cols), "lon", up)
+    right = lax.ppermute(edge(fields, wet_mask, 0, rows, 0, REACH), "lon", down)
+    return left, right
+
+
+def exchange_rows(fields, wet_mask, left, right):
+    nlat, nlon = lax.axis_size("lat"), lax.axis_size("lon")
+    rows, cols = wet_mask.shape
+    first = jnp.concatenate([left[:REACH], edge(fields, wet_mask, 0, REACH, 0, cols), right[:REACH]], axis=1)
+    last = edge(fields, wet_mask, rows - REACH, rows, 0, cols)
+    last = jnp.concatenate([left[rows - REACH :], last, right[rows - REACH :]], axis=1)
+    even = lax.axis_index("lat") % 2 == 0
     got_a = lax.ppermute(jnp.where(even, last, first), ("lat", "lon"), partners(nlat, nlon, 0))
     got_b = lax.ppermute(jnp.where(even, first, last), ("lat", "lon"), partners(nlat, nlon, 1))
-    return left, right, got_a, got_b
+    return got_a, got_b
 
 
 def regroup(parts, width):
@@ -69,23 +75,24 @@
     return parts
 
 
-def tap_kernel(k_ref, inw_ref, cbias_ref, gain_ref, nbias_ref, w_ref, spread_ref, lines_ref, kv_ref):
-    ch = k_ref.shape[2]
+def tap_kernel(blocks, small_ref, inw_ref, w_ref, spread_ref, lines_ref, kv_ref):
+    ch = small_ref.shape[1]
     lanes = w_ref.shape[3]
     width = lanes // OUTS
     groups = ch // width
-    gr = pl.program_id(1)
+    b, gr = pl.program_id(0), pl.program_id(1)
 
     @pl.when(gr == 0)
     def _():
         block = lax.broadcasted_iota(jnp.int32, (1, ch), 1) // width
-        for n, ref in enumerate((cbias_ref, gain_ref, nbias_ref)):
+        for n in range(3):
+            vec = small_ref[pl.ds(blocks * (TAPS * TAPS + n) + b, 1), :]
             for g in range(groups):
                 line = jnp.zeros((1, ch), F32)
                 for j in range(groups):
-                    line = jnp.where(block == j, pltpu.roll(ref[pl.ds(pl.program_id(0), 1), :], (j - g) * width % ch, 1), line)
+                    line = jnp.where(block == j, pltpu.roll(vec, (j - g) * width % ch, 1), line)
                 lines_ref[0, n * groups + g : n * groups + g + 1, :] = line
-        down = [k_ref[0, pl.ds(s, TAPS, stride=TAPS), :] for s in range(TAPS - 1, -1, -1)]
+        down = [small_ref[pl.ds(b * TAPS * TAPS + s, TAPS, stride=TAPS), :] for s in range(TAPS - 1, -1, -1)]
         down.append(jnp.zeros((TAPS, ch), F32))
         halves = [regroup(down[i : i + groups], width) for i in range(0, OUTS, groups)]
         out_col = lax.broadcasted_iota(jnp.int32, (TAPS, lanes), 1) // width
@@ -103,27 +110,23 @@
             vec = kv_ref[gr, p, r : r + 1, :]
             at = (r * 2 * OUTS + p) * width
             w_ref[0, 0, at : at + width, :] = jnp.where(own, vec, 0.0).astype(BF)
-    mine = inw_ref[0]
+    mine = inw_ref[b, pl.ds(pl.multiple_of(gr * width, width), width), :]
     for o in range(groups):
         for j in range(groups):
             spread_ref[0, o, j * width : (j + 1) * width, :] = mine if j == o else jnp.zeros_like(mine)
 
 
-def tap_matrices(conv_kernel, in_weight, conv_bias, norm_gain, norm_bias):
-    blocks, taps, ch = conv_kernel.shape
+def tap_matrices(blocks, small, in_weight):
+    ch = small.shape[1]
     hid = in_weight.shape[2]
     lanes = 2 * ch
     width = lanes // OUTS
     groups = ch // width
     depth = TAPS * 2 * OUTS * width
     return pl.pallas_call(
-        tap_kernel,
+        functools.partial(tap_kernel, blocks),
         grid=(blocks, groups),
-        in_specs=[
-            pl.BlockSpec((1, taps, ch), lambda b, g: (b, 0, 0)),
-            pl.BlockSpec((1, width, hid), lambda b, g: (b, g, 0)),
-        ]
-        + [pl.BlockSpec((blocks, ch), lambda b, g: (0, 0))] * 3,
+        in_specs=[pl.BlockSpec(memory_space=pltpu.VMEM)] * 2,
         out_specs=(
             pl.BlockSpec((1, 1, depth, lanes), lambda b, g: (b, g, 0, 0)),
             pl.BlockSpec((1, groups, ch, hid), lambda b, g: (b, 0, g, 0)),
@@ -140,7 +143,7 @@
             flops=0, bytes_accessed=2 * blocks * groups * depth * lanes, transcendentals=0
         ),
         name="tap_matrices",
-    )(conv_kernel, in_weight, conv_bias, norm_gain, norm_bias)
+    )(small, in_weight)
 
 
 class Sizes:
@@ -153,8 +156,8 @@
         self.lines = (rows + 2 * REACH) * self.pitch
         self.wide0 = cols + 16
 
-    def line(self, row):
-        return pl.multiple_of((row + REACH) * self.pitch, 8)
+    def line(self, row, above=REACH):
+        return pl.multiple_of((row + above) * self.pitch, 8)
 
 
 def place():
@@ -162,9 +165,8 @@
     return lat % 2 == 0, lat == lax.axis_size("lat") - 1, lat == 0
 
 
-def relay(size, src_ref, relaid_ref):
+def relay(size, lines, start, relaid_ref, first=0):
     octets, groups, width, ch = size.octets, size.groups, size.width, size.ch
-    lines = size.rows + 2 * HALO
     step = next(d for d in (6, 4, 3, 2, 1) if lines % d == 0)
     shape = (groups * ch, groups * ch)
     old = lax.broadcasted_iota(jnp.int32, shape, 0)
@@ -175,14 +177,15 @@
         cells = []
         for a in range(4):
             for i in range(step):
-                at = size.line(q * step + i - HALO) + BASE - HALO + 4 * a
+                src_ref, at = start(q * step + i)
+                at = at + BASE - HALO + 4 * a
                 parts = [src_ref[pl.ds(at + j, octets, stride=OUTS), :].astype(BF) for j in range(groups)]
                 cells.append(jnp.concatenate(parts, axis=1))
         moved = jnp.dot(jnp.concatenate(cells, axis=0), order, preferred_element_type=F32).astype(BF)
         n = step * octets
         for a in range(4):
             for gr in range(groups):
-                relaid_ref[gr, a, pl.ds(pl.multiple_of(q * n, 16), n), :] = moved[
+                relaid_ref[gr, a, pl.ds(pl.multiple_of(first * octets + q * n, 16), n), :] = moved[
                     a * n : (a + 1) * n, gr * ch : (gr + 1) * ch
                 ]
         return carry
@@ -190,96 +193,133 @@
     lax.fori_loop(0, lines // step, one, 0)
 
 
-def conv(size, relaid_ref, w_ref, acc_ref, beside=()):
+def conv(size, relaid_ref, ends_ref, w_ref, acc_ref, beside=()):
     octets, rows = size.octets, size.rows
 
     for gr in range(size.groups):
         parts = []
         for r in range(TAPS):
             for a in range(4):
-                parts.append(relaid_ref[gr, a, r * octets : (r + rows) * octets, :])
+                low, high = max(HALO - r, 0), max(r - HALO, 0)
+                rows_in = [relaid_ref[gr, a, high * octets : (rows - low) * octets, :]]
+                if low:
+                    rows_in.insert(0, ends_ref[gr, a, (HALO - low) * octets : HALO * octets, :])
+                if high:
+                    rows_in.append(ends_ref[gr, a, HALO * octets : (HALO + high) * octets, :])
+                parts.append(jnp.concatenate(rows_in, axis=0))
         acc_ref[gr] = jnp.dot(jnp.concatenate(parts, axis=1), w_ref[0, gr], preferred_element_type=F32)
         for work in beside[gr :: size.groups]:
             work()
 
 
-def column_strip(size, start, x0_ref, k_ref, strip_ref):
+def column_strip(size, side, x0_ref, edge_ref, k_ref, side_ref, strip_ref):
     rows, pitch = size.rows, size.pitch
+    start = BASE + (-HALO if side == 0 else size.cols) - HALO
+    north = (TAPS + HALO - 1 + HALO) * pitch
+    for c in range(TAPS + HALO - 1):
+        side_ref[side, c, 0:HALO, :] = edge_ref[pl.ds(HALO * pitch + start + c, HALO, stride=pitch), :]
+        side_ref[side, c, HALO : HALO + rows, :] = x0_ref[pl.ds(start + c, rows, stride=pitch), :]
+        side_ref[side, c, HALO + rows : 2 * HALO + rows, :] = edge_ref[pl.ds(north + start + c, HALO, stride=pitch), :]
     sums = [jnp.zeros((rows, size.ch), F32) for _ in range(HALO)]
     for r in range(TAPS):
         for c in range(TAPS + HALO - 1):
-            at = (REACH - HALO + r) * pitch + BASE + start - HALO + c
-            cells = x0_ref[pl.ds(at, rows, stride=pitch), :]
+            cells = side_ref[side, c, r : r + rows, :]
             for i in range(HALO):
                 if 0 <= c - i < TAPS:
                     tap = TAPS * r + c - i
-                    sums[i] = sums[i] + cells * k_ref[0, tap : tap + 1, :]
+                    sums[i] = sums[i] + cells * k_ref[tap : tap + 1, :]
     for i in range(HALO):
-        strip_ref[i] = sums[i]
-
-
-def row_strip(size, side, c, piece, top, x0_ref, k_ref, strip_ref):
+        strip_ref[side, i] = sums[i]
+
+
+def row_strip(size, side, c, piece, top, edge_ref, k_ref, strip_ref):
     pitch, lead = size.pitch, BASE - REACH
-    first = (0 if side == 0 else size.rows + HALO) * pitch
+    lines_in = TAPS + HALO - 1
+    first = side * lines_in * pitch
     sums = [jnp.zeros((piece, size.ch), F32) for _ in range(HALO)]
     for s in range(TAPS):
         at = first + lead + s + c
-        lines = [x0_ref[at + i * pitch : at + i * pitch + piece, :] for i in range(TAPS + HALO - 1)]
+        lines = [edge_ref[at + i * pitch : at + i * pitch + piece, :] for i in range(lines_in)]
         for r in range(TAPS):
             tap = TAPS * r + s
             if side == 1:
                 tap = jnp.where(top, TAPS * TAPS - 1 - tap, tap)
-            weight = k_ref[0, pl.ds(tap, 1), :]
+            weight = k_ref[pl.ds(tap, 1), :]
             for i in range(HALO):
                 sums[i] = sums[i] + lines[i + r] * weight
     for i in range(HALO):
         strip_ref[side * HALO + i, c : c + piece, :] = sums[i]
 
 
-def conv0_kernel(size, *refs):
-    x_ref, mask_ref, left_ref, right_ref, a_ref, b_ref, w_ref, k_ref = refs[:8]
-    x0_ref, acc_ref, row_ref, col_ref, relaid_ref, flip_ref = refs[8:]
+def lay_kernel(size, x_ref, mask_ref, left_ref, right_ref, x0_ref, relaid_ref):
+    rows, cols, ch, pitch = size.rows, size.cols, size.ch, size.pitch
+    lead = BASE - REACH
+
+    def fill(i, carry):
+        at = size.line(i, 0)
+        x0_ref[pl.ds(at, BASE), :] = jnp.zeros((BASE, ch), F32)
+        x0_ref[pl.ds(at + lead, REACH), :] = left_ref[i].astype(F32)
+        x0_ref[pl.ds(at + BASE, cols), :] = (x_ref[i] * mask_ref[i]).astype(F32)
+        x0_ref[pl.ds(at + BASE + cols, 16), :] = jnp.zeros((16, ch), F32)
+        x0_ref[pl.ds(at + BASE + cols, REACH), :] = right_ref[i].astype(F32)
+        return carry
+
+    lax.fori_loop(0, rows, fill, 0)
+    relay(size, rows, lambda i: (x0_ref, size.line(i, 0)), relaid_ref)
+
+
+def conv0_kernel(size, x0_ref, relaid_ref, a_ref, b_ref, w_ref, k_ref, *refs):
+    edge_ref, acc_ref, row_ref, col_ref, ends_ref, flip_ref, side_ref = refs
     rows, cols, ch, pitch, wide0 = size.rows, size.cols, size.ch, size.pitch, size.wide0
-    base, ext, lead = BASE, cols + 2 * REACH, BASE - REACH
-    line = size.line
+    ext, lead = cols + 2 * REACH, BASE - REACH
     even, top, _ = place()
-
-    def fill(i, carry):
-        at = line(i)
-        x0_ref[pl.ds(at, base), :] = jnp.zeros((base, ch), F32)
-        x0_ref[pl.ds(at + lead, REACH), :] = left_ref[i].astype(F32)
-        x0_ref[pl.ds(at + base, cols), :] = (x_ref[i] * mask_ref[i]).astype(F32)
-        x0_ref[pl.ds(at + base + cols, 16), :] = jnp.zeros((16, ch), F32)
-        x0_ref[pl.ds(at + base + cols, REACH), :] = right_ref[i].astype(F32)
-        return carry
-
-    lax.fori_loop(0, rows, fill, 0)
+    lines_in = TAPS + HALO - 1
+
     flip_ref[...] = jnp.zeros(flip_ref.shape, F32)
     at = lax.broadcasted_iota(jnp.int32, (wide0, wide0), 0)
     to = lax.broadcasted_iota(jnp.int32, (wide0, wide0), 1)
     mirror = jnp.where(to == jnp.where(top, ext - 1 - at, at), 1.0, 0.0).astype(BF)
+    edge_ref[0 : REACH * pitch, :] = jnp.zeros((REACH * pitch, ch), F32)
+    north = (lines_in + HALO) * pitch
+    edge_ref[north : north + REACH * pitch, :] = jnp.zeros((REACH * pitch, ch), F32)
+    turned = []
+    for i in range(0, REACH, 2):
+        for h in range(2):
+            south = (i + h) * pitch + lead
+            edge_ref[south : south + ext, :] = jnp.where(even, b_ref[i + h].astype(F32), a_ref[i + h].astype(F32))
+            src = jnp.where(top, REACH - 1 - i - h, i + h)
+            flip_ref[i + h, 0:ext, :] = jnp.where(even, a_ref[src].astype(F32), b_ref[src].astype(F32))
+        both = jnp.concatenate([flip_ref[i + h, 0:wide0, :].astype(BF) for h in range(2)], axis=1)
+        turned.append(jnp.dot(mirror, both, preferred_element_type=F32))
     for i in range(REACH):
-        south, north = i * pitch, (rows + REACH + i) * pitch
-        x0_ref[south : south + pitch, :] = jnp.zeros((pitch, ch), F32)
-        x0_ref[south + lead : south + lead + ext, :] = jnp.where(even, b_ref[i].astype(F32), a_ref[i].astype(F32))
-        src = jnp.where(top, REACH - 1 - i, i)
-        flip_ref[0:ext, :] = jnp.where(even, a_ref[src].astype(F32), b_ref[src].astype(F32))
-        turned = jnp.dot(mirror, flip_ref[0:wide0, :].astype(BF), preferred_element_type=F32)
-        x0_ref[north : north + pitch, :] = jnp.zeros((pitch, ch), F32)
-        x0_ref[north + lead : north + lead + wide0, :] = turned
-    relay(size, x0_ref, relaid_ref)
+        put = north + i * pitch + lead
+        edge_ref[put : put + wide0, :] = turned[i // 2][:, i % 2 * ch : (i % 2 + 1) * ch]
+    for i in range(HALO):
+        for slot, row in ((REACH + i, i), (lines_in + i, rows - HALO + i)):
+            edge_ref[slot * pitch : (slot + 1) * pitch, :] = x0_ref[row * pitch : (row + 1) * pitch, :]
+
+    def start(i):
+        return edge_ref, pl.multiple_of(jnp.where(i < HALO, HALO + i, lines_in + i) * pitch, 8)
+
+    relay(size, 2 * HALO, start, ends_ref)
     piece = wide0 // 3
-    beside = [functools.partial(column_strip, size, -HALO, x0_ref, k_ref, col_ref.at[0])]
-    beside.append(functools.partial(column_strip, size, cols, x0_ref, k_ref, col_ref.at[1]))
+    beside = [
+        functools.partial(column_strip, size, side, x0_ref, edge_ref, k_ref, side_ref, col_ref) for side in range(2)
+    ]
     for side in range(2):
         for c in range(0, wide0, piece):
-            beside.append(functools.partial(row_strip, size, side, c, piece, top, x0_ref, k_ref, row_ref))
-    conv(size, relaid_ref, w_ref, acc_ref, beside)
-
-
-def conv1_kernel(size, x1_ref, w_ref, acc_ref, relaid_ref):
-    relay(size, x1_ref, relaid_ref)
-    conv(size, relaid_ref, w_ref, acc_ref)
+            beside.append(functools.partial(row_strip, size, side, c, piece, top, edge_ref, k_ref, row_ref))
+    conv(size, relaid_ref, ends_ref, w_ref, acc_ref, beside)
+
+
+def conv1_kernel(size, x1_ref, w_ref, acc_ref, relaid_ref, ends_ref):
+    relay(size, size.rows, lambda i: (x1_ref, size.line(i)), relaid_ref)
+
+    def start(i):
+        return x1_ref, size.line(jnp.where(i < HALO, i - HALO, size.rows - HALO + i))
+
+    relay(size, 2 * HALO, start, ends_ref)
+    conv(size, relaid_ref, ends_ref, w_ref, acc_ref)
 
 
 def gelu_twice(h):
@@ -355,7 +395,7 @@
     return val.astype(BF).astype(F32)
 
 
-def inner(size, b, params, acc_ref, src_ref, dst_ref):
+def inner(size, b, params, acc_ref, src_ref, above, dst_ref):
     rows, octets, groups, ch = size.rows, size.octets, size.groups, size.ch
     spread_ref, lines_ref = params[8:]
     step = next(d for d in (24, 16, 12, 8, 6, 4, 3, 2, 1) if rows % d == 0)
@@ -370,15 +410,16 @@
             for j in range(groups):
                 branch = project(b, params, normed, spread_ref, (0, j))
                 for i in range(step):
-                    at = size.line(t * step + i) + BASE + half * groups + j
-                    spot = pl.ds(at, octets, stride=OUTS)
-                    dst_ref[spot, :] = rounded(src_ref[spot, :] + branch[i * octets : (i + 1) * octets])
+                    at = BASE + half * groups + j
+                    old = src_ref[pl.ds(size.line(t * step + i, above) + at, octets, stride=OUTS), :]
+                    new = rounded(old + branch[i * octets : (i + 1) * octets])
+                    dst_ref[pl.ds(size.line(t * step + i) + at, octets, stride=OUTS), :] = new
         return carry
 
     lax.fori_loop(0, rows // step, one, 0)
 
 
-def mlp0_kernel(size, acc_ref, x0_ref, row_ref, col_ref, *refs):
+def mlp0_kernel(size, acc_ref, x0_ref, edge_ref, row_ref, col_ref, *refs):
     params, x1_ref = refs[:10], refs[10]
     rows, cols, ch, pitch, wide0 = size.rows, size.cols, size.ch, size.pitch, size.wide0
     base, near = BASE, BASE - HALO
@@ -391,17 +432,18 @@
         return carry
 
     lax.fori_loop(0, rows, clear, 0)
-    inner(size, 0, params, acc_ref, x0_ref, x1_ref)
+    inner(size, 0, params, acc_ref, x0_ref, 0, x1_ref)
     for side, start in enumerate((-HALO, cols)):
         for i, branch in enumerate(mlp(0, params, [col_ref[side, i] for i in range(HALO)])):
-            spot = pl.ds(REACH * pitch + BASE + start + i, rows, stride=pitch)
-            x1_ref[spot, :] = rounded(x0_ref[spot, :] + branch)
+            old = x0_ref[pl.ds(BASE + start + i, rows, stride=pitch), :]
+            x1_ref[pl.ds(REACH * pitch + BASE + start + i, rows, stride=pitch), :] = rounded(old + branch)
     for side in range(2):
         branches = mlp(0, params, [row_ref[side * HALO + i] for i in range(HALO)])
         for i, branch in enumerate(branches):
             row = i - HALO if side == 0 else rows + i
             at = (row + REACH) * pitch + near
-            new = rounded(x0_ref[at : at + wide0, :] + branch)
+            here = (side * (TAPS + HALO - 1) + HALO + i) * pitch + near
+            new = rounded(edge_ref[here : here + wide0, :] + branch)
             if side == 0:
                 new = jnp.where(bottom, 0.0, new)
             x1_ref[at : at + wide0, :] = new
@@ -409,7 +451,7 @@
 
 def mlp1_kernel(size, acc_ref, x1_ref, mask_ref, *refs):
     params, (out_ref, x2_ref) = refs[:10], refs[10:]
-    inner(size, 1, params, acc_ref, x1_ref, x2_ref)
+    inner(size, 1, params, acc_ref, x1_ref, REACH, x2_ref)
 
     def finish(i, carry):
         out_ref[i] = x2_ref[pl.ds(size.line(i) + BASE, size.cols), :].astype(BF) * mask_ref[i]
@@ -432,16 +474,20 @@
     layer_scale,
 ):
     rows, cols, ch = fields.shape
-    left, right, got_a, got_b = exchange(fields, wet_mask)
-    conv_kernel, whole_mask, left, right = lax.optimization_barrier((conv_kernel, wet_mask, left, right))
-    mask = jnp.broadcast_to(whole_mask.astype(BF)[:, :, None], fields.shape)
-    taps, spread, lines = tap_matrices(conv_kernel, in_weight, conv_bias, norm_gain, norm_bias)
+    left, right = exchange_columns(fields, wet_mask)
+    mask = jnp.broadcast_to(wet_mask.astype(BF)[:, :, None], fields.shape)
+    small = jnp.concatenate([conv_kernel.reshape(-1, ch), conv_bias, norm_gain, norm_bias])
+    taps, spread, lines = tap_matrices(conv_kernel.shape[0], small, in_weight)
+    left, right, taps, spread, lines = lax.optimization_barrier((left, right, taps, spread, lines))
+    got_a, got_b = exchange_rows(fields, wet_mask, left, right)
     groups, depth, width = taps.shape[1:]
     hid = in_weight.shape[2]
     size = Sizes(rows, cols, ch)
     cells = rows * cols
     vmem = pl.BlockSpec(memory_space=pltpu.VMEM)
-    relaid = pltpu.VMEM((groups, 4, (rows + 2 * HALO) * size.octets, ch), BF)
+    relaid = jax.ShapeDtypeStruct((groups, 4, rows * size.octets, ch), BF)
+    ends = pltpu.VMEM((groups, 4, 2 * HALO * size.octets, ch), BF)
+    own = jax.ShapeDtypeStruct((rows * size.pitch, ch), F32)
     padded = jax.ShapeDtypeStruct((size.lines, ch), F32)
     sums = jax.ShapeDtypeStruct((groups, rows * size.octets, width), F32)
 
@@ -470,15 +516,18 @@
     params = (conv_bias, norm_gain, norm_bias, in_weight, in_bias, out_weight, out_bias, layer_scale, spread, lines)
     row_strips = jax.ShapeDtypeStruct((2 * HALO, size.wide0, ch), F32)
     col_strips = jax.ShapeDtypeStruct((2, HALO, rows, ch), F32)
-    x0, acc, row_sums, col_sums = call(
+    lines_in = TAPS + HALO - 1
+    edges = jax.ShapeDtypeStruct((2 * lines_in * size.pitch, ch), F32)
+    x0, moved = call(lay_kernel, (fields, mask, left, right), (own, relaid), [], conv_flops // 4)
+    edge, acc, row_sums, col_sums = call(
         conv0_kernel,
-        (fields, mask, left, right, got_a, got_b, taps, conv_kernel),
-        (padded, sums, row_strips, col_strips),
-        [relaid, pltpu.VMEM((cols + 24, ch), F32)],
+        (x0, moved, got_a, got_b, taps, small),
+        (edges, sums, row_strips, col_strips),
+        [ends, pltpu.VMEM((REACH, cols + 24, ch), F32), pltpu.VMEM((2, lines_in, rows + 8, ch), F32)],
         conv_flops,
     )
-    x1 = call(mlp0_kernel, (acc, x0, row_sums, col_sums) + params, padded, [], mlp_flops)
-    acc = call(conv1_kernel, (x1, taps), sums, [relaid], conv_flops)
+    x1 = call(mlp0_kernel, (acc, x0, edge, row_sums, col_sums) + params, padded, [], mlp_flops)
+    acc = call(conv1_kernel, (x1, taps), sums, [pltpu.VMEM(relaid.shape, BF), ends], conv_flops)
     whole = pltpu.VMEM((size.lines, ch), F32)
     return call(mlp1_kernel, (acc, x1, mask) + params, jax.ShapeDtypeStruct(fields.shape, BF), [whole], mlp_flops)
 

time: 68.3 us -> 61.8 us (0.905)
  waiting for transfers between devices: 3.95 us -> 0.12 us
  local copies, waits for them, and re-layouts: 4.91 us -> 2.88 us
  starting transfers between devices: 9.39 us -> 8.24 us
  Pallas kernels: 44.9 us -> 45.6 us
    ppermute x4, waiting for transfers between devices: 3.95 us -> 0.12 us  [the longest x1 0.11 us: exchange_rows(): lax.ppermute(jnp.where(even, first, last), ('lat', 'lon'), partners(nlat,...]
    unnamed x26 -> x21, local copies, waits for them, and re-layouts: 3.04 us -> 1.8 us
    ppermute x4, starting transfers between devices: 9.39 us -> 8.24 us  [the longest x1 4.2 us: exchange_columns(): right = lax.ppermute(edge(fields, wet_mask, 0, rows, 0, REACH), 'lon', down)]
    another operation x1 -> x0, other arithmetic: 0.86 us -> none
    optimization_barrier x1 -> x0, local copies, waits for them, and re-layouts: 0.81 us -> none  [shards(): lax.optimization_barrier((conv_kernel, wet_mask, left, right))]
    pallas_call x4 -> x5, Pallas kernels: 42.2 us -> 42.9 us  [call(): pl.pallas_call(functools.partial(kernel, size), grid=(1,), in_specs=[spec...]
    concatenate x0 -> x1, other arithmetic: none -> 0.72 us  [shards(): jnp.concatenate([conv_kernel.reshape(-1, ch), conv_bias, norm_gain, norm_...]
  transfers between devices with their start and end apart: 4 -> 4, of which waited for: 2 -> 1; matrix products, arithmetic and copies ran while one was open for 4% -> 6% of each run, Pallas kernels for 4% -> 11%
where the time goes in v9:
time: 61.8 us; the launch traced here: 61.2 us
  Pallas kernels  45.6 us (74%)
  starting transfers between devices  8.24 us (13%)
  other arithmetic  4.15 us (7%)
  local copies, waits for them, and re-layouts  2.88 us (5%)
    pallas_call x5, Pallas kernels, call(): pl.pallas_call(functools.partial(kernel, size), grid=(1,), in_specs=[spec...  42.9 us
    ppermute x1, starting transfers between devices, exchange_columns(): right = lax.ppermute(edge(fields, wet_mask, 0, rows, 0, REACH), 'lon', down)  4.2 us
    ppermute x1, starting transfers between devices, exchange_rows(): lax.ppermute(jnp.where(even, first, last), ('lat', 'lon'), partners(nlat,...  3.96 us
    pallas_call x1, Pallas kernels, tap_matrices(): pl.pallas_call(functools.partial(tap_kernel, blocks), grid=(blocks, group...  2.64 us
    mul x2, other arithmetic, edge(): return fields[r0:r1, c0:c1] * wet_mask[r0:r1, c0:c1].astype(BF)[:, :, None]  2.4 us
    unnamed x21, local copies, waits for them, and re-layouts  1.8 us
  transfers between devices with their start and end apart: 4, of which 1 were waited for; matrix products, arithmetic and copies ran while one was open for 6% of the time, Pallas kernels for 11%

profile of v9, /device:TPU:1, one launch (start us, length us, event | category | flops | bytes accessed | tf_op | source)
XLA Modules:
  0.0 61.2 jit_solution(16401824664364173441)
XLA Ops:
  0.0 0.9 %convert_element_type.2 = bf16[48,128]{1,0:T(8,128)(2,1)S(1)} convert(s32[48,128]{1,0:T(8,128)} %param.12) | non-fusion elementwise | flops 6144 | bytes 36864 | tf_op jit(solution)/shard_map/convert_element_type | solution.py:478
  0.9 0.1 fusion.3
  0.9 1.1 %slice_multiply_fusion.2 = (bf16[48,6,128]{2,1,0:T(8,128)(2,1)S(1)}, bf16[48,6,128]{2,1,0:T(8,128)(2,1)S(1)}) fusion(bf16[48,128,128]{2,1,0:T(8,128)(2,1)} %x_ref.1, bf16[48,6]{1,0:T(8,128)(2,1)S(1)} %get-tuple-element.45, bf16[48,6]{1,0:T(8,128)(2,1)S(1)} %get-tuple-element.46), kind=kLoop, calls=%fused_computation.6 | loop fusion | flops 73728 | bytes 296064 | tf_op jit(solution)/shard_map/mul | solution.py:37
  2.1 4.2 %collective-permute-start.1 = (bf16[48,6,128]{2,1,0:T(8,128)(2,1)S(1)}, bf16[48,6,128]{2,1,0:T(8,128)(2,1)S(1)}, u32[]{:S(2)}, u32[]{:S(2)}) collective-permute-start(bf16[48,6,128]{2,1,0:T(8,128)(2,1)S(1)} %get-tuple-element.35), channel_id=1, source_target_pairs={{1,0},{2,1},{3,2},{0,3},{5,4},{6,5},{7,6},{4,7},{9,8},{10,9},{11,1... | collective-permute-start | bytes 221192 | tf_op jit(solution)/shard_map/ppermute | solution.py:46
  6.3 0.0 collective-permute-start
  6.3 0.8 %copy.13 = f32[2,49,128]{2,1,0:T(8,128)S(1)} copy(f32[2,49,128]{2,0,1:T(2,128)} %param.13) | data formatting | bytes 100352 | tf_op args[2]
  7.1 1.3 %slice_multiply_fusion.1 = (bf16[6,128,128]{2,1,0:T(8,128)(2,1)S(1)}, bf16[6,128,128]{2,1,0:T(8,128)(2,1)S(1)}) fusion(bf16[48,128,128]{2,1,0:T(8,128)(2,1)} %x_ref.1, bf16[6,128]{1,0:T(8,128)(2,1)S(1)} %get-tuple-element.43, bf16[6,128]{1,0:T(8,128)(2,1)S(1)} %get-tuple-element.44), kind=kLoop, calls=%fused_computation.5 | loop fusion | flops 196608 | bytes 789504 | tf_op jit(solution)/shard_map/mul | solution.py:37
  8.4 0.7 %pad_maximum_fusion.2.small_ref.k_ref = f32[104,128]{1,0:T(8,128)S(1)} fusion(f32[2,128]{1,0:T(2,128)} %refs_2_.3, f32[2,128]{1,0:T(2,128)} %refs_1_.3, f32[2,128]{1,0:T(2,128)} %refs_0_.3, f32[98,128]{1,0:T(8,128)S(1)} %reshape.8), kind=kLoop, calls=%fused_computation.8 | loop fusion | flops 39936 | bytes 106496 | tf_op jit(solution)/shard_map/concatenate | solution.py:479
  9.1 0.9 %copy-done = bf16[2,128,512]{2,1,0:T(8,128)(2,1)S(1)} copy-done((bf16[2,128,512]{2,1,0:T(8,128)(2,1)S(1)}, bf16[2,128,512]{2,1,0:T(8,128)(2,1)}, u32[]{:S(2)}) %copy-start) | copy-done | bytes 262168
  10.1 2.6 %tap_matrices.1 = (bf16[2,4,3584,256]{3,2,1,0:T(8,128)(2,1)S(1)}, bf16[2,4,512,512]{3,2,1,0:T(8,128)(2,1)S(1)}, f32[2,12,128]{2,1,0:T(8,128)S(1)}) custom-call(f32[104,128]{1,0:T(8,128)S(1)} %pad_maximum_fusion.2.small_ref.k_ref, bf16[2,128,512]{2,1,0:T(8,128)(2,1)S(1)} %copy-done), custom_call_target="tpu_custom_call" | custom-call | bytes 14680064 | tf_op jit(solution)/shard_map/tap_matrices/pallas_call | solution.py:126
  12.7 0.0 collective-permute-done.1.right_ref
  12.7 0.0 collective-permute-done.left_ref
  12.7 0.2 broadcast_select_fusion
  12.9 4.0 %collective-permute-start.3 = (bf16[6,140,128]{2,1,0:T(8,128)(2,1)S(1)}, bf16[6,140,128]{2,1,0:T(8,128)(2,1)S(1)}, u32[]{:S(2)}, u32[]{:S(2)}) collective-permute-start(bf16[6,140,128]{2,1,0:T(8,128)(2,1)S(1)} %get-tuple-element.37), channel_id=1, source_target_pairs={{4,8},{5,9},{6,10},{7,11},{8,4},{9,5},{10,6},{11,7},{12,16},{13,17... | collective-permute-start | bytes 645128 | tf_op jit(solution)/shard_map/ppermute | solution.py:58
  16.9 0.1 collective-permute-start.2
  17.0 1.0 %broadcast_in_dim.2.mask_ref = bf16[48,128,128]{2,1,0:T(8,128)(2,1)S(1)} broadcast(bf16[48,128]{1,0:T(8,128)(2,1)S(1)} %convert_element_type.2), dimensions={0,1} | broadcast | bytes 1585152 | tf_op jit(solution)/shard_map/broadcast_in_dim | solution.py:478
  17.9 0.0 copy-done.3
  18.0 3.9 %lay_kernel.1 = (f32[7296,128]{1,0:T(8,128)S(1)}, bf16[4,4,768,128]{3,2,1,0:T(8,128)(2,1)S(1)}) custom-call(bf16[48,128,128]{2,1,0:T(8,128)(2,1)S(1)} %copy-done.3, bf16[48,128,128]{2,1,0:T(8,128)(2,1)S(1)} %broadcast_in_dim.2.mask_ref, bf16[48,6,128]{2,1,0:T(8,128)(2,1)S(1)} %collective-permute-done.left_ref, ...), custom_call_target="tpu_custom_call" | custom-call | flops 352321536 | bytes 4718592 | tf_op jit(solution)/shard_map/lay_kernel/pallas_call | solution.py:502
  21.9 0.1 collective-permute-done.3.b_ref
  22.0 0.0 collective-permute-done.2.a_ref
  22.0 0.0 copy-start.5
  22.0 0.0 copy-start.6
  22.0 0.0 copy-start.7
  22.0 0.0 copy-start.8
  22.0 0.0 copy-start.9
  22.0 8.7 %conv0_kernel.1 = (f32[2736,128]{1,0:T(8,128)S(1)}, f32[4,768,256]{2,1,0:T(8,128)S(1)}, f32[6,144,128]{2,1,0:T(8,128)S(1)}, f32[2,3,48,128]{3,2,1,0:T(8,128)S(1)}) custom-call(f32[7296,128]{1,0:T(8,128)S(1)} %get-tuple-element.24.x0_ref, bf16[4,4,768,128]{3,2,1,0:T(8,128)(2,1)S(1)} %get-tuple-element.25.relaid_ref, ...), custom_call_target="tpu_custom_call" | custom-call | flops 1409286144 | bytes 4718592 | tf_op jit(solution)/shard_map/conv0_kernel/pallas_call | solution.py:502
  30.7 0.0 copy-done.1
  30.7 0.0 copy-done.2
  30.8 0.0 copy-done.4
  30.8 10.5 %mlp0_kernel.1.x1_ref = f32[9120,128]{1,0:T(8,128)S(1)} custom-call(f32[4,768,256]{2,1,0:T(8,128)S(1)} %get-tuple-element.27.acc_ref, f32[7296,128]{1,0:T(8,128)S(1)} %get-tuple-element.24.x0_ref, f32[2736,128]{1,0:T(8,128)S(1)} %get-tuple-element.28.edge_ref, f32[6,144,128]{2,1,0:T(8,128)S(1)} %get-tuple-element.29.row_ref, ...), custom_call_target="tpu_custom_call" | custom-call | flops 1610612736 | bytes 4718592 | tf_op jit(solution)/shard_map/mlp0_kernel/pallas_call | solution.py:502
  41.3 9.5 %conv1_kernel.1.acc_ref = f32[4,768,256]{2,1,0:T(8,128)S(1)} custom-call(f32[9120,128]{1,0:T(8,128)S(1)} %mlp0_kernel.1.x1_ref, bf16[2,4,3584,256]{3,2,1,0:T(8,128)(2,1)S(1)} %get-tuple-element.26.w_ref), custom_call_target="tpu_custom_call" | custom-call | flops 1409286144 | bytes 4718592 | tf_op jit(solution)/shard_map/conv1_kernel/pallas_call | solution.py:502
  50.9 10.3 %mlp1_kernel.1 = bf16[48,128,128]{2,1,0:T(8,128)(2,1)} custom-call(f32[4,768,256]{2,1,0:T(8,128)S(1)} %conv1_kernel.1.acc_ref, f32[9120,128]{1,0:T(8,128)S(1)} %mlp0_kernel.1.x1_ref, bf16[48,128,128]{2,1,0:T(8,128)(2,1)S(1)} %broadcast_in_dim.2.mask_ref, f32[2,128]{1,0:T(2,128)S(1)} %copy-done.7, f32[2,128]{1,0:T(2,128)S(1)} %copy-done.6, ...), custom_call_target="tpu_custom_call" | custom-call | flops 1610612736 | bytes 4718592 | tf_op jit(solution)/shard_map/mlp1_kernel/pallas_call | solution.py:502
  (13 shorter events, 0.0 us)
Async XLA Ops:
  0.0 17.9 %copy-start.3 = (bf16[48,128,128]{2,1,0:T(8,128)(2,1)S(1)}, bf16[48,128,128]{2,1,0:T(8,128)(2,1)}, u32[]{:S(2)}) copy-start(bf16[48,128,128]{2,1,0:T(8,128)(2,1)} %x_ref.1) | copy-start | bytes 4718596
  2.1 10.6 %collective-permute-start.1 = (bf16[48,6,128]{2,1,0:T(8,128)(2,1)S(1)}, bf16[48,6,128]{2,1,0:T(8,128)(2,1)S(1)}, u32[]{:S(2)}, u32[]{:S(2)}) collective-permute-start(bf16[48,6,128]{2,1,0:T(8,128)(2,1)S(1)} %get-tuple-element.35), channel_id=1, source_target_pairs={{1,0},{2,1},{3,2},{0,3},{5,4},{6,5},{7,6},{4,7},{9,8},{10,9},{11,1... | collective-permute-start | bytes 221192 | tf_op jit(solution)/shard_map/ppermute | solution.py:46
  6.3 6.5 %collective-permute-start = (bf16[48,6,128]{2,1,0:T(8,128)(2,1)S(1)}, bf16[48,6,128]{2,1,0:T(8,128)(2,1)S(1)}, u32[]{:S(2)}, u32[]{:S(2)}) collective-permute-start(bf16[48,6,128]{2,1,0:T(8,128)(2,1)S(1)} %get-tuple-element.36), channel_id=1, source_target_pairs={{0,1},{1,2},{2,3},{3,0},{4,5},{5,6},{6,7},{7,4},{8,9},{9,10},{10,1... | collective-permute-start | bytes 221192 | tf_op jit(solution)/shard_map/ppermute | solution.py:45
  9.1 0.9 %copy-start = (bf16[2,128,512]{2,1,0:T(8,128)(2,1)S(1)}, bf16[2,128,512]{2,1,0:T(8,128)(2,1)}, u32[]{:S(2)}) copy-start(bf16[2,128,512]{2,1,0:T(8,128)(2,1)} %refs_3_.3) | copy-start | bytes 786436
  12.9 9.1 %collective-permute-start.3 = (bf16[6,140,128]{2,1,0:T(8,128)(2,1)S(1)}, bf16[6,140,128]{2,1,0:T(8,128)(2,1)S(1)}, u32[]{:S(2)}, u32[]{:S(2)}) collective-permute-start(bf16[6,140,128]{2,1,0:T(8,128)(2,1)S(1)} %get-tuple-element.37), channel_id=1, source_target_pairs={{4,8},{5,9},{6,10},{7,11},{8,4},{9,5},{10,6},{11,7},{12,16},{13,17... | collective-permute-start | bytes 645128 | tf_op jit(solution)/shard_map/ppermute | solution.py:58
  16.9 5.1 %collective-permute-start.2 = (bf16[6,140,128]{2,1,0:T(8,128)(2,1)S(1)}, bf16[6,140,128]{2,1,0:T(8,128)(2,1)S(1)}, u32[]{:S(2)}, u32[]{:S(2)}) collective-permute-start(bf16[6,140,128]{2,1,0:T(8,128)(2,1)S(1)} %get-tuple-element.38), channel_id=1, source_target_pairs={{0,4},{1,5},{2,6},{3,7},{4,0},{5,1},{6,2},{7,3},{8,12},{9,13},{10,... | collective-permute-start | bytes 645128 | tf_op jit(solution)/shard_map/ppermute | solution.py:57
  22.0 8.8 %copy-start.1 = (bf16[2,128,512]{2,1,0:T(8,128)(2,1)S(1)}, bf16[2,128,512]{2,1,0:T(8,128)(2,1)}, u32[]{:S(2)}) copy-start(bf16[2,128,512]{2,1,0:T(8,128)(2,1)} %refs_3_.3) | copy-start | bytes 786436
  22.0 8.8 %copy-start.2 = (bf16[2,512,128]{2,1,0:T(8,128)(2,1)S(1)}, bf16[2,512,128]{2,1,0:T(8,128)(2,1)}, u32[]{:S(2)}) copy-start(bf16[2,512,128]{2,1,0:T(8,128)(2,1)} %refs_5_.3) | copy-start | bytes 786436
  22.0 8.8 %copy-start.4 = (f32[2,512]{1,0:T(2,128)S(1)}, f32[2,512]{1,0:T(2,128)}, u32[]{:S(2)}) copy-start(f32[2,512]{1,0:T(2,128)} %refs_4_.3) | copy-start | bytes 12292
  22.0 8.8 %copy-start.5 = (f32[2,128]{1,0:T(2,128)S(1)}, f32[2,128]{1,0:T(2,128)}, u32[]{:S(2)}) copy-start(f32[2,128]{1,0:T(2,128)} %refs_2_.3) | copy-start | bytes 3076
  22.0 8.8 %copy-start.6 = (f32[2,128]{1,0:T(2,128)S(1)}, f32[2,128]{1,0:T(2,128)}, u32[]{:S(2)}) copy-start(f32[2,128]{1,0:T(2,128)} %refs_1_.3) | copy-start | bytes 3076
  22.0 8.8 %copy-start.7 = (f32[2,128]{1,0:T(2,128)S(1)}, f32[2,128]{1,0:T(2,128)}, u32[]{:S(2)}) copy-start(f32[2,128]{1,0:T(2,128)} %refs_0_.3) | copy-start | bytes 3076
  22.0 8.8 %copy-start.8 = (f32[2,128]{1,0:T(2,128)S(1)}, f32[2,128]{1,0:T(2,128)}, u32[]{:S(2)}) copy-start(f32[2,128]{1,0:T(2,128)} %refs_6_.3) | copy-start | bytes 3076
  22.0 8.8 %copy-start.9 = (f32[2,128]{1,0:T(2,128)S(1)}, f32[2,128]{1,0:T(2,128)}, u32[]{:S(2)}) copy-start(f32[2,128]{1,0:T(2,128)} %refs_7_.3) | copy-start | bytes 3076

commit v10 on v9

--- a/solution.py
+++ b/solution.py
@@ -34,7 +34,7 @@
 
 
 def edge(fields, wet_mask, r0, r1, c0, c1):
-    return fields[r0:r1, c0:c1] * wet_mask[r0:r1, c0:c1].astype(BF)[:, :, None]
+    return jnp.where(wet_mask[r0:r1, c0:c1][:, :, None] != 0, fields[r0:r1, c0:c1], jnp.zeros((), BF))
 
 
 def exchange_columns(fields, wet_mask):
@@ -193,23 +193,19 @@
     lax.fori_loop(0, lines // step, one, 0)
 
 
-def conv(size, relaid_ref, ends_ref, w_ref, acc_ref, beside=()):
+def conv(size, gr, first, count, relaid_ref, ends_ref, w_ref, acc_ref):
     octets, rows = size.octets, size.rows
-
-    for gr in range(size.groups):
-        parts = []
-        for r in range(TAPS):
-            for a in range(4):
-                low, high = max(HALO - r, 0), max(r - HALO, 0)
-                rows_in = [relaid_ref[gr, a, high * octets : (rows - low) * octets, :]]
-                if low:
-                    rows_in.insert(0, ends_ref[gr, a, (HALO - low) * octets : HALO * octets, :])
-                if high:
-                    rows_in.append(ends_ref[gr, a, HALO * octets : (HALO + high) * octets, :])
-                parts.append(jnp.concatenate(rows_in, axis=0))
-        acc_ref[gr] = jnp.dot(jnp.concatenate(parts, axis=1), w_ref[0, gr], preferred_element_type=F32)
-        for work in beside[gr :: size.groups]:
-            work()
+    parts = []
+    for r in range(TAPS):
+        for a in range(4):
+            low, high = first + r - HALO, first + r - HALO + count
+            rows_in = [relaid_ref[gr, a, max(low, 0) * octets : min(high, rows) * octets, :]]
+            if low < 0:
+                rows_in.insert(0, ends_ref[gr, a, (HALO + low) * octets : HALO * octets, :])
+            if high > rows:
+                rows_in.append(ends_ref[gr, a, HALO * octets : (HALO + high - rows) * octets, :])
+            parts.append(jnp.concatenate(rows_in, axis=0))
+    acc_ref[gr] = jnp.dot(jnp.concatenate(parts, axis=1), w_ref[0, gr], preferred_element_type=F32)
 
 
 def column_strip(size, side, x0_ref, edge_ref, k_ref, side_ref, strip_ref):
@@ -268,11 +264,121 @@
     relay(size, rows, lambda i: (x0_ref, size.line(i, 0)), relaid_ref)
 
 
-def conv0_kernel(size, x0_ref, relaid_ref, a_ref, b_ref, w_ref, k_ref, *refs):
-    edge_ref, acc_ref, row_ref, col_ref, ends_ref, flip_ref, side_ref = refs
+def gelu_twice(h):
+    z = h * h
+    p = jnp.full_like(z, ERF_POLY[-1])
+    for coef in ERF_POLY[-2::-1]:
+        p = p * z + jnp.asarray(coef, z.dtype)
+    return h + h * jnp.tanh(h * p)
+
+
+def norm(b, params, val):
+    cbias_ref, gain_ref, nbias_ref = params[:3]
+    val = val + cbias_ref[b : b + 1, :]
+    cen = val - jnp.mean(val, axis=-1, keepdims=True)
+    var = jnp.mean(cen * cen, axis=-1, keepdims=True)
+    return (cen * lax.rsqrt(var + 1e-6) * gain_ref[b : b + 1, :] + nbias_ref[b : b + 1, :]).astype(BF)
+
+
+def project(b, params, normed, weight_ref, index):
+    inb_ref, outw_ref, outb_ref, scale_ref = params[4:8]
+    rows = normed.shape[0]
+    tile = 48 if rows % 48 == 0 else 64
+    branch = None
+    half_hid = outw_ref.shape[1] // 2
+    for c in range(0, 2 * half_hid, half_hid):
+        hid = jnp.dot(normed, weight_ref[index + (slice(None), slice(c, c + half_hid))], preferred_element_type=F32)
+        bias = inb_ref[b : b + 1, c : c + half_hid]
+        act = [gelu_twice((hid[i : i + tile] + bias).astype(BF)) for i in range(0, rows, tile)]
+        part = jnp.dot(jnp.concatenate(act, axis=0), outw_ref[b, c : c + half_hid, :], preferred_element_type=F32)
+        branch = part if branch is None else branch + part
+    scale = scale_ref[b : b + 1, :]
+    return branch * (0.5 * scale) + outb_ref[b : b + 1, :] * scale
+
+
+def mlp(b, params, parts):
+    n = parts[0].shape[0]
+    normed = jnp.concatenate([norm(b, params, part) for part in parts], axis=0)
+    branch = project(b, params, normed, params[3], (b,))
+    return [branch[i * n : (i + 1) * n] for i in range(len(parts))]
+
+
+def block_sums(size, val):
+    ch = size.ch
+    row = lax.broadcasted_iota(jnp.int32, (2 * ch, ch), 0) % ch
+    col = lax.broadcasted_iota(jnp.int32, (2 * ch, ch), 1)
+    ones = jnp.where(row // size.width == col // size.width, 1.0, 0.0).astype(BF)
+    high = val.astype(BF)
+    low = (val - high.astype(F32)).astype(BF)
+    return jnp.dot(jnp.concatenate([high, low], axis=1), ones, preferred_element_type=F32)
+
+
+def norm_grouped(size, lines_ref, parts):
+    groups = size.groups
+    share = 1.0 / size.ch
+
+    def line(n, gr):
+        return lines_ref[0, n * groups + gr : n * groups + gr + 1, :]
+
+    vals = [part + line(0, gr) for gr, part in enumerate(parts)]
+    mean = block_sums(size, sum(vals[1:], vals[0])) * share
+    cens = [val - mean for val in vals]
+    squares = [cen * cen for cen in cens]
+    inv = lax.rsqrt(block_sums(size, sum(squares[1:], squares[0])) * share + 1e-6)
+    normed = [(cen * inv * line(1, gr) + line(2, gr)).astype(BF) for gr, cen in enumerate(cens)]
+    return jnp.concatenate(normed, axis=1)
+
+
+def rounded(val):
+    return val.astype(BF).astype(F32)
+
+
+def rounded(val):
+    return val.astype(BF).astype(F32)
+
+
+def mlp_pieces(size, b, params, first, count, acc_ref, src_ref, above, dst_ref):
+    octets, groups, ch = size.octets, size.groups, size.ch
+    spread_ref, lines_ref = params[8:]
+    for half in range(2):
+        parts = [acc_ref[gr, :, half * ch : (half + 1) * ch] for gr in range(groups)]
+        normed = norm_grouped(size, lines_ref, parts)
+        for j in range(groups):
+            branch = project(b, params, normed, spread_ref, (0, j))
+            for i in range(count):
+                at = BASE + half * groups + j
+                old = src_ref[pl.ds(size.line(first + i, above) + at, octets, stride=OUTS), :]
+                new = rounded(old + branch[i * octets : (i + 1) * octets])
+                dst_ref[pl.ds(size.line(first + i) + at, octets, stride=OUTS), :] = new
+            yield
+
+
+def block(size, b, params, relaid_ref, ends_ref, w_ref, accs, src_ref, above, dst_ref, beside=()):
+    count = size.rows // len(accs)
+    groups = size.groups
+    for c in range(len(accs) + 1):
+        if c:
+            pieces = mlp_pieces(size, b, params, (c - 1) * count, count, accs[c - 1], src_ref, above, dst_ref)
+        else:
+            pieces = iter(())
+        for gr in range(groups):
+            if c < len(accs):
+                conv(size, gr, c * count, count, relaid_ref, ends_ref, w_ref, accs[c])
+            for work in beside[gr::groups] if c == 0 else ():
+                work()
+            next(pieces, None)
+            next(pieces, None)
+        for _ in pieces:
+            pass
+
+
+def block0_kernel(size, x0_ref, relaid_ref, a_ref, b_ref, w_ref, k_ref, *refs):
+    params, x1_ref, ends_ref, flip_ref, side_ref, edge_ref, row_ref, col_ref = refs[:10], *refs[10:17]
+    accs = refs[17:]
     rows, cols, ch, pitch, wide0 = size.rows, size.cols, size.ch, size.pitch, size.wide0
     ext, lead = cols + 2 * REACH, BASE - REACH
-    even, top, _ = place()
+    even, top, bottom = place()
+    near = BASE - HALO
     lines_in = TAPS + HALO - 1
 
     flip_ref[...] = jnp.zeros(flip_ref.shape, F32)
@@ -309,130 +415,15 @@
     for side in range(2):
         for c in range(0, wide0, piece):
             beside.append(functools.partial(row_strip, size, side, c, piece, top, edge_ref, k_ref, row_ref))
-    conv(size, relaid_ref, ends_ref, w_ref, acc_ref, beside)
-
-
-def conv1_kernel(size, x1_ref, w_ref, acc_ref, relaid_ref, ends_ref):
-    relay(size, size.rows, lambda i: (x1_ref, size.line(i)), relaid_ref)
-
-    def start(i):
-        return x1_ref, size.line(jnp.where(i < HALO, i - HALO, size.rows - HALO + i))
-
-    relay(size, 2 * HALO, start, ends_ref)
-    conv(size, relaid_ref, ends_ref, w_ref, acc_ref)
-
-
-def gelu_twice(h):
-    z = h * h
-    p = jnp.full_like(z, ERF_POLY[-1])
-    for coef in ERF_POLY[-2::-1]:
-        p = p * z + jnp.asarray(coef, z.dtype)
-    return h + h * jnp.tanh(h * p)
-
-
-def norm(b, params, val):
-    cbias_ref, gain_ref, nbias_ref = params[:3]
-    val = val + cbias_ref[b : b + 1, :]
-    cen = val - jnp.mean(val, axis=-1, keepdims=True)
-    var = jnp.mean(cen * cen, axis=-1, keepdims=True)
-    return (cen * lax.rsqrt(var + 1e-6) * gain_ref[b : b + 1, :] + nbias_ref[b : b + 1, :]).astype(BF)
-
-
-def project(b, params, normed, weight_ref, index):
-    inb_ref, outw_ref, outb_ref, scale_ref = params[4:8]
-    rows = normed.shape[0]
-    tile = 48 if rows % 48 == 0 else 64
-    branch = None
-    half_hid = outw_ref.shape[1] // 2
-    for c in range(0, 2 * half_hid, half_hid):
-        hid = jnp.dot(normed, weight_ref[index + (slice(None), slice(c, c + half_hid))], preferred_element_type=F32)
-        bias = inb_ref[b : b + 1, c : c + half_hid]
-        act = [gelu_twice((hid[i : i + tile] + bias).astype(BF)) for i in range(0, rows, tile)]
-        part = jnp.dot(jnp.concatenate(act, axis=0), outw_ref[b, c : c + half_hid, :], preferred_element_type=F32)
-        branch = part if branch is None else branch + part
-    scale = scale_ref[b : b + 1, :]
-    return branch * (0.5 * scale) + outb_ref[b : b + 1, :] * scale
-
-
-def mlp(b, params, parts):
-    n = parts[0].shape[0]
-    normed = jnp.concatenate([norm(b, params, part) for part in parts], axis=0)
-    branch = project(b, params, normed, params[3], (b,))
-    return [branch[i * n : (i + 1) * n] for i in range(len(parts))]
-
-
-def block_sums(size, val):
-    ch = size.ch
-    row = lax.broadcasted_iota(jnp.int32, (2 * ch, ch), 0) % ch
-    col = lax.broadcasted_iota(jnp.int32, (2 * ch, ch), 1)
-    ones = jnp.where(row // size.width == col // size.width, 1.0, 0.0).astype(BF)
-    high = val.astype(BF)
-    low = (val - high.astype(F32)).astype(BF)
-    return jnp.dot(jnp.concatenate([high, low], axis=1), ones, preferred_element_type=F32)
-
-
-def norm_grouped(size, lines_ref, parts):
-    groups = size.groups
-    share = 1.0 / size.ch
-
-    def line(n, gr):
-        return lines_ref[0, n * groups + gr : n * groups + gr + 1, :]
-
-    vals = [part + line(0, gr) for gr, part in enumerate(parts)]
-    mean = block_sums(size, sum(vals[1:], vals[0])) * share
-    cens = [val - mean for val in vals]
-    squares = [cen * cen for cen in cens]
-    inv = lax.rsqrt(block_sums(size, sum(squares[1:], squares[0])) * share + 1e-6)
-    normed = [(cen * inv * line(1, gr) + line(2, gr)).astype(BF) for gr, cen in enumerate(cens)]
-    return jnp.concatenate(normed, axis=1)
-
-
-def rounded(val):
-    return val.astype(BF).astype(F32)
-
-
-def rounded(val):
-    return val.astype(BF).astype(F32)
-
-
-def inner(size, b, params, acc_ref, src_ref, above, dst_ref):
-    rows, octets, groups, ch = size.rows, size.octets, size.groups, size.ch
-    spread_ref, lines_ref = params[8:]
-    step = next(d for d in (24, 16, 12, 8, 6, 4, 3, 2, 1) if rows % d == 0)
-    n = step * octets
-
-    def one(t, carry):
-        for half in range(2):
-            parts = [
-                acc_ref[gr, pl.ds(pl.multiple_of(t * n, 16), n), half * ch : (half + 1) * ch] for gr in range(groups)
-            ]
-            normed = norm_grouped(size, lines_ref, parts)
-            for j in range(groups):
-                branch = project(b, params, normed, spread_ref, (0, j))
-                for i in range(step):
-                    at = BASE + half * groups + j
-                    old = src_ref[pl.ds(size.line(t * step + i, above) + at, octets, stride=OUTS), :]
-                    new = rounded(old + branch[i * octets : (i + 1) * octets])
-                    dst_ref[pl.ds(size.line(t * step + i) + at, octets, stride=OUTS), :] = new
-        return carry
-
-    lax.fori_loop(0, rows // step, one, 0)
-
-
-def mlp0_kernel(size, acc_ref, x0_ref, edge_ref, row_ref, col_ref, *refs):
-    params, x1_ref = refs[:10], refs[10]
-    rows, cols, ch, pitch, wide0 = size.rows, size.cols, size.ch, size.pitch, size.wide0
-    base, near = BASE, BASE - HALO
-    _, _, bottom = place()
 
     def clear(i, carry):
         at = size.line(i)
-        x1_ref[pl.ds(at, base), :] = jnp.zeros((base, ch), F32)
-        x1_ref[pl.ds(at + base + cols, 16), :] = jnp.zeros((16, ch), F32)
+        x1_ref[pl.ds(at, BASE), :] = jnp.zeros((BASE, ch), F32)
+        x1_ref[pl.ds(at + BASE + cols, 16), :] = jnp.zeros((16, ch), F32)
         return carry
 
     lax.fori_loop(0, rows, clear, 0)
-    inner(size, 0, params, acc_ref, x0_ref, 0, x1_ref)
+    block(size, 0, params, relaid_ref, ends_ref, w_ref, accs, x0_ref, 0, x1_ref, beside)
     for side, start in enumerate((-HALO, cols)):
         for i, branch in enumerate(mlp(0, params, [col_ref[side, i] for i in range(HALO)])):
             old = x0_ref[pl.ds(BASE + start + i, rows, stride=pitch), :]
@@ -449,9 +440,16 @@
             x1_ref[at : at + wide0, :] = new
 
 
-def mlp1_kernel(size, acc_ref, x1_ref, mask_ref, *refs):
-    params, (out_ref, x2_ref) = refs[:10], refs[10:]
-    inner(size, 1, params, acc_ref, x1_ref, REACH, x2_ref)
+def block1_kernel(size, x1_ref, w_ref, mask_ref, *refs):
+    params, out_ref, relaid_ref, ends_ref, x2_ref = refs[:10], *refs[10:14]
+    accs = refs[14:]
+    relay(size, size.rows, lambda i: (x1_ref, size.line(i)), relaid_ref)
+
+    def start(i):
+        return x1_ref, size.line(jnp.where(i < HALO, i - HALO, size.rows - HALO + i))
+
+    relay(size, 2 * HALO, start, ends_ref)
+    block(size, 1, params, relaid_ref, ends_ref, w_ref, accs, x1_ref, REACH, x2_ref)
 
     def finish(i, carry):
         out_ref[i] = x2_ref[pl.ds(size.line(i) + BASE, size.cols), :].astype(BF) * mask_ref[i]
@@ -489,14 +487,15 @@
     ends = pltpu.VMEM((groups, 4, 2 * HALO * size.octets, ch), BF)
     own = jax.ShapeDtypeStruct((rows * size.pitch, ch), F32)
     padded = jax.ShapeDtypeStruct((size.lines, ch), F32)
-    sums = jax.ShapeDtypeStruct((groups, rows * size.octets, width), F32)
+    chunks = 2 if rows % 2 == 0 else 1
+    accs = [pltpu.VMEM((groups, rows // chunks * size.octets, width), F32)] * chunks
 
     def call(kernel, ins, out_shape, scratch, flops):
         def spec(value):
             if value is not taps and value is not spread and value is not lines:
                 return vmem
-            block = 0 if kernel in (conv0_kernel, mlp0_kernel) else 1
-            return pl.BlockSpec((1,) + value.shape[1:], lambda i: (block,) + (0,) * (value.ndim - 1))
+            which = 0 if kernel is block0_kernel else 1
+            return pl.BlockSpec((1,) + value.shape[1:], lambda i: (which,) + (0,) * (value.ndim - 1))
 
         several = isinstance(out_shape, tuple)
         return pl.pallas_call(
@@ -514,22 +513,31 @@
     conv_flops = 2 * cells * ch * depth // OUTS * 2
     mlp_flops = 4 * cells * ch * hid
     params = (conv_bias, norm_gain, norm_bias, in_weight, in_bias, out_weight, out_bias, layer_scale, spread, lines)
-    row_strips = jax.ShapeDtypeStruct((2 * HALO, size.wide0, ch), F32)
-    col_strips = jax.ShapeDtypeStruct((2, HALO, rows, ch), F32)
     lines_in = TAPS + HALO - 1
-    edges = jax.ShapeDtypeStruct((2 * lines_in * size.pitch, ch), F32)
     x0, moved = call(lay_kernel, (fields, mask, left, right), (own, relaid), [], conv_flops // 4)
-    edge, acc, row_sums, col_sums = call(
-        conv0_kernel,
-        (x0, moved, got_a, got_b, taps, small),
-        (edges, sums, row_strips, col_strips),
-        [ends, pltpu.VMEM((REACH, cols + 24, ch), F32), pltpu.VMEM((2, lines_in, rows + 8, ch), F32)],
-        conv_flops,
+    x1 = call(
+        block0_kernel,
+        (x0, moved, got_a, got_b, taps, small) + params,
+        padded,
+        [
+            ends,
+            pltpu.VMEM((REACH, cols + 24, ch), F32),
+            pltpu.VMEM((2, lines_in, rows + 8, ch), F32),
+            pltpu.VMEM((2 * lines_in * size.pitch, ch), F32),
+            pltpu.VMEM((2 * HALO, size.wide0, ch), F32),
+            pltpu.VMEM((2, HALO, rows, ch), F32),
+        ]
+        + accs,
+        conv_flops + mlp_flops,
     )
-    x1 = call(mlp0_kernel, (acc, x0, edge, row_sums, col_sums) + params, padded, [], mlp_flops)
-    acc = call(conv1_kernel, (x1, taps), sums, [pltpu.VMEM(relaid.shape, BF), ends], conv_flops)
     whole = pltpu.VMEM((size.lines, ch), F32)
-    return call(mlp1_kernel, (acc, x1, mask) + params, jax.ShapeDtypeStruct(fields.shape, BF), [whole], mlp_flops)
+    return call(
+        block1_kernel,
+        (x1, taps, mask) + params,
+        jax.ShapeDtypeStruct(fields.shape, BF),
+        [pltpu.VMEM(relaid.shape, BF), ends, whole] + accs,
+        conv_flops + mlp_flops,
+    )
 
 
 def solution(mesh):

time: 61.8 us -> 60.9 us (0.985)
  Pallas kernels: 45.6 us -> 43.1 us
  other arithmetic: 4.15 us -> 5.69 us
    pallas_call x5 -> x3, Pallas kernels: 42.9 us -> 40.5 us  [call(): pl.pallas_call(functools.partial(kernel, size), grid=(1,), in_specs=[spec...]
    select_n x0 -> x2, other arithmetic: none -> 2.4 us  [edge(): jnp.where(wet_mask[r0:r1, c0:c1][:, :, None] != 0, fields[r0:r1, c0:c1],...]
    mul x2 -> x0, other arithmetic: 2.4 us -> none  [edge(): return fields[r0:r1, c0:c1] * wet_mask[r0:r1, c0:c1].astype(BF)[:, :, None]]
    ne x0 -> x2, other arithmetic: none -> 1.66 us  [edge(): wet_mask[r0:r1, c0:c1][:, :, None] != 0]
    unnamed x21 -> x19, local copies, waits for them, and re-layouts: 1.8 us -> 1.8 us
  transfers between devices with their start and end apart: 4 -> 4, of which waited for: 1 -> 0; matrix products, arithmetic and copies ran while one was open for 6% -> 9% of each run, Pallas kernels for 11% -> 11%
where the time goes in v10:
time: 60.9 us; the launch traced here: 60.1 us
  Pallas kernels  43.1 us (71%)
  starting transfers between devices  8.24 us (14%)
  other arithmetic  5.69 us (9%)
  local copies, waits for them, and re-layouts  2.78 us (5%)
    pallas_call x3, Pallas kernels, call(): pl.pallas_call(functools.partial(kernel, size), grid=(1,), in_specs=[spec...  40.5 us
    ppermute x1, starting transfers between devices, exchange_columns(): right = lax.ppermute(edge(fields, wet_mask, 0, rows, 0, REACH), 'lon', down)  4.2 us
    ppermute x1, starting transfers between devices, exchange_rows(): lax.ppermute(jnp.where(even, first, last), ('lat', 'lon'), partners(nlat,...  3.96 us
    pallas_call x1, Pallas kernels, tap_matrices(): pl.pallas_call(functools.partial(tap_kernel, blocks), grid=(blocks, group...  2.63 us
    select_n x2, other arithmetic, edge(): jnp.where(wet_mask[r0:r1, c0:c1][:, :, None] != 0, fields[r0:r1, c0:c1],...  2.4 us
    unnamed x19, local copies, waits for them, and re-layouts  1.8 us
    ne x2, other arithmetic, edge(): wet_mask[r0:r1, c0:c1][:, :, None] != 0  1.66 us
  transfers between devices with their start and end apart: 4, of which 0 were waited for; matrix products, arithmetic and copies ran while one was open for 9% of the time, Pallas kernels for 11%

profile of v10, /device:TPU:1, one launch (start us, length us, event | category | flops | bytes accessed | tf_op | source)
XLA Modules:
  0.0 60.1 jit_solution(6479826322810367754)
XLA Ops:
  0.0 1.0 %slice_compare_fusion = (pred[48,6]{1,0:T(8,128)(4,1)S(1)}, pred[48,6]{1,0:T(8,128)(4,1)S(1)}) fusion(s32[48,128]{1,0:T(8,128)} %param.12), kind=kLoop, calls=%fused_computation.9 | loop fusion | flops 576 | bytes 2880 | tf_op jit(solution)/shard_map/ne | solution.py:37
  1.0 1.1 %slice_select_fusion.2 = (bf16[48,6,128]{2,1,0:T(8,128)(2,1)S(1)}, bf16[48,6,128]{2,1,0:T(8,128)(2,1)S(1)}) fusion(bf16[48,128,128]{2,1,0:T(8,128)(2,1)} %x_ref.1, pred[48,6]{1,0:T(8,128)(4,1)S(1)} %get-tuple-element.37, pred[48,6]{1,0:T(8,128)(4,1)S(1)} %get-tuple-element.38), kind=kLoop, calls=%fused_computation.6 | loop fusion | flops 73728 | bytes 295488 | tf_op jit(solution)/shard_map/jit(_where)/select_n | solution.py:37
  2.1 4.2 %collective-permute-start.1 = (bf16[48,6,128]{2,1,0:T(8,128)(2,1)S(1)}, bf16[48,6,128]{2,1,0:T(8,128)(2,1)S(1)}, u32[]{:S(2)}, u32[]{:S(2)}) collective-permute-start(bf16[48,6,128]{2,1,0:T(8,128)(2,1)S(1)} %get-tuple-element.27), channel_id=1, source_target_pairs={{1,0},{2,1},{3,2},{0,3},{5,4},{6,5},{7,6},{4,7},{9,8},{10,9},{11,1... | collective-permute-start | bytes 221192 | tf_op jit(solution)/shard_map/ppermute | solution.py:46
  6.3 0.0 collective-permute-start
  6.3 0.7 %slice_compare_fusion.3 = (pred[6,128]{1,0:T(8,128)(4,1)S(1)}, pred[6,128]{1,0:T(8,128)(4,1)S(1)}) fusion(s32[48,128]{1,0:T(8,128)} %param.12), kind=kLoop, calls=%fused_computation.12 | loop fusion | flops 1536 | bytes 7680 | tf_op jit(solution)/shard_map/ne | solution.py:37
  7.0 0.8 %copy.13 = f32[2,49,128]{2,1,0:T(8,128)S(1)} copy(f32[2,49,128]{2,0,1:T(2,128)} %param.13) | data formatting | bytes 100352 | tf_op args[2]
  7.8 1.3 %slice_select_fusion.1 = (bf16[6,128,128]{2,1,0:T(8,128)(2,1)S(1)}, bf16[6,128,128]{2,1,0:T(8,128)(2,1)S(1)}) fusion(bf16[48,128,128]{2,1,0:T(8,128)(2,1)} %x_ref.1, pred[6,128]{1,0:T(8,128)(4,1)S(1)} %get-tuple-element.35, pred[6,128]{1,0:T(8,128)(4,1)S(1)} %get-tuple-element.36), kind=kLoop, calls=%fused_computation.5 | loop fusion | flops 196608 | bytes 787968 | tf_op jit(solution)/shard_map/jit(_where)/select_n | solution.py:37
  9.1 0.7 %pad_maximum_fusion.2.small_ref.k_ref = f32[104,128]{1,0:T(8,128)S(1)} fusion(f32[2,128]{1,0:T(2,128)} %refs_2_.3, f32[2,128]{1,0:T(2,128)} %refs_1_.3, f32[2,128]{1,0:T(2,128)} %refs_0_.3, f32[98,128]{1,0:T(8,128)S(1)} %reshape.12), kind=kLoop, calls=%fused_computation.8 | loop fusion | flops 39936 | bytes 106496 | tf_op jit(solution)/shard_map/concatenate | solution.py:477
  9.8 0.9 %copy-done = bf16[2,128,512]{2,1,0:T(8,128)(2,1)S(1)} copy-done((bf16[2,128,512]{2,1,0:T(8,128)(2,1)S(1)}, bf16[2,128,512]{2,1,0:T(8,128)(2,1)}, u32[]{:S(2)}) %copy-start) | copy-done | bytes 262168
  10.8 2.6 %tap_matrices.1 = (bf16[2,4,3584,256]{3,2,1,0:T(8,128)(2,1)S(1)}, bf16[2,4,512,512]{3,2,1,0:T(8,128)(2,1)S(1)}, f32[2,12,128]{2,1,0:T(8,128)S(1)}) custom-call(f32[104,128]{1,0:T(8,128)S(1)} %pad_maximum_fusion.2.small_ref.k_ref, bf16[2,128,512]{2,1,0:T(8,128)(2,1)S(1)} %copy-done), custom_call_target="tpu_custom_call" | custom-call | bytes 14680064 | tf_op jit(solution)/shard_map/tap_matrices/pallas_call | solution.py:126
  13.4 0.0 collective-permute-done.1.right_ref
  13.4 0.0 collective-permute-done.left_ref
  13.5 0.2 broadcast_select_fusion
  13.6 4.0 %collective-permute-start.3 = (bf16[6,140,128]{2,1,0:T(8,128)(2,1)S(1)}, bf16[6,140,128]{2,1,0:T(8,128)(2,1)S(1)}, u32[]{:S(2)}, u32[]{:S(2)}) collective-permute-start(bf16[6,140,128]{2,1,0:T(8,128)(2,1)S(1)} %get-tuple-element.29), channel_id=1, source_target_pairs={{4,8},{5,9},{6,10},{7,11},{8,4},{9,5},{10,6},{11,7},{12,16},{13,17... | collective-permute-start | bytes 645128 | tf_op jit(solution)/shard_map/ppermute | solution.py:58
  17.6 0.1 collective-permute-start.2
  17.7 0.7 %convert_element_type.3 = bf16[48,128]{1,0:T(8,128)(2,1)S(1)} convert(s32[48,128]{1,0:T(8,128)} %param.12) | non-fusion elementwise | flops 6144 | bytes 36864 | tf_op jit(solution)/shard_map/convert_element_type | solution.py:476
  18.4 1.0 %broadcast_in_dim.46.mask_ref = bf16[48,128,128]{2,1,0:T(8,128)(2,1)S(1)} broadcast(bf16[48,128]{1,0:T(8,128)(2,1)S(1)} %convert_element_type.3), dimensions={0,1} | broadcast | bytes 1585152 | tf_op jit(solution)/shard_map/broadcast_in_dim | solution.py:476
  19.4 0.0 copy-done.2
  19.4 0.0 copy-start.1
  19.4 0.0 copy-start.3
  19.4 0.0 copy-start.4
  19.4 0.0 copy-start.5
  19.4 0.0 copy-start.6
  19.5 0.0 copy-start.7
  19.5 0.0 copy-start.8
  19.5 3.9 %lay_kernel.1 = (f32[7296,128]{1,0:T(8,128)S(1)}, bf16[4,4,768,128]{3,2,1,0:T(8,128)(2,1)S(1)}) custom-call(bf16[48,128,128]{2,1,0:T(8,128)(2,1)S(1)} %copy-done.2, bf16[48,128,128]{2,1,0:T(8,128)(2,1)S(1)} %broadcast_in_dim.46.mask_ref, bf16[48,6,128]{2,1,0:T(8,128)(2,1)S(1)} %collective-permute-done.left_ref, ...), custom_call_target="tpu_custom_call" | custom-call | flops 352321536 | bytes 4718592 | tf_op jit(solution)/shard_map/lay_kernel/pallas_call | solution.py:501
  23.4 0.0 collective-permute-done.3.b_ref
  23.4 0.0 collective-permute-done.2.a_ref
  23.4 0.0 copy-done.1
  23.4 0.0 copy-done.3
  23.5 18.1 %block0_kernel.1.x1_ref = f32[9120,128]{1,0:T(8,128)S(1)} custom-call(f32[7296,128]{1,0:T(8,128)S(1)} %get-tuple-element.20.x0_ref, bf16[4,4,768,128]{3,2,1,0:T(8,128)(2,1)S(1)} %get-tuple-element.21.relaid_ref, bf16[6,140,128]{2,1,0:T(8,128)(2,1)S(1)} %collective-permute-done.2.a_ref, bf16[6,140,128]{2,1,0:T(8,128)(2,1)S(1)} %collective-permute-done.3.b_ref, ...), custom_call_target="tpu_custom_call" | custom-call | flops 3019898880 | bytes 4718592 | tf_op jit(solution)/shard_map/block0_kernel/pallas_call | solution.py:501
  41.6 18.5 %block1_kernel.1 = bf16[48,128,128]{2,1,0:T(8,128)(2,1)} custom-call(f32[9120,128]{1,0:T(8,128)S(1)} %block0_kernel.1.x1_ref, bf16[2,4,3584,256]{3,2,1,0:T(8,128)(2,1)S(1)} %get-tuple-element.22.w_ref, bf16[48,128,128]{2,1,0:T(8,128)(2,1)S(1)} %broadcast_in_dim.46.mask_ref, f32[2,128]{1,0:T(2,128)S(1)} %copy-done.6, f32[2,128]{1,0:T(2,128)S(1)} %copy-done.5, ...), custom_call_target="tpu_custom_call" | custom-call | flops 3019898880 | bytes 4718592 | tf_op jit(solution)/shard_map/block1_kernel/pallas_call | solution.py:501
  (9 shorter events, 0.0 us)
Async XLA Ops:
  0.0 19.4 %copy-start.2 = (bf16[48,128,128]{2,1,0:T(8,128)(2,1)S(1)}, bf16[48,128,128]{2,1,0:T(8,128)(2,1)}, u32[]{:S(2)}) copy-start(bf16[48,128,128]{2,1,0:T(8,128)(2,1)} %x_ref.1) | copy-start | bytes 4718596
  2.1 11.3 %collective-permute-start.1 = (bf16[48,6,128]{2,1,0:T(8,128)(2,1)S(1)}, bf16[48,6,128]{2,1,0:T(8,128)(2,1)S(1)}, u32[]{:S(2)}, u32[]{:S(2)}) collective-permute-start(bf16[48,6,128]{2,1,0:T(8,128)(2,1)S(1)} %get-tuple-element.27), channel_id=1, source_target_pairs={{1,0},{2,1},{3,2},{0,3},{5,4},{6,5},{7,6},{4,7},{9,8},{10,9},{11,1... | collective-permute-start | bytes 221192 | tf_op jit(solution)/shard_map/ppermute | solution.py:46
  6.3 7.2 %collective-permute-start = (bf16[48,6,128]{2,1,0:T(8,128)(2,1)S(1)}, bf16[48,6,128]{2,1,0:T(8,128)(2,1)S(1)}, u32[]{:S(2)}, u32[]{:S(2)}) collective-permute-start(bf16[48,6,128]{2,1,0:T(8,128)(2,1)S(1)} %get-tuple-element.28), channel_id=1, source_target_pairs={{0,1},{1,2},{2,3},{3,0},{4,5},{5,6},{6,7},{7,4},{8,9},{9,10},{10,1... | collective-permute-start | bytes 221192 | tf_op jit(solution)/shard_map/ppermute | solution.py:45
  9.8 0.9 %copy-start = (bf16[2,128,512]{2,1,0:T(8,128)(2,1)S(1)}, bf16[2,128,512]{2,1,0:T(8,128)(2,1)}, u32[]{:S(2)}) copy-start(bf16[2,128,512]{2,1,0:T(8,128)(2,1)} %refs_3_.3) | copy-start | bytes 786436
  13.6 9.8 %collective-permute-start.3 = (bf16[6,140,128]{2,1,0:T(8,128)(2,1)S(1)}, bf16[6,140,128]{2,1,0:T(8,128)(2,1)S(1)}, u32[]{:S(2)}, u32[]{:S(2)}) collective-permute-start(bf16[6,140,128]{2,1,0:T(8,128)(2,1)S(1)} %get-tuple-element.29), channel_id=1, source_target_pairs={{4,8},{5,9},{6,10},{7,11},{8,4},{9,5},{10,6},{11,7},{12,16},{13,17... | collective-permute-start | bytes 645128 | tf_op jit(solution)/shard_map/ppermute | solution.py:58
  17.6 5.8 %collective-permute-start.2 = (bf16[6,140,128]{2,1,0:T(8,128)(2,1)S(1)}, bf16[6,140,128]{2,1,0:T(8,128)(2,1)S(1)}, u32[]{:S(2)}, u32[]{:S(2)}) collective-permute-start(bf16[6,140,128]{2,1,0:T(8,128)(2,1)S(1)} %get-tuple-element.30), channel_id=1, source_target_pairs={{0,4},{1,5},{2,6},{3,7},{4,0},{5,1},{6,2},{7,3},{8,12},{9,13},{10,... | collective-permute-start | bytes 645128 | tf_op jit(solution)/shard_map/ppermute | solution.py:57
  19.4 4.0 %copy-start.1 = (bf16[2,512,128]{2,1,0:T(8,128)(2,1)S(1)}, bf16[2,512,128]{2,1,0:T(8,128)(2,1)}, u32[]{:S(2)}) copy-start(bf16[2,512,128]{2,1,0:T(8,128)(2,1)} %refs_5_.3) | copy-start | bytes 786436
  19.4 4.0 %copy-start.3 = (f32[2,512]{1,0:T(2,128)S(1)}, f32[2,512]{1,0:T(2,128)}, u32[]{:S(2)}) copy-start(f32[2,512]{1,0:T(2,128)} %refs_4_.3) | copy-start | bytes 12292
  19.4 4.0 %copy-start.4 = (f32[2,128]{1,0:T(2,128)S(1)}, f32[2,128]{1,0:T(2,128)}, u32[]{:S(2)}) copy-start(f32[2,128]{1,0:T(2,128)} %refs_2_.3) | copy-start | bytes 3076
  19.4 4.0 %copy-start.5 = (f32[2,128]{1,0:T(2,128)S(1)}, f32[2,128]{1,0:T(2,128)}, u32[]{:S(2)}) copy-start(f32[2,128]{1,0:T(2,128)} %refs_1_.3) | copy-start | bytes 3076
  19.4 4.0 %copy-start.6 = (f32[2,128]{1,0:T(2,128)S(1)}, f32[2,128]{1,0:T(2,128)}, u32[]{:S(2)}) copy-start(f32[2,128]{1,0:T(2,128)} %refs_0_.3) | copy-start | bytes 3076
  19.5 4.0 %copy-start.7 = (f32[2,128]{1,0:T(2,128)S(1)}, f32[2,128]{1,0:T(2,128)}, u32[]{:S(2)}) copy-start(f32[2,128]{1,0:T(2,128)} %refs_6_.3) | copy-start | bytes 3076
  19.5 4.0 %copy-start.8 = (f32[2,128]{1,0:T(2,128)S(1)}, f32[2,128]{1,0:T(2,128)}, u32[]{:S(2)}) copy-start(f32[2,128]{1,0:T(2,128)} %refs_7_.3) | copy-start | bytes 3076

commit v11 on v10

--- a/solution.py
+++ b/solution.py
@@ -34,7 +34,7 @@
 
 
 def edge(fields, wet_mask, r0, r1, c0, c1):
-    return jnp.where(wet_mask[r0:r1, c0:c1][:, :, None] != 0, fields[r0:r1, c0:c1], jnp.zeros((), BF))
+    return fields[r0:r1, c0:c1] * wet_mask[r0:r1, c0:c1].astype(BF)[:, :, None]
 
 
 def exchange_columns(fields, wet_mask):
@@ -167,7 +167,7 @@
 
 def relay(size, lines, start, relaid_ref, first=0):
     octets, groups, width, ch = size.octets, size.groups, size.width, size.ch
-    step = next(d for d in (6, 4, 3, 2, 1) if lines % d == 0)
+    step = next(d for d in (12, 6, 4, 3, 2, 1) if lines % d == 0)
     shape = (groups * ch, groups * ch)
     old = lax.broadcasted_iota(jnp.int32, shape, 0)
     new = lax.broadcasted_iota(jnp.int32, shape, 1)
@@ -297,10 +297,12 @@
 
 
 def mlp(b, params, parts):
-    n = parts[0].shape[0]
     normed = jnp.concatenate([norm(b, params, part) for part in parts], axis=0)
     branch = project(b, params, normed, params[3], (b,))
-    return [branch[i * n : (i + 1) * n] for i in range(len(parts))]
+    ends = [0]
+    for part in parts:
+        ends.append(ends[-1] + part.shape[0])
+    return [branch[low:high] for low, high in zip(ends, ends[1:])]
 
 
 def block_sums(size, val):
@@ -353,7 +355,7 @@
             yield
 
 
-def block(size, b, params, relaid_ref, ends_ref, w_ref, accs, src_ref, above, dst_ref, beside=()):
+def block(size, b, params, relaid_ref, ends_ref, w_ref, accs, src_ref, above, dst_ref, beside=(), after=None):
     count = size.rows // len(accs)
     groups = size.groups
     for c in range(len(accs) + 1):
@@ -370,6 +372,8 @@
             next(pieces, None)
         for _ in pieces:
             pass
+        if after is not None and c == len(accs) - 1:
+            after()
 
 
 def block0_kernel(size, x0_ref, relaid_ref, a_ref, b_ref, w_ref, k_ref, *refs):
@@ -423,21 +427,25 @@
         return carry
 
     lax.fori_loop(0, rows, clear, 0)
-    block(size, 0, params, relaid_ref, ends_ref, w_ref, accs, x0_ref, 0, x1_ref, beside)
-    for side, start in enumerate((-HALO, cols)):
-        for i, branch in enumerate(mlp(0, params, [col_ref[side, i] for i in range(HALO)])):
-            old = x0_ref[pl.ds(BASE + start + i, rows, stride=pitch), :]
-            x1_ref[pl.ds(REACH * pitch + BASE + start + i, rows, stride=pitch), :] = rounded(old + branch)
-    for side in range(2):
-        branches = mlp(0, params, [row_ref[side * HALO + i] for i in range(HALO)])
-        for i, branch in enumerate(branches):
+
+    def strips():
+        parts = [row_ref[i] for i in range(2 * HALO)] + [col_ref[side, i] for side in range(2) for i in range(HALO)]
+        branches = mlp(0, params, parts)
+        for n, branch in enumerate(branches[: 2 * HALO]):
+            side, i = n // HALO, n % HALO
             row = i - HALO if side == 0 else rows + i
             at = (row + REACH) * pitch + near
-            here = (side * (TAPS + HALO - 1) + HALO + i) * pitch + near
+            here = (side * lines_in + HALO + i) * pitch + near
             new = rounded(edge_ref[here : here + wide0, :] + branch)
             if side == 0:
                 new = jnp.where(bottom, 0.0, new)
             x1_ref[at : at + wide0, :] = new
+        for n, branch in enumerate(branches[2 * HALO :]):
+            col = n - HALO if n < HALO else cols + n - HALO
+            old = x0_ref[pl.ds(BASE + col, rows, stride=pitch), :]
+            x1_ref[pl.ds(REACH * pitch + BASE + col, rows, stride=pitch), :] = rounded(old + branch)
+
+    block(size, 0, params, relaid_ref, ends_ref, w_ref, accs, x0_ref, 0, x1_ref, beside, strips)
 
 
 def block1_kernel(size, x1_ref, w_ref, mask_ref, *refs):
@@ -487,7 +495,7 @@
     ends = pltpu.VMEM((groups, 4, 2 * HALO * size.octets, ch), BF)
     own = jax.ShapeDtypeStruct((rows * size.pitch, ch), F32)
     padded = jax.ShapeDtypeStruct((size.lines, ch), F32)
-    chunks = 2 if rows % 2 == 0 else 1
+    chunks = next(d for d in (3, 2, 1) if rows % d == 0)
     accs = [pltpu.VMEM((groups, rows // chunks * size.octets, width), F32)] * chunks
 
     def call(kernel, ins, out_shape, scratch, flops):

time: 60.9 us -> 59.9 us (0.984)
  other arithmetic: 5.69 us -> 4.15 us
  waiting for transfers between devices: 0.01 us -> 0.79 us
    select_n x2 -> x0, other arithmetic: 2.4 us -> none  [edge(): jnp.where(wet_mask[r0:r1, c0:c1][:, :, None] != 0, fields[r0:r1, c0:c1],...]
    mul x0 -> x2, other arithmetic: none -> 2.4 us  [edge(): return fields[r0:r1, c0:c1] * wet_mask[r0:r1, c0:c1].astype(BF)[:, :, None]]
    ne x2 -> x0, other arithmetic: 1.66 us -> none  [edge(): wet_mask[r0:r1, c0:c1][:, :, None] != 0]
    ppermute x1, waiting for transfers between devices: 0.01 us -> 0.78 us  [exchange_rows(): lax.ppermute(jnp.where(even, first, last), ('lat', 'lon'), partners(nlat,...]
  transfers between devices with their start and end apart: 4 -> 4, of which waited for: 0 -> 1; matrix products, arithmetic and copies ran while one was open for 9% -> 6% of each run, Pallas kernels for 11% -> 10%
where the time goes in v11:
time: 59.9 us; the launch traced here: 59.3 us
  Pallas kernels  43.1 us (72%)
  starting transfers between devices  8.24 us (14%)
  other arithmetic  4.15 us (7%)
  local copies, waits for them, and re-layouts  2.88 us (5%)
  waiting for transfers between devices  0.79 us (1%)
    pallas_call x3, Pallas kernels, call(): pl.pallas_call(functools.partial(kernel, size), grid=(1,), in_specs=[spec...  40.4 us
    ppermute x1, starting transfers between devices, exchange_columns(): right = lax.ppermute(edge(fields, wet_mask, 0, rows, 0, REACH), 'lon', down)  4.2 us
    ppermute x1, starting transfers between devices, exchange_rows(): lax.ppermute(jnp.where(even, first, last), ('lat', 'lon'), partners(nlat,...  3.96 us
    pallas_call x1, Pallas kernels, tap_matrices(): pl.pallas_call(functools.partial(tap_kernel, blocks), grid=(blocks, group...  2.63 us
    mul x2, other arithmetic, edge(): return fields[r0:r1, c0:c1] * wet_mask[r0:r1, c0:c1].astype(BF)[:, :, None]  2.4 us
    unnamed x19, local copies, waits for them, and re-layouts  1.8 us
  transfers between devices with their start and end apart: 4, of which 1 were waited for; matrix products, arithmetic and copies ran while one was open for 6% of the time, Pallas kernels for 10%

profile of v11, /device:TPU:1, one launch (start us, length us, event | category | flops | bytes accessed | tf_op | source)
XLA Modules:
  0.0 59.3 jit_solution(14362354777533430916)
XLA Ops:
  0.0 0.9 %convert_element_type.2 = bf16[48,128]{1,0:T(8,128)(2,1)S(1)} convert(s32[48,128]{1,0:T(8,128)} %param.12) | non-fusion elementwise | flops 6144 | bytes 36864 | tf_op jit(solution)/shard_map/convert_element_type | solution.py:484
  0.9 0.1 fusion.3
  0.9 1.1 %slice_multiply_fusion.2 = (bf16[48,6,128]{2,1,0:T(8,128)(2,1)S(1)}, bf16[48,6,128]{2,1,0:T(8,128)(2,1)S(1)}) fusion(bf16[48,128,128]{2,1,0:T(8,128)(2,1)} %x_ref.1, bf16[48,6]{1,0:T(8,128)(2,1)S(1)} %get-tuple-element.37, bf16[48,6]{1,0:T(8,128)(2,1)S(1)} %get-tuple-element.38), kind=kLoop, calls=%fused_computation.6 | loop fusion | flops 73728 | bytes 296064 | tf_op jit(solution)/shard_map/mul | solution.py:37
  2.1 4.2 %collective-permute-start.1 = (bf16[48,6,128]{2,1,0:T(8,128)(2,1)S(1)}, bf16[48,6,128]{2,1,0:T(8,128)(2,1)S(1)}, u32[]{:S(2)}, u32[]{:S(2)}) collective-permute-start(bf16[48,6,128]{2,1,0:T(8,128)(2,1)S(1)} %get-tuple-element.27), channel_id=1, source_target_pairs={{1,0},{2,1},{3,2},{0,3},{5,4},{6,5},{7,6},{4,7},{9,8},{10,9},{11,1... | collective-permute-start | bytes 221192 | tf_op jit(solution)/shard_map/ppermute | solution.py:46
  6.3 0.0 collective-permute-start
  6.3 0.8 %copy.13 = f32[2,49,128]{2,1,0:T(8,128)S(1)} copy(f32[2,49,128]{2,0,1:T(2,128)} %param.13) | data formatting | bytes 100352 | tf_op args[2]
  7.1 1.3 %slice_multiply_fusion.1 = (bf16[6,128,128]{2,1,0:T(8,128)(2,1)S(1)}, bf16[6,128,128]{2,1,0:T(8,128)(2,1)S(1)}) fusion(bf16[48,128,128]{2,1,0:T(8,128)(2,1)} %x_ref.1, bf16[6,128]{1,0:T(8,128)(2,1)S(1)} %get-tuple-element.35, bf16[6,128]{1,0:T(8,128)(2,1)S(1)} %get-tuple-element.36), kind=kLoop, calls=%fused_computation.5 | loop fusion | flops 196608 | bytes 789504 | tf_op jit(solution)/shard_map/mul | solution.py:37
  8.4 0.7 %pad_maximum_fusion.2.small_ref.k_ref = f32[104,128]{1,0:T(8,128)S(1)} fusion(f32[2,128]{1,0:T(2,128)} %refs_2_.3, f32[2,128]{1,0:T(2,128)} %refs_1_.3, f32[2,128]{1,0:T(2,128)} %refs_0_.3, f32[98,128]{1,0:T(8,128)S(1)} %reshape.8), kind=kLoop, calls=%fused_computation.8 | loop fusion | flops 39936 | bytes 106496 | tf_op jit(solution)/shard_map/concatenate | solution.py:485
  9.1 0.9 %copy-done = bf16[2,128,512]{2,1,0:T(8,128)(2,1)S(1)} copy-done((bf16[2,128,512]{2,1,0:T(8,128)(2,1)S(1)}, bf16[2,128,512]{2,1,0:T(8,128)(2,1)}, u32[]{:S(2)}) %copy-start) | copy-done | bytes 262168
  10.1 2.6 %tap_matrices.1 = (bf16[2,4,3584,256]{3,2,1,0:T(8,128)(2,1)S(1)}, bf16[2,4,512,512]{3,2,1,0:T(8,128)(2,1)S(1)}, f32[2,12,128]{2,1,0:T(8,128)S(1)}) custom-call(f32[104,128]{1,0:T(8,128)S(1)} %pad_maximum_fusion.2.small_ref.k_ref, bf16[2,128,512]{2,1,0:T(8,128)(2,1)S(1)} %copy-done), custom_call_target="tpu_custom_call" | custom-call | bytes 14680064 | tf_op jit(solution)/shard_map/tap_matrices/pallas_call | solution.py:126
  12.7 0.0 collective-permute-done.1.right_ref
  12.7 0.0 collective-permute-done.left_ref
  12.7 0.2 broadcast_select_fusion
  12.9 4.0 %collective-permute-start.3 = (bf16[6,140,128]{2,1,0:T(8,128)(2,1)S(1)}, bf16[6,140,128]{2,1,0:T(8,128)(2,1)S(1)}, u32[]{:S(2)}, u32[]{:S(2)}) collective-permute-start(bf16[6,140,128]{2,1,0:T(8,128)(2,1)S(1)} %get-tuple-element.29), channel_id=1, source_target_pairs={{4,8},{5,9},{6,10},{7,11},{8,4},{9,5},{10,6},{11,7},{12,16},{13,17... | collective-permute-start | bytes 645128 | tf_op jit(solution)/shard_map/ppermute | solution.py:58
  16.9 0.1 collective-permute-start.2
  16.9 1.0 %broadcast_in_dim.2.mask_ref = bf16[48,128,128]{2,1,0:T(8,128)(2,1)S(1)} broadcast(bf16[48,128]{1,0:T(8,128)(2,1)S(1)} %convert_element_type.2), dimensions={0,1} | broadcast | bytes 1585152 | tf_op jit(solution)/shard_map/broadcast_in_dim | solution.py:484
  17.9 0.0 copy-done.2
  17.9 0.0 copy-start.1
  18.0 0.0 copy-start.3
  18.0 0.0 copy-start.4
  18.0 0.0 copy-start.5
  18.0 0.0 copy-start.6
  18.0 0.0 copy-start.7
  18.0 0.0 copy-start.8
  18.0 3.1 %lay_kernel.1 = (f32[7296,128]{1,0:T(8,128)S(1)}, bf16[4,4,768,128]{3,2,1,0:T(8,128)(2,1)S(1)}) custom-call(bf16[48,128,128]{2,1,0:T(8,128)(2,1)S(1)} %copy-done.2, bf16[48,128,128]{2,1,0:T(8,128)(2,1)S(1)} %broadcast_in_dim.2.mask_ref, bf16[48,6,128]{2,1,0:T(8,128)(2,1)S(1)} %collective-permute-done.left_ref, ...), custom_call_target="tpu_custom_call" | custom-call | flops 352321536 | bytes 4718592 | tf_op jit(solution)/shard_map/lay_kernel/pallas_call | solution.py:509
  21.2 0.8 %collective-permute-done.3.b_ref = bf16[6,140,128]{2,1,0:T(8,128)(2,1)S(1)} collective-permute-done((bf16[6,140,128]{2,1,0:T(8,128)(2,1)S(1)}, bf16[6,140,128]{2,1,0:T(8,128)(2,1)S(1)}, u32[]{:S(2)}, u32[]{:S(2)}) %collective-permute-start.3) | collective-permute-done | bytes 215072 | tf_op jit(solution)/shard_map/ppermute | solution.py:58
  22.0 0.0 collective-permute-done.2.a_ref
  22.0 0.0 copy-done.1
  22.0 0.0 copy-done.3
  22.0 0.0 copy-done.4
  22.0 18.8 %block0_kernel.1.x1_ref = f32[9120,128]{1,0:T(8,128)S(1)} custom-call(f32[7296,128]{1,0:T(8,128)S(1)} %get-tuple-element.20.x0_ref, bf16[4,4,768,128]{3,2,1,0:T(8,128)(2,1)S(1)} %get-tuple-element.21.relaid_ref, bf16[6,140,128]{2,1,0:T(8,128)(2,1)S(1)} %collective-permute-done.2.a_ref, bf16[6,140,128]{2,1,0:T(8,128)(2,1)S(1)} %collective-permute-done.3.b_ref, ...), custom_call_target="tpu_custom_call" | custom-call | flops 3019898880 | bytes 4718592 | tf_op jit(solution)/shard_map/block0_kernel/pallas_call | solution.py:509
  40.8 18.5 %block1_kernel.1 = bf16[48,128,128]{2,1,0:T(8,128)(2,1)} custom-call(f32[9120,128]{1,0:T(8,128)S(1)} %block0_kernel.1.x1_ref, bf16[2,4,3584,256]{3,2,1,0:T(8,128)(2,1)S(1)} %get-tuple-element.22.w_ref, bf16[48,128,128]{2,1,0:T(8,128)(2,1)S(1)} %broadcast_in_dim.2.mask_ref, f32[2,128]{1,0:T(2,128)S(1)} %copy-done.6, f32[2,128]{1,0:T(2,128)S(1)} %copy-done.5, ...), custom_call_target="tpu_custom_call" | custom-call | flops 3019898880 | bytes 4718592 | tf_op jit(solution)/shard_map/block1_kernel/pallas_call | solution.py:509
  (9 shorter events, 0.0 us)
Async XLA Ops:
  0.0 17.9 %copy-start.2 = (bf16[48,128,128]{2,1,0:T(8,128)(2,1)S(1)}, bf16[48,128,128]{2,1,0:T(8,128)(2,1)}, u32[]{:S(2)}) copy-start(bf16[48,128,128]{2,1,0:T(8,128)(2,1)} %x_ref.1) | copy-start | bytes 4718596
  2.1 10.6 %collective-permute-start.1 = (bf16[48,6,128]{2,1,0:T(8,128)(2,1)S(1)}, bf16[48,6,128]{2,1,0:T(8,128)(2,1)S(1)}, u32[]{:S(2)}, u32[]{:S(2)}) collective-permute-start(bf16[48,6,128]{2,1,0:T(8,128)(2,1)S(1)} %get-tuple-element.27), channel_id=1, source_target_pairs={{1,0},{2,1},{3,2},{0,3},{5,4},{6,5},{7,6},{4,7},{9,8},{10,9},{11,1... | collective-permute-start | bytes 221192 | tf_op jit(solution)/shard_map/ppermute | solution.py:46
  6.3 6.4 %collective-permute-start = (bf16[48,6,128]{2,1,0:T(8,128)(2,1)S(1)}, bf16[48,6,128]{2,1,0:T(8,128)(2,1)S(1)}, u32[]{:S(2)}, u32[]{:S(2)}) collective-permute-start(bf16[48,6,128]{2,1,0:T(8,128)(2,1)S(1)} %get-tuple-element.28), channel_id=1, source_target_pairs={{0,1},{1,2},{2,3},{3,0},{4,5},{5,6},{6,7},{7,4},{8,9},{9,10},{10,1... | collective-permute-start | bytes 221192 | tf_op jit(solution)/shard_map/ppermute | solution.py:45
  9.1 0.9 %copy-start = (bf16[2,128,512]{2,1,0:T(8,128)(2,1)S(1)}, bf16[2,128,512]{2,1,0:T(8,128)(2,1)}, u32[]{:S(2)}) copy-start(bf16[2,128,512]{2,1,0:T(8,128)(2,1)} %refs_3_.3) | copy-start | bytes 786436
  12.9 9.1 %collective-permute-start.3 = (bf16[6,140,128]{2,1,0:T(8,128)(2,1)S(1)}, bf16[6,140,128]{2,1,0:T(8,128)(2,1)S(1)}, u32[]{:S(2)}, u32[]{:S(2)}) collective-permute-start(bf16[6,140,128]{2,1,0:T(8,128)(2,1)S(1)} %get-tuple-element.29), channel_id=1, source_target_pairs={{4,8},{5,9},{6,10},{7,11},{8,4},{9,5},{10,6},{11,7},{12,16},{13,17... | collective-permute-start | bytes 645128 | tf_op jit(solution)/shard_map/ppermute | solution.py:58
  16.9 5.1 %collective-permute-start.2 = (bf16[6,140,128]{2,1,0:T(8,128)(2,1)S(1)}, bf16[6,140,128]{2,1,0:T(8,128)(2,1)S(1)}, u32[]{:S(2)}, u32[]{:S(2)}) collective-permute-start(bf16[6,140,128]{2,1,0:T(8,128)(2,1)S(1)} %get-tuple-element.30), channel_id=1, source_target_pairs={{0,4},{1,5},{2,6},{3,7},{4,0},{5,1},{6,2},{7,3},{8,12},{9,13},{10,... | collective-permute-start | bytes 645128 | tf_op jit(solution)/shard_map/ppermute | solution.py:57
  17.9 4.0 %copy-start.1 = (bf16[2,512,128]{2,1,0:T(8,128)(2,1)S(1)}, bf16[2,512,128]{2,1,0:T(8,128)(2,1)}, u32[]{:S(2)}) copy-start(bf16[2,512,128]{2,1,0:T(8,128)(2,1)} %refs_5_.3) | copy-start | bytes 786436
  18.0 4.0 %copy-start.3 = (f32[2,512]{1,0:T(2,128)S(1)}, f32[2,512]{1,0:T(2,128)}, u32[]{:S(2)}) copy-start(f32[2,512]{1,0:T(2,128)} %refs_4_.3) | copy-start | bytes 12292
  18.0 4.0 %copy-start.4 = (f32[2,128]{1,0:T(2,128)S(1)}, f32[2,128]{1,0:T(2,128)}, u32[]{:S(2)}) copy-start(f32[2,128]{1,0:T(2,128)} %refs_2_.3) | copy-start | bytes 3076
  18.0 4.0 %copy-start.5 = (f32[2,128]{1,0:T(2,128)S(1)}, f32[2,128]{1,0:T(2,128)}, u32[]{:S(2)}) copy-start(f32[2,128]{1,0:T(2,128)} %refs_1_.3) | copy-start | bytes 3076
  18.0 4.0 %copy-start.6 = (f32[2,128]{1,0:T(2,128)S(1)}, f32[2,128]{1,0:T(2,128)}, u32[]{:S(2)}) copy-start(f32[2,128]{1,0:T(2,128)} %refs_0_.3) | copy-start | bytes 3076
  18.0 4.0 %copy-start.7 = (f32[2,128]{1,0:T(2,128)S(1)}, f32[2,128]{1,0:T(2,128)}, u32[]{:S(2)}) copy-start(f32[2,128]{1,0:T(2,128)} %refs_6_.3) | copy-start | bytes 3076
  18.0 4.0 %copy-start.8 = (f32[2,128]{1,0:T(2,128)S(1)}, f32[2,128]{1,0:T(2,128)}, u32[]{:S(2)}) copy-start(f32[2,128]{1,0:T(2,128)} %refs_7_.3) | copy-start | bytes 3076

commit v12 on v11

--- a/solution.py
+++ b/solution.py
@@ -495,7 +495,7 @@
     ends = pltpu.VMEM((groups, 4, 2 * HALO * size.octets, ch), BF)
     own = jax.ShapeDtypeStruct((rows * size.pitch, ch), F32)
     padded = jax.ShapeDtypeStruct((size.lines, ch), F32)
-    chunks = next(d for d in (3, 2, 1) if rows % d == 0)
+    chunks = next(d for d in (2, 1) if rows % d == 0)
     accs = [pltpu.VMEM((groups, rows // chunks * size.octets, width), F32)] * chunks
 
     def call(kernel, ins, out_shape, scratch, flops):

time: 59.9 us -> 57.9 us (0.967)
  Pallas kernels: 43.1 us -> 41 us
    pallas_call x3, Pallas kernels: 40.4 us -> 38.4 us  [call(): pl.pallas_call(functools.partial(kernel, size), grid=(1,), in_specs=[spec...]
  transfers between devices with their start and end apart: 4 -> 4, of which waited for: 1 -> 1; matrix products, arithmetic and copies ran while one was open for 6% -> 7% of each run, Pallas kernels for 10% -> 10%
where the time goes in v12:
time: 57.9 us; the launch traced here: 57.3 us
  Pallas kernels  41 us (71%)
  starting transfers between devices  8.24 us (14%)
  other arithmetic  4.15 us (7%)
  local copies, waits for them, and re-layouts  2.88 us (5%)
  waiting for transfers between devices  0.79 us (1%)
    pallas_call x3, Pallas kernels, call(): pl.pallas_call(functools.partial(kernel, size), grid=(1,), in_specs=[spec...  38.4 us
    ppermute x1, starting transfers between devices, exchange_columns(): right = lax.ppermute(edge(fields, wet_mask, 0, rows, 0, REACH), 'lon', down)  4.2 us
    ppermute x1, starting transfers between devices, exchange_rows(): lax.ppermute(jnp.where(even, first, last), ('lat', 'lon'), partners(nlat,...  3.96 us
    pallas_call x1, Pallas kernels, tap_matrices(): pl.pallas_call(functools.partial(tap_kernel, blocks), grid=(blocks, group...  2.63 us
    mul x2, other arithmetic, edge(): return fields[r0:r1, c0:c1] * wet_mask[r0:r1, c0:c1].astype(BF)[:, :, None]  2.4 us
    unnamed x19, local copies, waits for them, and re-layouts  1.8 us
  transfers between devices with their start and end apart: 4, of which 1 were waited for; matrix products, arithmetic and copies ran while one was open for 7% of the time, Pallas kernels for 10%

profile of v12, /device:TPU:1, one launch (start us, length us, event | category | flops | bytes accessed | tf_op | source)
XLA Modules:
  0.0 57.3 jit_solution(7003942461889556337)
XLA Ops:
  0.0 0.9 %convert_element_type.2 = bf16[48,128]{1,0:T(8,128)(2,1)S(1)} convert(s32[48,128]{1,0:T(8,128)} %param.12) | non-fusion elementwise | flops 6144 | bytes 36864 | tf_op jit(solution)/shard_map/convert_element_type | solution.py:484
  0.9 0.1 fusion.3
  0.9 1.1 %slice_multiply_fusion.2 = (bf16[48,6,128]{2,1,0:T(8,128)(2,1)S(1)}, bf16[48,6,128]{2,1,0:T(8,128)(2,1)S(1)}) fusion(bf16[48,128,128]{2,1,0:T(8,128)(2,1)} %x_ref.1, bf16[48,6]{1,0:T(8,128)(2,1)S(1)} %get-tuple-element.37, bf16[48,6]{1,0:T(8,128)(2,1)S(1)} %get-tuple-element.38), kind=kLoop, calls=%fused_computation.6 | loop fusion | flops 73728 | bytes 296064 | tf_op jit(solution)/shard_map/mul | solution.py:37
  2.1 4.2 %collective-permute-start.1 = (bf16[48,6,128]{2,1,0:T(8,128)(2,1)S(1)}, bf16[48,6,128]{2,1,0:T(8,128)(2,1)S(1)}, u32[]{:S(2)}, u32[]{:S(2)}) collective-permute-start(bf16[48,6,128]{2,1,0:T(8,128)(2,1)S(1)} %get-tuple-element.27), channel_id=1, source_target_pairs={{1,0},{2,1},{3,2},{0,3},{5,4},{6,5},{7,6},{4,7},{9,8},{10,9},{11,1... | collective-permute-start | bytes 221192 | tf_op jit(solution)/shard_map/ppermute | solution.py:46
  6.3 0.0 collective-permute-start
  6.3 0.8 %copy.13 = f32[2,49,128]{2,1,0:T(8,128)S(1)} copy(f32[2,49,128]{2,0,1:T(2,128)} %param.13) | data formatting | bytes 100352 | tf_op args[2]
  7.1 1.3 %slice_multiply_fusion.1 = (bf16[6,128,128]{2,1,0:T(8,128)(2,1)S(1)}, bf16[6,128,128]{2,1,0:T(8,128)(2,1)S(1)}) fusion(bf16[48,128,128]{2,1,0:T(8,128)(2,1)} %x_ref.1, bf16[6,128]{1,0:T(8,128)(2,1)S(1)} %get-tuple-element.35, bf16[6,128]{1,0:T(8,128)(2,1)S(1)} %get-tuple-element.36), kind=kLoop, calls=%fused_computation.5 | loop fusion | flops 196608 | bytes 789504 | tf_op jit(solution)/shard_map/mul | solution.py:37
  8.4 0.7 %pad_maximum_fusion.2.small_ref.k_ref = f32[104,128]{1,0:T(8,128)S(1)} fusion(f32[2,128]{1,0:T(2,128)} %refs_2_.3, f32[2,128]{1,0:T(2,128)} %refs_1_.3, f32[2,128]{1,0:T(2,128)} %refs_0_.3, f32[98,128]{1,0:T(8,128)S(1)} %reshape.8), kind=kLoop, calls=%fused_computation.8 | loop fusion | flops 39936 | bytes 106496 | tf_op jit(solution)/shard_map/concatenate | solution.py:485
  9.1 0.9 %copy-done = bf16[2,128,512]{2,1,0:T(8,128)(2,1)S(1)} copy-done((bf16[2,128,512]{2,1,0:T(8,128)(2,1)S(1)}, bf16[2,128,512]{2,1,0:T(8,128)(2,1)}, u32[]{:S(2)}) %copy-start) | copy-done | bytes 262168
  10.1 2.6 %tap_matrices.1 = (bf16[2,4,3584,256]{3,2,1,0:T(8,128)(2,1)S(1)}, bf16[2,4,512,512]{3,2,1,0:T(8,128)(2,1)S(1)}, f32[2,12,128]{2,1,0:T(8,128)S(1)}) custom-call(f32[104,128]{1,0:T(8,128)S(1)} %pad_maximum_fusion.2.small_ref.k_ref, bf16[2,128,512]{2,1,0:T(8,128)(2,1)S(1)} %copy-done), custom_call_target="tpu_custom_call" | custom-call | bytes 14680064 | tf_op jit(solution)/shard_map/tap_matrices/pallas_call | solution.py:126
  12.7 0.0 collective-permute-done.1.right_ref
  12.7 0.0 collective-permute-done.left_ref
  12.7 0.2 broadcast_select_fusion
  12.9 4.0 %collective-permute-start.3 = (bf16[6,140,128]{2,1,0:T(8,128)(2,1)S(1)}, bf16[6,140,128]{2,1,0:T(8,128)(2,1)S(1)}, u32[]{:S(2)}, u32[]{:S(2)}) collective-permute-start(bf16[6,140,128]{2,1,0:T(8,128)(2,1)S(1)} %get-tuple-element.29), channel_id=1, source_target_pairs={{4,8},{5,9},{6,10},{7,11},{8,4},{9,5},{10,6},{11,7},{12,16},{13,17... | collective-permute-start | bytes 645128 | tf_op jit(solution)/shard_map/ppermute | solution.py:58
  16.9 0.1 collective-permute-start.2
  16.9 1.0 %broadcast_in_dim.2.mask_ref = bf16[48,128,128]{2,1,0:T(8,128)(2,1)S(1)} broadcast(bf16[48,128]{1,0:T(8,128)(2,1)S(1)} %convert_element_type.2), dimensions={0,1} | broadcast | bytes 1585152 | tf_op jit(solution)/shard_map/broadcast_in_dim | solution.py:484
  17.9 0.0 copy-done.2
  17.9 0.0 copy-start.1
  18.0 0.0 copy-start.3
  18.0 0.0 copy-start.4
  18.0 0.0 copy-start.5
  18.0 0.0 copy-start.6
  18.0 0.0 copy-start.7
  18.0 0.0 copy-start.8
  18.0 3.1 %lay_kernel.1 = (f32[7296,128]{1,0:T(8,128)S(1)}, bf16[4,4,768,128]{3,2,1,0:T(8,128)(2,1)S(1)}) custom-call(bf16[48,128,128]{2,1,0:T(8,128)(2,1)S(1)} %copy-done.2, bf16[48,128,128]{2,1,0:T(8,128)(2,1)S(1)} %broadcast_in_dim.2.mask_ref, bf16[48,6,128]{2,1,0:T(8,128)(2,1)S(1)} %collective-permute-done.left_ref, ...), custom_call_target="tpu_custom_call" | custom-call | flops 352321536 | bytes 4718592 | tf_op jit(solution)/shard_map/lay_kernel/pallas_call | solution.py:509
  21.2 0.8 %collective-permute-done.3.b_ref = bf16[6,140,128]{2,1,0:T(8,128)(2,1)S(1)} collective-permute-done((bf16[6,140,128]{2,1,0:T(8,128)(2,1)S(1)}, bf16[6,140,128]{2,1,0:T(8,128)(2,1)S(1)}, u32[]{:S(2)}, u32[]{:S(2)}) %collective-permute-start.3) | collective-permute-done | bytes 215072 | tf_op jit(solution)/shard_map/ppermute | solution.py:58
  22.0 0.0 collective-permute-done.2.a_ref
  22.0 0.0 copy-done.1
  22.0 0.0 copy-done.3
  22.0 0.0 copy-done.4
  22.0 17.6 %block0_kernel.1.x1_ref = f32[9120,128]{1,0:T(8,128)S(1)} custom-call(f32[7296,128]{1,0:T(8,128)S(1)} %get-tuple-element.20.x0_ref, bf16[4,4,768,128]{3,2,1,0:T(8,128)(2,1)S(1)} %get-tuple-element.21.relaid_ref, bf16[6,140,128]{2,1,0:T(8,128)(2,1)S(1)} %collective-permute-done.2.a_ref, bf16[6,140,128]{2,1,0:T(8,128)(2,1)S(1)} %collective-permute-done.3.b_ref, ...), custom_call_target="tpu_custom_call" | custom-call | flops 3019898880 | bytes 4718592 | tf_op jit(solution)/shard_map/block0_kernel/pallas_call | solution.py:509
  39.6 17.6 %block1_kernel.1 = bf16[48,128,128]{2,1,0:T(8,128)(2,1)} custom-call(f32[9120,128]{1,0:T(8,128)S(1)} %block0_kernel.1.x1_ref, bf16[2,4,3584,256]{3,2,1,0:T(8,128)(2,1)S(1)} %get-tuple-element.22.w_ref, bf16[48,128,128]{2,1,0:T(8,128)(2,1)S(1)} %broadcast_in_dim.2.mask_ref, f32[2,128]{1,0:T(2,128)S(1)} %copy-done.6, f32[2,128]{1,0:T(2,128)S(1)} %copy-done.5, ...), custom_call_target="tpu_custom_call" | custom-call | flops 3019898880 | bytes 4718592 | tf_op jit(solution)/shard_map/block1_kernel/pallas_call | solution.py:509
  (9 shorter events, 0.0 us)
Async XLA Ops:
  0.0 17.9 %copy-start.2 = (bf16[48,128,128]{2,1,0:T(8,128)(2,1)S(1)}, bf16[48,128,128]{2,1,0:T(8,128)(2,1)}, u32[]{:S(2)}) copy-start(bf16[48,128,128]{2,1,0:T(8,128)(2,1)} %x_ref.1) | copy-start | bytes 4718596
  2.1 10.6 %collective-permute-start.1 = (bf16[48,6,128]{2,1,0:T(8,128)(2,1)S(1)}, bf16[48,6,128]{2,1,0:T(8,128)(2,1)S(1)}, u32[]{:S(2)}, u32[]{:S(2)}) collective-permute-start(bf16[48,6,128]{2,1,0:T(8,128)(2,1)S(1)} %get-tuple-element.27), channel_id=1, source_target_pairs={{1,0},{2,1},{3,2},{0,3},{5,4},{6,5},{7,6},{4,7},{9,8},{10,9},{11,1... | collective-permute-start | bytes 221192 | tf_op jit(solution)/shard_map/ppermute | solution.py:46
  6.3 6.4 %collective-permute-start = (bf16[48,6,128]{2,1,0:T(8,128)(2,1)S(1)}, bf16[48,6,128]{2,1,0:T(8,128)(2,1)S(1)}, u32[]{:S(2)}, u32[]{:S(2)}) collective-permute-start(bf16[48,6,128]{2,1,0:T(8,128)(2,1)S(1)} %get-tuple-element.28), channel_id=1, source_target_pairs={{0,1},{1,2},{2,3},{3,0},{4,5},{5,6},{6,7},{7,4},{8,9},{9,10},{10,1... | collective-permute-start | bytes 221192 | tf_op jit(solution)/shard_map/ppermute | solution.py:45
  9.1 0.9 %copy-start = (bf16[2,128,512]{2,1,0:T(8,128)(2,1)S(1)}, bf16[2,128,512]{2,1,0:T(8,128)(2,1)}, u32[]{:S(2)}) copy-start(bf16[2,128,512]{2,1,0:T(8,128)(2,1)} %refs_3_.3) | copy-start | bytes 786436
  12.9 9.1 %collective-permute-start.3 = (bf16[6,140,128]{2,1,0:T(8,128)(2,1)S(1)}, bf16[6,140,128]{2,1,0:T(8,128)(2,1)S(1)}, u32[]{:S(2)}, u32[]{:S(2)}) collective-permute-start(bf16[6,140,128]{2,1,0:T(8,128)(2,1)S(1)} %get-tuple-element.29), channel_id=1, source_target_pairs={{4,8},{5,9},{6,10},{7,11},{8,4},{9,5},{10,6},{11,7},{12,16},{13,17... | collective-permute-start | bytes 645128 | tf_op jit(solution)/shard_map/ppermute | solution.py:58
  16.9 5.1 %collective-permute-start.2 = (bf16[6,140,128]{2,1,0:T(8,128)(2,1)S(1)}, bf16[6,140,128]{2,1,0:T(8,128)(2,1)S(1)}, u32[]{:S(2)}, u32[]{:S(2)}) collective-permute-start(bf16[6,140,128]{2,1,0:T(8,128)(2,1)S(1)} %get-tuple-element.30), channel_id=1, source_target_pairs={{0,4},{1,5},{2,6},{3,7},{4,0},{5,1},{6,2},{7,3},{8,12},{9,13},{10,... | collective-permute-start | bytes 645128 | tf_op jit(solution)/shard_map/ppermute | solution.py:57
  17.9 4.0 %copy-start.1 = (bf16[2,512,128]{2,1,0:T(8,128)(2,1)S(1)}, bf16[2,512,128]{2,1,0:T(8,128)(2,1)}, u32[]{:S(2)}) copy-start(bf16[2,512,128]{2,1,0:T(8,128)(2,1)} %refs_5_.3) | copy-start | bytes 786436
  18.0 4.0 %copy-start.3 = (f32[2,512]{1,0:T(2,128)S(1)}, f32[2,512]{1,0:T(2,128)}, u32[]{:S(2)}) copy-start(f32[2,512]{1,0:T(2,128)} %refs_4_.3) | copy-start | bytes 12292
  18.0 4.0 %copy-start.4 = (f32[2,128]{1,0:T(2,128)S(1)}, f32[2,128]{1,0:T(2,128)}, u32[]{:S(2)}) copy-start(f32[2,128]{1,0:T(2,128)} %refs_2_.3) | copy-start | bytes 3076
  18.0 4.0 %copy-start.5 = (f32[2,128]{1,0:T(2,128)S(1)}, f32[2,128]{1,0:T(2,128)}, u32[]{:S(2)}) copy-start(f32[2,128]{1,0:T(2,128)} %refs_1_.3) | copy-start | bytes 3076
  18.0 4.0 %copy-start.6 = (f32[2,128]{1,0:T(2,128)S(1)}, f32[2,128]{1,0:T(2,128)}, u32[]{:S(2)}) copy-start(f32[2,128]{1,0:T(2,128)} %refs_0_.3) | copy-start | bytes 3076
  18.0 4.0 %copy-start.7 = (f32[2,128]{1,0:T(2,128)S(1)}, f32[2,128]{1,0:T(2,128)}, u32[]{:S(2)}) copy-start(f32[2,128]{1,0:T(2,128)} %refs_6_.3) | copy-start | bytes 3076
  18.0 4.0 %copy-start.8 = (f32[2,128]{1,0:T(2,128)S(1)}, f32[2,128]{1,0:T(2,128)}, u32[]{:S(2)}) copy-start(f32[2,128]{1,0:T(2,128)} %refs_7_.3) | copy-start | bytes 3076
